TPU v7x, 32 devices: a whole 2x2x4 slice. The times are simulated.
32 devices in a mesh: parts: 2 (over y), tensor: 4 (over z), dp: 4 (over x, core).
Axes of the slice: x: 2, y: 2, z: 4, core: 2. Of those that a mesh axis runs over, the one named last changes fastest.
Arguments:
- acts_in: bfloat16 [2, 16, 512, 8192], P(None, ('parts', 'dp'), None, 'tensor'), parts along dimension 1, may hold values from -6 to 6
- grads_out: bfloat16 [2, 16, 512, 8192], P(None, ('parts', 'dp'), None, 'tensor'), parts along dimension 1, may hold values from -6 to 6
- basis_in: bfloat16 [2, 8192, 64], P(None, 'tensor'), may hold values from -0.0625 to 0.0625
- basis_out: bfloat16 [2, 8192, 64], P(None, 'tensor'), may hold values from -0.0625 to 0.0625
- lengths: int32 [16], P(('parts', 'dp')), parts along dimension 0, may hold values from 64 to 512, as said below
- fisher_inv: bfloat16 [2, 4096, 4096], P(None, 'dp', 'tensor'), may hold values from -3 to 3
- queries: bfloat16 [2, 1024, 4096], P(None, 'tensor', 'dp'), may hold values from -0.75 to 0.75
Outputs:
- scores: float32 [16, 1024], P(('parts', 'dp'), 'tensor'), parts along dimension 0
There are 2 independent parts, one for each index of `parts`. A program takes and returns all parts, laid end to end along the dimension named above; an argument that names none is the same for every part. Nothing has to cross between parts.
Inputs may be any that keep to these rules, and one draw needn't show every extreme that they name: `lengths`: positions at or beyond an example's length are padding; some example has all 512 tokens.
All inputs are finite; a program needn't handle non-finite values.
Results may differ from a plain program's by a relative error of at most 0.0003.
Values may be sent and summed in bfloat16 or wider, within the bound.
No kernel may reach another device: no remote copies, remote signals or barrier semaphores. Data moves between devices by JAX's collectives and lax.ppermute only.
A program may use at most 128 MiB of HBM per device.

v0:
```python
import jax
import jax.numpy as jnp
from jax import lax
from jax.sharding import PartitionSpec as P


def local(acts_in, grads_out, basis_in, basis_out, lengths, fisher_inv, queries):
    proj_width = basis_in.shape[2]
    layer_count = acts_in.shape[0]
    local_examples = acts_in.shape[1]
    proj_in = jnp.einsum("letd,ldr->letr", acts_in, basis_in, preferred_element_type=jnp.float32)
    proj_out = jnp.einsum(
        "letd,ldr->letr", grads_out, basis_out, preferred_element_type=jnp.float32
    )
    partial_proj = jnp.concatenate([proj_out, proj_in], axis=3)
    summed_proj = lax.psum(partial_proj, "tensor")
    share_len = summed_proj.shape[2]
    proj_out = summed_proj[..., :proj_width]
    proj_in = summed_proj[..., proj_width:]
    positions = lax.broadcasted_iota(jnp.int32, (share_len,), 0)
    token_weight = jnp.where(positions[None, :] < lengths[:, None], 1.0, 0.0).astype(jnp.float32)
    token_weight = token_weight / lengths[:, None].astype(jnp.float32)
    weighted = proj_out * token_weight[None, :, :, None]
    outer_prod = jnp.einsum("leta,letb->leab", weighted, proj_in, precision=lax.Precision.HIGHEST)
    example_grads = outer_prod.reshape(layer_count, local_examples, proj_width * proj_width)
    row_blocks = lax.all_to_all(example_grads, "dp", split_axis=2, concat_axis=1, tiled=True)
    gathered_queries = lax.all_gather(queries, "dp", axis=2, tiled=True)
    mapped = jnp.einsum(
        "lqj,lij->lqi",
        gathered_queries,
        lax.all_gather(fisher_inv, "tensor", axis=2, tiled=True),
        preferred_element_type=jnp.float32,
    )
    score_terms = jnp.einsum("lei,lqi->eq", row_blocks, mapped, precision=lax.Precision.HIGHEST)
    scores = lax.psum_scatter(score_terms, "dp", scatter_dimension=0, tiled=True)
    return scores


def solution(mesh):
    in_specs = (
        P(None, ("parts", "dp"), None, "tensor"),
        P(None, ("parts", "dp"), None, "tensor"),
        P(None, "tensor", None),
        P(None, "tensor", None),
        P(("parts", "dp")),
        P(None, "dp", "tensor"),
        P(None, "tensor", "dp"),
    )
    out_specs = P(("parts", "dp"), "tensor")
    return jax.shard_map(local, mesh=mesh, in_specs=in_specs, out_specs=out_specs, check_vma=False)
```

profile of v0, /device:TPU:0, one launch (start us, length us, event | category | flops | bytes accessed | tf_op | source)
XLA Modules:
  0.0 371.9 jit_solution(984562276386043586)
XLA Ops:
  7.4 1.0 copy-done
  8.4 6.2 %fusion.2 = f32[2,2,512,64]{2,3,1,0:T(8,128)S(1)} fusion(bf16[2,2,512,2048]{3,2,1,0:T(8,128)(2,1)} %param.7, bf16[2,2048,64]{1,2,0:T(8,128)(2,1)S(1)} %copy-done), kind=kOutput, calls=%fused_computation.5 | convolution fusion | flops 536870912 | bytes 9437184 | tf_op jit(solution)/shard_map/letd,ldr->letr/dot_general | solution.py:11
  14.6 2.7 fusion.4
  17.3 1.1 pad_maximum_fusion
  18.5 0.5 all-gather.3.cloned.1.call-update
  19.0 0.5 all-gather.5.cloned.1.call-update
  19.6 0.1 fusion.7
  19.7 53.4 %all-reduce.3.cloned.1.call-done = f32[2,2,512,128]{2,3,1,0:T(8,128)} async-done(((f32[2,2,512,128]{2,3,1,0:T(8,128)}), f32[2,2,512,128]{2,3,1,0:T(8,128)}) %all-reduce.3.cloned.1.call-update) | async-done | bytes 1048592 | tf_op jit(solution)/shard_map/psum | solution.py:16
  73.1 1.9 fusion
  75.0 4.5 %copy.13 = f32[2,2,64,64]{1,0,3,2:T(2,128)} copy(f32[2,2,64,64]{3,2,1,0:T(8,128)S(1)} %fusion) | data formatting | bytes 131072 | tf_op jit(solution)/shard_map/reshape | solution.py:25
  79.5 8.1 %reshape.46 = f32[4,1,4096]{2,1,0:T(1,128)} reshape(f32[4096,2,2]{2,1,0:T(2,128)} %bitcast.24) | data formatting | bytes 131072
  87.6 3.5 all-to-all-start
  91.1 0.6 dynamic-slice
  92.3 2.7 all-to-all-done
  95.0 0.5 broadcast.33
  95.5 0.8 reduce
  96.3 8.4 %reshape.47 = f32[4096,2,2]{2,1,0:T(2,128)} reshape(f32[4,4096]{1,0:T(4,128)S(1)} %reduce) | data formatting | bytes 131072
  104.7 5.2 %copy.10 = f32[2,2,4,1024]{3,1,2,0:T(2,128)S(1)} copy(f32[2,2,4,1024]{1,0,3,2:T(2,128)} %bitcast.25) | data formatting | bytes 131072 | tf_op jit(solution)/shard_map/all_to_all | solution.py:26
  109.9 0.1 all_to_all.16
  110.0 235.8 %all-gather.5.cloned.1.call-done = bf16[2,1024,4096]{2,1,0:T(8,128)(2,1)} async-done(((bf16[2,1024,1024]{2,1,0:T(8,128)(2,1)}), bf16[2,1024,4096]{2,1,0:T(8,128)(2,1)}) %all-gather.5.cloned.1.call-update) | async-done | bytes 16777232 | tf_op jit(solution)/shard_map/all_gather | solution.py:31
  345.8 9.4 %fusion.8 = f32[2,256,1024]{2,1,0:T(8,128)S(1)} fusion(bf16[2,256,4096]{2,1,0:T(8,128)(2,1)} %all-gather.3.cloned.1.call-done, bf16[2,1024,4096]{2,1,0:T(8,128)(2,1)} %all-gather.5.cloned.1.call-done), kind=kOutput, calls=%fused_computation.13 | convolution fusion | flops 4294967296 | bytes 23068672 | tf_op jit(solution)/shard_map/lqj,lij->lqi/dot_general | solution.py:28
  355.2 1.7 convolution_bitcast_fusion
  356.9 7.0 %all-reduce = f32[8,256]{1,0:T(8,128)S(1)} all-reduce(f32[8,256]{1,0:T(8,128)S(1)} %convolution_bitcast_fusion), channel_id=2, replica_groups=mesh['parts'=2,'tensor'=4,'dp'=4] {'dp'}, use_global_device_ids=true, to_apply=%region_1.2.clone | all-reduce | flops 2048 | bytes 16384
  363.9 0.6 constant_dynamic-slice_fusion
  (15 shorter events, 0.2 us)
Async XLA Ops:
  7.4 1.0 copy-start
  7.4 7.2 %copy-start.2 = (bf16[2,2048,64]{1,2,0:T(8,128)(2,1)S(1)}, bf16[2,2048,64]{1,2,0:T(8,128)(2,1)}, u32[]{:S(2)}) copy-start(bf16[2,2048,64]{1,2,0:T(8,128)(2,1)} %param.10) | copy-start | bytes 1572868
  7.4 65.7 %all-reduce.3.cloned.1.call-start = ((), (), s32[]{:S(2)}) async-start(), calls=%async_computation.1 | async-start | bytes 2097152 | tf_op jit(solution)/shard_map/psum | solution.py:16
  8.4 6.2 %copy-start.1 = (bf16[2,2,512,2048]{3,2,1,0:T(8,128)(2,1)S(1)}, bf16[2,2,512,2048]{3,2,1,0:T(8,128)(2,1)}, u32[]{:S(2)}) copy-start(bf16[2,2,512,2048]{3,2,1,0:T(8,128)(2,1)} %param.8) | copy-start | bytes 25165828
  14.6 5.0 %copy-start.3 = (s32[2]{0:T(128)S(1)}, s32[2]{0:T(128)}, u32[]{:S(2)}) copy-start(s32[2]{0:T(128)} %param.11) | copy-start | bytes 28
  18.4 72.7 %copy-start.4 = (u32[32]{0:T(128)S(1)}, u32[32]{0:T(128)}, u32[]{:S(2)}) copy-start(u32[32]{0:T(128)} %constant.9) | copy-start | bytes 388
  18.4 91.6 %all-gather.3.cloned.1.call-start = ((), (), s32[]{:S(2)}) async-start(), calls=%async_computation.2 | async-start | bytes 5242880 | tf_op jit(solution)/shard_map/all_gather | solution.py:27
  19.0 326.8 %all-gather.5.cloned.1.call-start = ((), (), s32[]{:S(2)}) async-start(), calls=%async_computation.3 | async-start | bytes 20971520 | tf_op jit(solution)/shard_map/all_gather | solution.py:31
  87.6 7.4 %all-to-all-start = ((f32[4,1,4096]{2,1,0:T(1,128)}), f32[4,1,4096]{2,1,0:T(1,128)S(1)}, u32[]{:S(2)}, u32[]{:S(2)}) async-start(f32[4,1,4096]{2,1,0:T(1,128)} %reshape.46), calls=%async_computation | async-start | bytes 131072 | tf_op jit(solution)/shard_map/all_to_all | solution.py:26
Sparse Core Ops, SparseCore 0:
  18.5 54.5 all-reduce.2
Sparse Core Ops, SparseCore 1:
  20.5 37.0 all-gather.2
  59.1 286.6 all-gather.4
where the time goes:
time: 372 us
  waiting for transfers between devices  293 us (79%)
  local copies, waits for them, and re-layouts  29 us (8%)
  matrix products  21.9 us (6%)
  between operations  15.6 us (4%)
  blocking collectives  6.95 us (2%)
    all_gather x1, waiting for transfers between devices, local(): lax.all_gather(fisher_inv, 'tensor', axis=2, tiled=True)  236 us
    psum x1, waiting for transfers between devices, local(): summed_proj = lax.psum(partial_proj, 'tensor')  53.4 us
    unnamed x14, local copies, waits for them, and re-layouts  18.7 us
    dot_general x1, matrix products, local(): jnp.einsum('lqj,lij->lqi', gathered_queries, lax.all_gather(fisher_inv, '...  9.44 us
  transfers between devices with their start and end apart: 4, of which 3 were waited for; matrix products, arithmetic and copies ran while one was open for 8% of the time, Pallas kernels for 0%

commit v1 on v0

--- a/solution.py
+++ b/solution.py
@@ -1,10 +1,278 @@
 import jax
 import jax.numpy as jnp
 from jax import lax
+from jax.experimental import pallas as pl
+from jax.experimental.pallas import tpu as pltpu
 from jax.sharding import PartitionSpec as P
 
-
-def local(acts_in, grads_out, basis_in, basis_out, lengths, fisher_inv, queries):
+STEPS = 64.0
+TOP = 32767.0
+CHUNKS = 2
+AHEAD = 2
+VMEM = 24 * 1024 * 1024
+
+
+def nn(a, b):
+    return lax.dot_general(a, b, (((1,), (0,)), ((), ())), preferred_element_type=jnp.float32)
+
+
+def nt(a, b):
+    return lax.dot_general(a, b, (((1,), (1,)), ((), ())), preferred_element_type=jnp.float32)
+
+
+def tn(a, b):
+    return lax.dot_general(a, b, (((0,), (0,)), ((), ())), preferred_element_type=jnp.float32)
+
+
+def thirds(x):
+    first = x.astype(jnp.bfloat16).astype(jnp.float32)
+    rest = x - first
+    second = rest.astype(jnp.bfloat16).astype(jnp.float32)
+    return jnp.concatenate([first, second, rest - second], axis=0).astype(jnp.bfloat16)
+
+
+def add_thirds(x):
+    rows = x.shape[0] // 3
+    return x[:rows] + (x[rows : 2 * rows] + x[2 * rows :])
+
+
+def project(flips, groups, acts, grads, basis_in, basis_out, *refs):
+    outs, (a_buf, g_buf, in_buf, out_buf, scale_log, sems, basis_sems) = refs[: len(flips)], refs[len(flips) :]
+    examples, tokens = acts.shape[1], acts.shape[2]
+    here = lax.axis_index("tensor")
+    layer = (here ^ flips[0]) // examples
+    size = tokens // CHUNKS
+    bases = (
+        pltpu.make_async_copy(basis_out.at[layer], out_buf, basis_sems.at[0]),
+        pltpu.make_async_copy(basis_in.at[layer], in_buf, basis_sems.at[1]),
+    )
+    copies = []
+    for k, flip in enumerate(flips):
+        example = (here ^ flip) % examples
+        for c in range(CHUNKS):
+            rows, at = pl.ds(c * size, size), k * CHUNKS + c
+            copies.append(
+                (
+                    pltpu.make_async_copy(grads.at[layer, example, rows, :], g_buf.at[at], sems.at[0, at]),
+                    pltpu.make_async_copy(acts.at[layer, example, rows, :], a_buf.at[at], sems.at[1, at]),
+                )
+            )
+    for copy in bases:
+        copy.start()
+    for c in range(AHEAD):
+        for copy in copies[c]:
+            copy.start()
+    for copy in bases:
+        copy.wait()
+    for k, out in enumerate(outs):
+        for c in range(CHUNKS):
+            rows, at = pl.ds(c * size, size), k * CHUNKS + c
+            for copy in copies[at]:
+                copy.wait()
+            if at + AHEAD < len(copies):
+                for copy in copies[at + AHEAD]:
+                    copy.start()
+            proj_out = nt(g_buf[at], out_buf[...])
+            proj_in = nt(a_buf[at], in_buf[...])
+            both = jnp.concatenate([proj_out, proj_in], axis=1)
+            group = groups[k]
+            if not group:
+                out[rows, :] = both
+                continue
+            grouped = both.reshape(size // group, group, both.shape[1])
+            most = jnp.maximum(jnp.max(jnp.abs(grouped), axis=1), 1e-30)
+            log = jnp.ceil(jnp.log2(most) * STEPS)
+            scale = jnp.exp2(log * (-1.0 / STEPS)) * TOP
+            codes = jnp.round(grouped * scale[:, None, :])
+            codes = jnp.minimum(jnp.maximum(codes, -TOP), TOP).reshape(both.shape)
+            out[rows, :] = codes.astype(jnp.int32).astype(jnp.int16)
+            scale_log[pl.ds(c * (size // group), size // group), :] = log
+        if group:
+            log = scale_log[pl.ds(0, tokens // group), :]
+            out[pl.ds(tokens, tokens // group), :] = log.astype(jnp.int32).astype(jnp.int16)
+
+
+def projector(flips, groups, acts, grads, basis_in, basis_out):
+    tokens, width = acts.shape[2], acts.shape[3]
+    both = 2 * basis_in.shape[1]
+
+    def project_pairs(*refs):
+        project(flips, groups, *refs)
+
+    pieces = len(flips) * CHUNKS
+    hbm = pl.BlockSpec(memory_space=pltpu.HBM)
+    vmem = pl.BlockSpec(memory_space=pltpu.VMEM)
+    return pl.pallas_call(
+        project_pairs,
+        out_shape=[
+            jax.ShapeDtypeStruct((tokens + tokens // g, both), jnp.int16)
+            if g
+            else jax.ShapeDtypeStruct((tokens, both), jnp.float32)
+            for g in groups
+        ],
+        in_specs=[hbm] * 4,
+        out_specs=[vmem] * len(groups),
+        scratch_shapes=[
+            pltpu.VMEM((pieces, tokens // CHUNKS, width), acts.dtype),
+            pltpu.VMEM((pieces, tokens // CHUNKS, width), grads.dtype),
+            pltpu.VMEM(basis_in.shape[1:], basis_in.dtype),
+            pltpu.VMEM(basis_out.shape[1:], basis_out.dtype),
+            pltpu.VMEM((tokens // 16, both), jnp.float32),
+            pltpu.SemaphoreType.DMA((2, pieces)),
+            pltpu.SemaphoreType.DMA((2,)),
+        ],
+        compiler_params=pltpu.CompilerParams(vmem_limit_bytes=VMEM),
+        cost_estimate=pl.CostEstimate(
+            flops=2 * len(flips) * tokens * width * both,
+            bytes_accessed=4 * len(flips) * tokens * width,
+            transcendentals=0,
+        ),
+    )(*(pltpu.with_memory_space_constraint(x, pltpu.HBM) for x in (acts, grads, basis_in, basis_out)))
+
+
+def outer(lengths, own, *refs):
+    coded, out, grad = refs[:-2], refs[-2], refs[-1]
+    tokens, both = own.shape
+    half = both // 2
+    example = lax.axis_index("tensor") % lengths.shape[0]
+    count = lengths[example]
+    total = own[...]
+    for ref in coded:
+        shared = ref.shape[0] - tokens
+        log = ref[pl.ds(tokens, shared), :].astype(jnp.int32).astype(jnp.float32)
+        scale = jnp.exp2(log * (1.0 / STEPS)) * (1.0 / TOP)
+        codes = ref[pl.ds(0, tokens), :].astype(jnp.int32).astype(jnp.float32)
+        codes = codes.reshape(shared, tokens // shared, both) * scale[:, None, :]
+        total = total + codes.reshape(tokens, both)
+    row = lax.broadcasted_iota(jnp.int32, (tokens, both), 0)
+    lane = lax.broadcasted_iota(jnp.int32, (tokens, both), 1)
+    kept = jnp.where(row < count, total, 0.0)
+    weighted = jnp.where(lane < half, kept / count.astype(jnp.float32), kept)
+    first = weighted.astype(jnp.bfloat16)
+    rest = (weighted - first.astype(jnp.float32)).astype(jnp.bfloat16)
+    product = tn(first, first) + (tn(first, rest) + tn(rest, first))
+    grad[...] = product[:half, :]
+    even = grad[pl.ds(0, half // 2, stride=2), :][:, half:]
+    odd = grad[pl.ds(1, half // 2, stride=2), :][:, half:]
+    blocks = jnp.concatenate([even, odd], axis=1)
+    block_rows = blocks.shape[0] // 2
+    for t in range(4):
+        for x in range(2):
+            out[t * 2 + x] = blocks[x * block_rows : (x + 1) * block_rows]
+
+
+def through_fisher(grads, fisher, beside, out):
+    layers, depth, width = fisher.shape
+    lanes = grads.shape[2]
+    rows = grads.shape[0] // layers
+    cut = out.shape[2]
+    halves = width // cut
+    core = lax.axis_index("core")
+    steps = depth // lanes
+    for layer in range(layers):
+        mapped = None
+        for block, owner in ((fisher, core), (beside, 1 - core)):
+            parts = [
+                jnp.concatenate([grads[layer * rows + s, pl.ds(owner * steps + r, 1), :] for s in range(rows)], axis=0)
+                for r in range(steps)
+            ]
+            term = nn(thirds(jnp.concatenate(parts, axis=1)), block[layer])
+            mapped = term if mapped is None else mapped + term
+        mapped = add_thirds(mapped)
+        for x in range(2):
+            for e in range(rows // 2):
+                row = e * 2 + x
+                for h in range(halves):
+                    at = (layer * (rows // 2) + e) * halves + h
+                    piece = mapped[row : row + 1, h * cut : (h + 1) * cut]
+                    for t in range(4):
+                        out[t * 2 + x, pl.ds(at, 1), :] = piece
+
+
+def with_queries(mapped, *refs):
+    queries, out = refs[:-1], refs[-1]
+    layers = queries[0].shape[0]
+    groups = len(queries)
+    rows, cut = mapped.shape[1], mapped.shape[2]
+    halves = queries[0].shape[2] // cut
+    examples = rows // (layers * halves)
+    here = lax.axis_index("x") * 2 + lax.axis_index("core")
+    sums = [None] * (layers * halves)
+    for k, block in enumerate(queries):
+        column = here ^ k
+        left = thirds(mapped[column * 2] + mapped[column * 2 + 1])
+        for layer in range(layers):
+            for h in range(halves):
+                term = nt(left, block[layer, :, h * cut : (h + 1) * cut])
+                at = layer * halves + h
+                sums[at] = term if sums[at] is None else sums[at] + term
+    result = [None] * examples
+    for layer in range(layers):
+        for h in range(halves):
+            scores = add_thirds(sums[layer * halves + h])
+            for e in range(examples):
+                row = (layer * examples + e) * halves + h
+                term = scores[row : row + 1]
+                result[e] = term if result[e] is None else result[e] + term
+    out[...] = jnp.concatenate(result, axis=0)
+
+
+def swap(x, axis, flip):
+    return lax.ppermute(x, axis, [(i, i ^ flip) for i in range(lax.axis_size(axis))])
+
+
+def in_vmem(x):
+    return pltpu.with_memory_space_constraint(x, pltpu.VMEM)
+
+
+def small(acts_in, grads_out, basis_in, basis_out, lengths, fisher_inv, queries):
+    vmem = pl.BlockSpec(memory_space=pltpu.VMEM)
+    params = pltpu.CompilerParams(vmem_limit_bytes=VMEM)
+    proj_width = basis_in.shape[2]
+    operands = (acts_in, grads_out, jnp.swapaxes(basis_in, 1, 2), jnp.swapaxes(basis_out, 1, 2))
+
+    far, middle = projector((3, 2), (16, 16), *operands)
+    acts_in, grads_out, far, middle = lax.optimization_barrier((acts_in, grads_out, far, middle))
+    far, middle = swap(far, "tensor", 3), swap(middle, "tensor", 2)
+    near, own = projector((1, 0), (32, 0), acts_in, grads_out, *operands[2:])
+    far, near, own, fisher_inv, queries = lax.optimization_barrier((far, near, own, fisher_inv, queries))
+    near = swap(near, "tensor", 1)
+    across = swap(queries, "x", 1)
+    fisher_beside = swap(fisher_inv, "core", 1)
+    beside = swap(queries, "core", 1)
+
+    blocks = pl.pallas_call(
+        outer,
+        out_shape=jax.ShapeDtypeStruct((8, proj_width // 4, 2 * proj_width), jnp.float32),
+        in_specs=[pl.BlockSpec(memory_space=pltpu.SMEM)] + [vmem] * 4,
+        out_specs=vmem,
+        scratch_shapes=[pltpu.VMEM((proj_width, 2 * proj_width), jnp.float32)],
+        compiler_params=params,
+    )(lengths, own, far, middle, near)
+    blocks, beside, fisher_beside = lax.optimization_barrier((blocks, beside, fisher_beside))
+    blocks = lax.all_to_all(blocks, ("tensor", "x"), 0, 0, tiled=True)
+
+    mapped = pl.pallas_call(
+        through_fisher,
+        out_shape=jax.ShapeDtypeStruct((8, 8, fisher_inv.shape[2] // 2), jnp.float32),
+        in_specs=[vmem] * 3,
+        out_specs=vmem,
+        compiler_params=params,
+    )(blocks, in_vmem(fisher_inv), in_vmem(fisher_beside))
+    across, mapped = lax.optimization_barrier((across, mapped))
+    corner = swap(across, "core", 1)
+    mapped = lax.all_to_all(mapped, ("tensor", "x"), 0, 0, tiled=True)
+
+    return pl.pallas_call(
+        with_queries,
+        out_shape=jax.ShapeDtypeStruct((acts_in.shape[1], queries.shape[1]), jnp.float32),
+        in_specs=[vmem] * 5,
+        out_specs=vmem,
+        compiler_params=params,
+    )(mapped, queries, beside, across, corner)
+
+
+def general(acts_in, grads_out, basis_in, basis_out, lengths, fisher_inv, queries):
     proj_width = basis_in.shape[2]
     layer_count = acts_in.shape[0]
     local_examples = acts_in.shape[1]
@@ -32,19 +300,24 @@
         preferred_element_type=jnp.float32,
     )
     score_terms = jnp.einsum("lei,lqi->eq", row_blocks, mapped, precision=lax.Precision.HIGHEST)
-    scores = lax.psum_scatter(score_terms, "dp", scatter_dimension=0, tiled=True)
-    return scores
+    return lax.psum_scatter(score_terms, "dp", scatter_dimension=0, tiled=True)
 
 
 def solution(mesh):
+    dp = ("dp",)
+    local = general
+    if mesh.shape["tensor"] == 4 and mesh.shape["dp"] == 4:
+        mesh = jax.sharding.Mesh(mesh.devices.reshape(-1, 4, 2, 2), ("parts", "tensor", "x", "core"))
+        dp = ("x", "core")
+        local = small
     in_specs = (
-        P(None, ("parts", "dp"), None, "tensor"),
-        P(None, ("parts", "dp"), None, "tensor"),
+        P(None, ("parts", *dp), None, "tensor"),
+        P(None, ("parts", *dp), None, "tensor"),
         P(None, "tensor", None),
         P(None, "tensor", None),
-        P(("parts", "dp")),
-        P(None, "dp", "tensor"),
-        P(None, "tensor", "dp"),
+        P(("parts", *dp)),
+        P(None, dp, "tensor"),
+        P(None, "tensor", dp),
     )
-    out_specs = P(("parts", "dp"), "tensor")
+    out_specs = P(("parts", *dp), "tensor")
     return jax.shard_map(local, mesh=mesh, in_specs=in_specs, out_specs=out_specs, check_vma=False)

time: 372 us -> 57.3 us (0.15)
  waiting for transfers between devices: 293 us -> 7.02 us
  local copies, waits for them, and re-layouts: 29 us -> 0.02 us
  matrix products: 21.9 us -> 0 us
  blocking collectives: 6.95 us -> 25.4 us
  between operations: 15.6 us -> 0.12 us
  Pallas kernels: 0 us -> 14.9 us
  starting transfers between devices: 3.55 us -> 9.72 us
    all_gather x2 -> x0, waiting for transfers between devices: 236 us -> none  [the longest x1 236 us: local(): lax.all_gather(fisher_inv, 'tensor', axis=2, tiled=True)]
    psum x1 -> x0, waiting for transfers between devices: 53.4 us -> none  [local(): summed_proj = lax.psum(partial_proj, 'tensor')]
    all_to_all x0 -> x2, blocking collectives: none -> 25.4 us  [the longest x1 13.8 us: small(): blocks = lax.all_to_all(blocks, ('tensor', 'x'), 0, 0, tiled=True)]
    dot_general x5 -> x0, matrix products: 21.9 us -> none  [the longest x1 9.44 us: local(): jnp.einsum('lqj,lij->lqi', gathered_queries, lax.all_gather(fisher_inv, '...]
    unnamed x14 -> x6, local copies, waits for them, and re-layouts: 18.7 us -> 0.02 us
    pallas_call x0 -> x5, Pallas kernels: none -> 14.9 us  [the longest x2 10.6 us: projector(): pl.pallas_call(project_pairs, out_shape=[jax.ShapeDtypeStruct((tokens + t...]
    ppermute x0 -> x7, starting transfers between devices: none -> 9.72 us  [swap(): lax.ppermute(x, axis, [(i, i ^ flip) for i in range(lax.axis_size(axis))])]
    ppermute x0 -> x7, waiting for transfers between devices: none -> 7.02 us  [swap(): lax.ppermute(x, axis, [(i, i ^ flip) for i in range(lax.axis_size(axis))])]
  transfers between devices with their start and end apart: 4 -> 7, of which waited for: 3 -> 2; matrix products, arithmetic and copies ran while one was open for 8% -> 0% of each run, Pallas kernels for 0% -> 13%
where the time goes in v1:
time: 57.3 us; the launch traced here: 57.1 us
  blocking collectives  25.4 us (44%)
  Pallas kernels  14.9 us (26%)
  starting transfers between devices  9.72 us (17%)
  waiting for transfers between devices  7.02 us (12%)
    all_to_all x1, blocking collectives, small(): blocks = lax.all_to_all(blocks, ('tensor', 'x'), 0, 0, tiled=True)  13.8 us
    all_to_all x1, blocking collectives, small(): mapped = lax.all_to_all(mapped, ('tensor', 'x'), 0, 0, tiled=True)  11.6 us
    pallas_call x2, Pallas kernels, projector(): pl.pallas_call(project_pairs, out_shape=[jax.ShapeDtypeStruct((tokens + t...  10.6 us
    ppermute x7, starting transfers between devices, swap(): lax.ppermute(x, axis, [(i, i ^ flip) for i in range(lax.axis_size(axis))])  9.72 us
    ppermute x7, waiting for transfers between devices, swap(): lax.ppermute(x, axis, [(i, i ^ flip) for i in range(lax.axis_size(axis))])  7.02 us
    pallas_call x1, Pallas kernels, small(): pl.pallas_call(with_queries, out_shape=jax.ShapeDtypeStruct((acts_in.shap...  1.92 us
    pallas_call x1, Pallas kernels, small(): pl.pallas_call(through_fisher, out_shape=jax.ShapeDtypeStruct((8, 8, fish...  1.21 us
  transfers between devices with their start and end apart: 7, of which 2 were waited for; matrix products, arithmetic and copies ran while one was open for 0% of the time, Pallas kernels for 13%

profile of v1, /device:TPU:0, one launch (start us, length us, event | category | flops | bytes accessed | tf_op | source)
XLA Modules:
  0.0 57.1 jit_solution(17226622523572476579)
XLA Ops:
  0.0 5.3 %shard_map.73 = (s16[544,128]{1,0:T(8,128)(2,1)S(1)}, s16[544,128]{1,0:T(8,128)(2,1)S(1)}) custom-call(bf16[2,2,512,2048]{3,2,1,0:T(8,128)(2,1)} %refs_0_.2, bf16[2,2,512,2048]{3,2,1,0:T(8,128)(2,1)} %refs_1_.2, bf16[2,64,2048]{2,1,0:T(8,128)(2,1)} %bitcast.2, bf16[2,64,2048]{2,1,0:T(8,128)(2,1)} %bitcast.4), custom_call_target="tpu_custom_call" | custom-call | flops 536870912 | bytes 8388608 | tf_op jit(solution)/shard_map/pallas_call | solution.py:105
  5.3 0.0 copy-start
  5.4 0.0 copy-start.1
  5.4 0.0 copy-start.2
  5.4 5.1 %collective-permute-start = (s16[544,128]{1,0:T(8,128)(2,1)S(1)}, s16[544,128]{1,0:T(8,128)(2,1)S(1)}, u32[]{:S(2)}, u32[]{:S(2)}) collective-permute-start(s16[544,128]{1,0:T(8,128)(2,1)S(1)} %get-tuple-element.25), channel_id=1, source_target_pairs={{0,12},{4,8},{8,4},{12,0},{1,13},{5,9},{9,5},{13,1},{2,14},{6,10},... | collective-permute-start | bytes 417800 | tf_op jit(solution)/shard_map/ppermute | solution.py:221
  10.5 5.3 %shard_map.74 = (s16[528,128]{1,0:T(8,128)(2,1)S(1)}, f32[512,128]{1,0:T(8,128)S(1)}) custom-call(bf16[2,2,512,2048]{3,2,1,0:T(8,128)(2,1)} %refs_0_.2, bf16[2,2,512,2048]{3,2,1,0:T(8,128)(2,1)} %refs_1_.2, bf16[2,64,2048]{2,1,0:T(8,128)(2,1)} %bitcast.3, bf16[2,64,2048]{2,1,0:T(8,128)(2,1)} %bitcast.5), custom_call_target="tpu_custom_call" | custom-call | flops 536870912 | bytes 8388608 | tf_op jit(solution)/shard_map/pallas_call | solution.py:105
  15.8 0.0 collective-permute-done.refs_0_
  15.8 0.1 collective-permute-start.5
  15.9 0.5 collective-permute-start.4
  16.4 1.5 %collective-permute-start.1 = (bf16[2,256,1024]{2,1,0:T(8,128)(2,1)S(1)}, bf16[2,256,1024]{2,1,0:T(8,128)(2,1)S(1)}, u32[]{:S(2)}, u32[]{:S(2)}) collective-permute-start(bf16[2,256,1024]{2,1,0:T(8,128)(2,1)S(1)} %copy-done.1), channel_id=1, source_target_pairs={{0,2},{2,0},{1,3},{3,1},{4,6},{6,4},{5,7},{7,5},{8,10},{10,8},{9,1... | collective-permute-start | bytes 3145736 | tf_op jit(solution)/shard_map/ppermute | solution.py:221
  17.9 2.0 %collective-permute-start.2 = (s16[544,128]{1,0:T(8,128)(2,1)S(1)}, s16[544,128]{1,0:T(8,128)(2,1)S(1)}, u32[]{:S(2)}, u32[]{:S(2)}) collective-permute-start(s16[544,128]{1,0:T(8,128)(2,1)S(1)} %get-tuple-element.33), channel_id=1, source_target_pairs={{0,8},{4,12},{8,0},{12,4},{1,9},{5,13},{9,1},{13,5},{2,10},{6,14},... | collective-permute-start | bytes 417800 | tf_op jit(solution)/shard_map/ppermute | solution.py:221
  19.9 0.5 collective-permute-start.3
  20.4 6.9 %collective-permute-done.2.refs_1_ = s16[544,128]{1,0:T(8,128)(2,1)S(1)} collective-permute-done((s16[544,128]{1,0:T(8,128)(2,1)S(1)}, s16[544,128]{1,0:T(8,128)(2,1)S(1)}, u32[]{:S(2)}, u32[]{:S(2)}) %collective-permute-start.2) | collective-permute-done | bytes 139296 | tf_op jit(solution)/shard_map/ppermute | solution.py:221
  27.3 0.1 collective-permute-done.3.refs_2_
  27.4 1.1 %shard_map.75 = f32[8,16,128]{2,1,0:T(8,128)S(1)} custom-call(s32[2]{0:T(128)S(1)} %copy-done.2, f32[512,128]{1,0:T(8,128)S(1)} %get-tuple-element.31.own, s16[544,128]{1,0:T(8,128)(2,1)S(1)} %collective-permute-done.refs_0_, s16[544,128]{1,0:T(8,128)(2,1)S(1)} %collective-permute-done.2.refs_1_, s16[528,128]{1,0:T(8,128)(2,1)S(1)} %collective-permute-done.3.refs_2_), custom_call_target="tpu_custom_call" | custom-call | tf_op jit(solution)/shard_map/pallas_call | solution.py:244
  28.5 0.0 collective-permute-done.4.refs_1_
  28.5 0.0 collective-permute-done.5.beside
  28.5 13.8 %all_to_all.10.grads = f32[8,16,128]{2,1,0:T(8,128)S(1)} all-to-all(f32[8,16,128]{2,1,0:T(8,128)S(1)} %shard_map.75), channel_id=1, replica_groups=mesh['parts'=2,'tensor'=4,'x'=2,'core'=2] {'tensor','x'}, dimensions={0} | all-to-all | bytes 131072 | tf_op jit(solution)/shard_map/all_to_all | solution.py:253
  42.3 1.2 %shard_map.76 = f32[8,8,512]{2,1,0:T(8,128)S(1)} custom-call(f32[8,16,128]{2,1,0:T(8,128)S(1)} %all_to_all.10.grads, bf16[2,1024,1024]{2,1,0:T(8,128)(2,1)S(1)} %copy-done, bf16[2,1024,1024]{2,1,0:T(8,128)(2,1)S(1)} %collective-permute-done.5.beside), custom_call_target="tpu_custom_call" | custom-call | tf_op jit(solution)/shard_map/pallas_call | solution.py:255
  43.5 0.0 collective-permute-done.1.refs_2_
  43.5 0.1 collective-permute-start.6
  43.6 11.6 %all_to_all.11.mapped = f32[8,8,512]{2,1,0:T(8,128)S(1)} all-to-all(f32[8,8,512]{2,1,0:T(8,128)S(1)} %shard_map.76), channel_id=1, replica_groups=mesh['parts'=2,'tensor'=4,'x'=2,'core'=2] {'tensor','x'}, dimensions={0} | all-to-all | bytes 262144 | tf_op jit(solution)/shard_map/all_to_all | solution.py:264
  55.2 0.0 collective-permute-done.6.refs_3_
  55.2 1.9 %shard_map.77 = f32[2,256]{1,0:T(2,128)} custom-call(f32[8,8,512]{2,1,0:T(8,128)S(1)} %all_to_all.11.mapped, bf16[2,256,1024]{2,1,0:T(8,128)(2,1)S(1)} %copy-done.1, bf16[2,256,1024]{2,1,0:T(8,128)(2,1)S(1)} %collective-permute-done.4.refs_1_, bf16[2,256,1024]{2,1,0:T(8,128)(2,1)S(1)} %collective-permute-done.1.refs_2_, ...), custom_call_target="tpu_custom_call" | custom-call | tf_op jit(solution)/shard_map/pallas_call | solution.py:266
  (3 shorter events, 0.0 us)
Async XLA Ops:
  5.3 10.5 %copy-start = (bf16[2,1024,1024]{2,1,0:T(8,128)(2,1)S(1)}, bf16[2,1024,1024]{2,1,0:T(8,128)(2,1)}, u32[]{:S(2)}) copy-start(bf16[2,1024,1024]{2,1,0:T(8,128)(2,1)} %fisher) | copy-start | bytes 12582916
  5.4 10.6 %copy-start.1 = (bf16[2,256,1024]{2,1,0:T(8,128)(2,1)S(1)}, bf16[2,256,1024]{2,1,0:T(8,128)(2,1)}, u32[]{:S(2)}) copy-start(bf16[2,256,1024]{2,1,0:T(8,128)(2,1)} %refs_0_.3) | copy-start | bytes 3145732
  5.4 22.0 %copy-start.2 = (s32[2]{0:T(128)S(1)}, s32[2]{0:T(128)}, u32[]{:S(2)}) copy-start(s32[2]{0:T(128)} %lengths.1) | copy-start | bytes 28
  5.4 10.4 %collective-permute-start = (s16[544,128]{1,0:T(8,128)(2,1)S(1)}, s16[544,128]{1,0:T(8,128)(2,1)S(1)}, u32[]{:S(2)}, u32[]{:S(2)}) collective-permute-start(s16[544,128]{1,0:T(8,128)(2,1)S(1)} %get-tuple-element.25), channel_id=1, source_target_pairs={{0,12},{4,8},{8,4},{12,0},{1,13},{5,9},{9,5},{13,1},{2,14},{6,10},... | collective-permute-start | bytes 417800 | tf_op jit(solution)/shard_map/ppermute | solution.py:221
  15.8 12.7 %collective-permute-start.5 = (bf16[2,1024,1024]{2,1,0:T(8,128)(2,1)S(1)}, bf16[2,1024,1024]{2,1,0:T(8,128)(2,1)S(1)}, u32[]{:S(2)}, u32[]{:S(2)}) collective-permute-start(bf16[2,1024,1024]{2,1,0:T(8,128)(2,1)S(1)} %copy-done), channel_id=1, source_target_pairs={{0,1},{1,0},{2,3},{3,2},{4,5},{5,4},{6,7},{7,6},{8,9},{9,8},{10,11... | collective-permute-start | bytes 12582920 | tf_op jit(solution)/shard_map/ppermute | solution.py:221
  15.9 12.6 %collective-permute-start.4 = (bf16[2,256,1024]{2,1,0:T(8,128)(2,1)S(1)}, bf16[2,256,1024]{2,1,0:T(8,128)(2,1)S(1)}, u32[]{:S(2)}, u32[]{:S(2)}) collective-permute-start(bf16[2,256,1024]{2,1,0:T(8,128)(2,1)S(1)} %copy-done.1), channel_id=1, source_target_pairs={{0,1},{1,0},{2,3},{3,2},{4,5},{5,4},{6,7},{7,6},{8,9},{9,8},{10,11... | collective-permute-start | bytes 3145736 | tf_op jit(solution)/shard_map/ppermute | solution.py:221
  16.4 27.1 %collective-permute-start.1 = (bf16[2,256,1024]{2,1,0:T(8,128)(2,1)S(1)}, bf16[2,256,1024]{2,1,0:T(8,128)(2,1)S(1)}, u32[]{:S(2)}, u32[]{:S(2)}) collective-permute-start(bf16[2,256,1024]{2,1,0:T(8,128)(2,1)S(1)} %copy-done.1), channel_id=1, source_target_pairs={{0,2},{2,0},{1,3},{3,1},{4,6},{6,4},{5,7},{7,5},{8,10},{10,8},{9,1... | collective-permute-start | bytes 3145736 | tf_op jit(solution)/shard_map/ppermute | solution.py:221
  17.9 9.4 %collective-permute-start.2 = (s16[544,128]{1,0:T(8,128)(2,1)S(1)}, s16[544,128]{1,0:T(8,128)(2,1)S(1)}, u32[]{:S(2)}, u32[]{:S(2)}) collective-permute-start(s16[544,128]{1,0:T(8,128)(2,1)S(1)} %get-tuple-element.33), channel_id=1, source_target_pairs={{0,8},{4,12},{8,0},{12,4},{1,9},{5,13},{9,1},{13,5},{2,10},{6,14},... | collective-permute-start | bytes 417800 | tf_op jit(solution)/shard_map/ppermute | solution.py:221
  19.9 7.5 %collective-permute-start.3 = (s16[528,128]{1,0:T(8,128)(2,1)S(1)}, s16[528,128]{1,0:T(8,128)(2,1)S(1)}, u32[]{:S(2)}, u32[]{:S(2)}) collective-permute-start(s16[528,128]{1,0:T(8,128)(2,1)S(1)} %get-tuple-element.34), channel_id=1, source_target_pairs={{0,4},{4,0},{8,12},{12,8},{1,5},{5,1},{9,13},{13,9},{2,6},{6,2},{1... | collective-permute-start | bytes 405512 | tf_op jit(solution)/shard_map/ppermute | solution.py:221
  43.5 11.7 %collective-permute-start.6 = (bf16[2,256,1024]{2,1,0:T(8,128)(2,1)S(1)}, bf16[2,256,1024]{2,1,0:T(8,128)(2,1)S(1)}, u32[]{:S(2)}, u32[]{:S(2)}) collective-permute-start(bf16[2,256,1024]{2,1,0:T(8,128)(2,1)S(1)} %collective-permute-done.1.refs_2_), channel_id=1, source_target_pairs={{0,1},{1,0},{2,3},{3,2},{4,5},{5,4},{6,7},{7,6},{8,9},{9,8},{10,11... | collective-permute-start | bytes 3145736 | tf_op jit(solution)/shard_map/ppermute | solution.py:221

commit v2 on v1

--- a/solution.py
+++ b/solution.py
@@ -36,8 +36,9 @@
     return x[:rows] + (x[rows : 2 * rows] + x[2 * rows :])
 
 
-def project(flips, groups, acts, grads, basis_in, basis_out, *refs):
-    outs, (a_buf, g_buf, in_buf, out_buf, scale_log, sems, basis_sems) = refs[: len(flips)], refs[len(flips) :]
+def project(flips, groups, moves, acts, grads, basis_in, basis_out, *refs):
+    *refs, a_buf, g_buf, in_buf, out_buf, scale_log, sems, basis_sems, move_sems = refs
+    outs = refs[-len(flips) :]
     examples, tokens = acts.shape[1], acts.shape[2]
     here = lax.axis_index("tensor")
     layer = (here ^ flips[0]) // examples
@@ -57,6 +58,10 @@
                     pltpu.make_async_copy(acts.at[layer, example, rows, :], a_buf.at[at], sems.at[1, at]),
                 )
             )
+    moved = [
+        pltpu.make_async_copy(source, target, move_sems.at[i])
+        for i, (source, target) in enumerate(moves(*refs[: -len(flips)]))
+    ]
     for copy in bases:
         copy.start()
     for c in range(AHEAD):
@@ -65,6 +70,7 @@
     for copy in bases:
         copy.wait()
     for k, out in enumerate(outs):
+        group = groups[k]
         for c in range(CHUNKS):
             rows, at = pl.ds(c * size, size), k * CHUNKS + c
             for copy in copies[at]:
@@ -72,10 +78,12 @@
             if at + AHEAD < len(copies):
                 for copy in copies[at + AHEAD]:
                     copy.start()
+            elif at + AHEAD == len(copies):
+                for copy in moved:
+                    copy.start()
             proj_out = nt(g_buf[at], out_buf[...])
             proj_in = nt(a_buf[at], in_buf[...])
             both = jnp.concatenate([proj_out, proj_in], axis=1)
-            group = groups[k]
             if not group:
                 out[rows, :] = both
                 continue
@@ -90,28 +98,36 @@
         if group:
             log = scale_log[pl.ds(0, tokens // group), :]
             out[pl.ds(tokens, tokens // group), :] = log.astype(jnp.int32).astype(jnp.int16)
-
-
-def projector(flips, groups, acts, grads, basis_in, basis_out):
+    for copy in moved:
+        copy.wait()
+
+
+def no_moves():
+    return ()
+
+
+def projector(flips, groups, acts, grads, basis_in, basis_out, sources=(), targets=(), moves=no_moves, count=1):
     tokens, width = acts.shape[2], acts.shape[3]
     both = 2 * basis_in.shape[1]
-
-    def project_pairs(*refs):
-        project(flips, groups, *refs)
-
     pieces = len(flips) * CHUNKS
+    operands = (acts, grads, basis_in, basis_out, *sources)
     hbm = pl.BlockSpec(memory_space=pltpu.HBM)
     vmem = pl.BlockSpec(memory_space=pltpu.VMEM)
+
+    def project_pairs(*refs):
+        project(flips, groups, moves, *refs)
+
     return pl.pallas_call(
         project_pairs,
-        out_shape=[
+        out_shape=[*targets]
+        + [
             jax.ShapeDtypeStruct((tokens + tokens // g, both), jnp.int16)
             if g
             else jax.ShapeDtypeStruct((tokens, both), jnp.float32)
             for g in groups
         ],
-        in_specs=[hbm] * 4,
-        out_specs=[vmem] * len(groups),
+        in_specs=[hbm] * len(operands),
+        out_specs=[vmem] * (len(targets) + len(groups)),
         scratch_shapes=[
             pltpu.VMEM((pieces, tokens // CHUNKS, width), acts.dtype),
             pltpu.VMEM((pieces, tokens // CHUNKS, width), grads.dtype),
@@ -120,6 +136,7 @@
             pltpu.VMEM((tokens // 16, both), jnp.float32),
             pltpu.SemaphoreType.DMA((2, pieces)),
             pltpu.SemaphoreType.DMA((2,)),
+            pltpu.SemaphoreType.DMA((count,)),
         ],
         compiler_params=pltpu.CompilerParams(vmem_limit_bytes=VMEM),
         cost_estimate=pl.CostEstimate(
@@ -127,23 +144,36 @@
             bytes_accessed=4 * len(flips) * tokens * width,
             transcendentals=0,
         ),
-    )(*(pltpu.with_memory_space_constraint(x, pltpu.HBM) for x in (acts, grads, basis_in, basis_out)))
-
-
-def outer(lengths, own, *refs):
-    coded, out, grad = refs[:-2], refs[-2], refs[-1]
-    tokens, both = own.shape
+    )(*(pltpu.with_memory_space_constraint(x, pltpu.HBM) for x in operands))
+
+
+def blocks_together(fisher, queries, both):
+    for layer in range(fisher.shape[0]):
+        depth, rows = fisher.shape[1], queries.shape[1]
+        yield fisher.at[layer], both.at[layer, pl.ds(0, depth), :]
+        yield queries.at[layer], both.at[layer, pl.ds(depth, rows), :]
+
+
+def decode(ref, tokens):
+    shared = ref.shape[0] - tokens
+    both = ref.shape[1]
+    log = ref[pl.ds(tokens, shared), :].astype(jnp.int32).astype(jnp.float32)
+    scale = jnp.exp2(log * (1.0 / STEPS)) * (1.0 / TOP)
+    codes = ref[pl.ds(0, tokens), :].astype(jnp.int32).astype(jnp.float32)
+    return (codes.reshape(shared, tokens // shared, both) * scale[:, None, :]).reshape(tokens, both)
+
+
+def add_up(own, first, second, out):
+    tokens = own.shape[0]
+    out[...] = own[...] + decode(first, tokens) + decode(second, tokens)
+
+
+def outer(lengths, most, last, out, grad):
+    tokens, both = most.shape
     half = both // 2
     example = lax.axis_index("tensor") % lengths.shape[0]
     count = lengths[example]
-    total = own[...]
-    for ref in coded:
-        shared = ref.shape[0] - tokens
-        log = ref[pl.ds(tokens, shared), :].astype(jnp.int32).astype(jnp.float32)
-        scale = jnp.exp2(log * (1.0 / STEPS)) * (1.0 / TOP)
-        codes = ref[pl.ds(0, tokens), :].astype(jnp.int32).astype(jnp.float32)
-        codes = codes.reshape(shared, tokens // shared, both) * scale[:, None, :]
-        total = total + codes.reshape(tokens, both)
+    total = most[...] + decode(last, tokens)
     row = lax.broadcasted_iota(jnp.int32, (tokens, both), 0)
     lane = lax.broadcasted_iota(jnp.int32, (tokens, both), 1)
     kept = jnp.where(row < count, total, 0.0)
@@ -162,9 +192,10 @@
 
 
 def through_fisher(grads, fisher, beside, out):
-    layers, depth, width = fisher.shape
+    layers, _, width = fisher.shape
     lanes = grads.shape[2]
     rows = grads.shape[0] // layers
+    depth = grads.shape[1] * lanes // 2
     cut = out.shape[2]
     halves = width // cut
     core = lax.axis_index("core")
@@ -176,7 +207,7 @@
                 jnp.concatenate([grads[layer * rows + s, pl.ds(owner * steps + r, 1), :] for s in range(rows)], axis=0)
                 for r in range(steps)
             ]
-            term = nn(thirds(jnp.concatenate(parts, axis=1)), block[layer])
+            term = nn(thirds(jnp.concatenate(parts, axis=1)), block[layer, pl.ds(0, depth), :])
             mapped = term if mapped is None else mapped + term
         mapped = add_thirds(mapped)
         for x in range(2):
@@ -189,21 +220,19 @@
                         out[t * 2 + x, pl.ds(at, 1), :] = piece
 
 
-def with_queries(mapped, *refs):
-    queries, out = refs[:-1], refs[-1]
-    layers = queries[0].shape[0]
-    groups = len(queries)
-    rows, cut = mapped.shape[1], mapped.shape[2]
-    halves = queries[0].shape[2] // cut
-    examples = rows // (layers * halves)
+def with_queries(mapped, own, beside, across, corner, out):
+    layers, cut = own.shape[0], mapped.shape[2]
+    halves = own.shape[2] // cut
+    count = out.shape[1]
+    examples = mapped.shape[1] // (layers * halves)
     here = lax.axis_index("x") * 2 + lax.axis_index("core")
     sums = [None] * (layers * halves)
-    for k, block in enumerate(queries):
-        column = here ^ k
-        left = thirds(mapped[column * 2] + mapped[column * 2 + 1])
+    for k, block in enumerate((own, beside, across, corner)):
+        left = thirds(mapped[(here ^ k) * 2] + mapped[(here ^ k) * 2 + 1])
+        rows = pl.ds(block.shape[1] - count, count)
         for layer in range(layers):
             for h in range(halves):
-                term = nt(left, block[layer, :, h * cut : (h + 1) * cut])
+                term = nt(left, block[layer, rows, h * cut : (h + 1) * cut])
                 at = layer * halves + h
                 sums[at] = term if sums[at] is None else sums[at] + term
     result = [None] * examples
@@ -232,24 +261,33 @@
     operands = (acts_in, grads_out, jnp.swapaxes(basis_in, 1, 2), jnp.swapaxes(basis_out, 1, 2))
 
     far, middle = projector((3, 2), (16, 16), *operands)
-    acts_in, grads_out, far, middle = lax.optimization_barrier((acts_in, grads_out, far, middle))
+    acts_in, grads_out, fisher_inv, queries, far, middle = lax.optimization_barrier(
+        (acts_in, grads_out, fisher_inv, queries, far, middle)
+    )
     far, middle = swap(far, "tensor", 3), swap(middle, "tensor", 2)
-    near, own = projector((1, 0), (32, 0), acts_in, grads_out, *operands[2:])
-    far, near, own, fisher_inv, queries = lax.optimization_barrier((far, near, own, fisher_inv, queries))
+    across = swap(queries, "x", 1)
+    near, here = projector((1, 0), (32, 0), acts_in, grads_out, *operands[2:])
     near = swap(near, "tensor", 1)
-    across = swap(queries, "x", 1)
     fisher_beside = swap(fisher_inv, "core", 1)
-    beside = swap(queries, "core", 1)
+
+    most = pl.pallas_call(
+        add_up,
+        out_shape=jax.ShapeDtypeStruct(here.shape, jnp.float32),
+        in_specs=[vmem] * 3,
+        out_specs=vmem,
+        compiler_params=params,
+        cost_estimate=pl.CostEstimate(flops=0, bytes_accessed=1 << 21, transcendentals=0),
+    )(here, far, middle)
 
     blocks = pl.pallas_call(
         outer,
         out_shape=jax.ShapeDtypeStruct((8, proj_width // 4, 2 * proj_width), jnp.float32),
-        in_specs=[pl.BlockSpec(memory_space=pltpu.SMEM)] + [vmem] * 4,
+        in_specs=[pl.BlockSpec(memory_space=pltpu.SMEM)] + [vmem] * 2,
         out_specs=vmem,
         scratch_shapes=[pltpu.VMEM((proj_width, 2 * proj_width), jnp.float32)],
         compiler_params=params,
-    )(lengths, own, far, middle, near)
-    blocks, beside, fisher_beside = lax.optimization_barrier((blocks, beside, fisher_beside))
+    )(lengths, most, near)
+    blocks, fisher_beside = lax.optimization_barrier((blocks, fisher_beside))
     blocks = lax.all_to_all(blocks, ("tensor", "x"), 0, 0, tiled=True)
 
     mapped = pl.pallas_call(
@@ -259,8 +297,8 @@
         out_specs=vmem,
         compiler_params=params,
     )(blocks, in_vmem(fisher_inv), in_vmem(fisher_beside))
-    across, mapped = lax.optimization_barrier((across, mapped))
-    corner = swap(across, "core", 1)
+    across, queries, mapped = lax.optimization_barrier((across, queries, mapped))
+    corner, beside = swap(across, "core", 1), swap(queries, "core", 1)
     mapped = lax.all_to_all(mapped, ("tensor", "x"), 0, 0, tiled=True)
 
     return pl.pallas_call(
@@ -306,8 +344,8 @@
 def solution(mesh):
     dp = ("dp",)
     local = general
-    if mesh.shape["tensor"] == 4 and mesh.shape["dp"] == 4:
-        mesh = jax.sharding.Mesh(mesh.devices.reshape(-1, 4, 2, 2), ("parts", "tensor", "x", "core"))
+    if (mesh.shape["parts"], mesh.shape["tensor"], mesh.shape["dp"]) == (2, 4, 4):
+        mesh = jax.sharding.Mesh(mesh.devices.reshape(2, 4, 2, 2), ("parts", "tensor", "x", "core"))
         dp = ("x", "core")
         local = small
     in_specs = (

time: 57.3 us -> 51.9 us (0.906)
  blocking collectives: 25.4 us -> 20.2 us
  starting transfers between devices: 9.72 us -> 8.11 us
  Pallas kernels: 14.9 us -> 15.8 us
    all_to_all x1, blocking collectives: 13.8 us -> 10.3 us  [small(): blocks = lax.all_to_all(blocks, ('tensor', 'x'), 0, 0, tiled=True)]
    all_to_all x1, blocking collectives: 11.6 us -> 9.89 us  [small(): mapped = lax.all_to_all(mapped, ('tensor', 'x'), 0, 0, tiled=True)]
    ppermute x7, starting transfers between devices: 9.72 us -> 8.11 us  [swap(): lax.ppermute(x, axis, [(i, i ^ flip) for i in range(lax.axis_size(axis))])]
    pallas_call x2 -> x3, Pallas kernels: 10.6 us -> 11.7 us  [the longest x2 11.6 us: projector(): pl.pallas_call(project_pairs, out_shape=[*targets] + [jax.ShapeDtypeStruc...]
  transfers between devices with their start and end apart: 7 -> 7, of which waited for: 2 -> 2; matrix products, arithmetic and copies ran while one was open for 0% -> 0% of each run, Pallas kernels for 13% -> 15%
where the time goes in v2:
time: 51.9 us; the launch traced here: 51.7 us
  blocking collectives  20.2 us (39%)
  Pallas kernels  15.8 us (30%)
  starting transfers between devices  8.11 us (16%)
  waiting for transfers between devices  7.48 us (14%)
    pallas_call x2, Pallas kernels, projector(): pl.pallas_call(project_pairs, out_shape=[*targets] + [jax.ShapeDtypeStruc...  11.6 us
    all_to_all x1, blocking collectives, small(): blocks = lax.all_to_all(blocks, ('tensor', 'x'), 0, 0, tiled=True)  10.3 us
    all_to_all x1, blocking collectives, small(): mapped = lax.all_to_all(mapped, ('tensor', 'x'), 0, 0, tiled=True)  9.89 us
    ppermute x7, starting transfers between devices, swap(): lax.ppermute(x, axis, [(i, i ^ flip) for i in range(lax.axis_size(axis))])  8.11 us
    ppermute x7, waiting for transfers between devices, swap(): lax.ppermute(x, axis, [(i, i ^ flip) for i in range(lax.axis_size(axis))])  7.48 us
    pallas_call x1, Pallas kernels, small(): pl.pallas_call(with_queries, out_shape=jax.ShapeDtypeStruct((acts_in.shap...  1.92 us
    pallas_call x1, Pallas kernels, small(): pl.pallas_call(through_fisher, out_shape=jax.ShapeDtypeStruct((8, 8, fish...  1.21 us
  transfers between devices with their start and end apart: 7, of which 2 were waited for; matrix products, arithmetic and copies ran while one was open for 0% of the time, Pallas kernels for 15%

profile of v2, /device:TPU:0, one launch (start us, length us, event | category | flops | bytes accessed | tf_op | source)
XLA Modules:
  0.0 51.7 jit_solution(6901210466627924457)
XLA Ops:
  0.0 6.3 %shard_map.73 = (s16[544,128]{1,0:T(8,128)(2,1)S(1)}, s16[544,128]{1,0:T(8,128)(2,1)S(1)}) custom-call(bf16[2,2,512,2048]{3,2,1,0:T(8,128)(2,1)} %refs_0_.2, bf16[2,2,512,2048]{3,2,1,0:T(8,128)(2,1)} %refs_1_.2, bf16[2,64,2048]{2,1,0:T(8,128)(2,1)} %bitcast.2, bf16[2,64,2048]{2,1,0:T(8,128)(2,1)} %bitcast.4), custom_call_target="tpu_custom_call" | custom-call | flops 536870912 | bytes 8388608 | tf_op jit(solution)/shard_map/pallas_call | solution.py:120
  6.3 0.0 copy-done
  6.3 0.0 copy-start.2
  6.3 0.5 %collective-permute-start.4 = (bf16[2,1024,1024]{2,1,0:T(8,128)(2,1)S(1)}, bf16[2,1024,1024]{2,1,0:T(8,128)(2,1)S(1)}, u32[]{:S(2)}, u32[]{:S(2)}) collective-permute-start(bf16[2,1024,1024]{2,1,0:T(8,128)(2,1)S(1)} %copy-done), channel_id=1, source_target_pairs={{0,1},{1,0},{2,3},{3,2},{4,5},{5,4},{6,7},{7,6},{8,9},{9,8},{10,11... | collective-permute-start | bytes 12582920 | tf_op jit(solution)/shard_map/ppermute | solution.py:250
  6.8 2.6 %collective-permute-start = (bf16[2,256,1024]{2,1,0:T(8,128)(2,1)S(1)}, bf16[2,256,1024]{2,1,0:T(8,128)(2,1)S(1)}, u32[]{:S(2)}, u32[]{:S(2)}) collective-permute-start(bf16[2,256,1024]{2,1,0:T(8,128)(2,1)S(1)} %copy-done.1), channel_id=1, source_target_pairs={{0,2},{2,0},{1,3},{3,1},{4,6},{6,4},{5,7},{7,5},{8,10},{10,8},{9,1... | collective-permute-start | bytes 3145736 | tf_op jit(solution)/shard_map/ppermute | solution.py:250
  9.4 3.6 %collective-permute-start.1 = (s16[544,128]{1,0:T(8,128)(2,1)S(1)}, s16[544,128]{1,0:T(8,128)(2,1)S(1)}, u32[]{:S(2)}, u32[]{:S(2)}) collective-permute-start(s16[544,128]{1,0:T(8,128)(2,1)S(1)} %get-tuple-element.26), channel_id=1, source_target_pairs={{0,12},{4,8},{8,4},{12,0},{1,13},{5,9},{9,5},{13,1},{2,14},{6,10},... | collective-permute-start | bytes 417800 | tf_op jit(solution)/shard_map/ppermute | solution.py:250
  13.0 0.0 collective-permute-start.2
  13.0 5.3 %shard_map.74 = (s16[528,128]{1,0:T(8,128)(2,1)S(1)}, f32[512,128]{1,0:T(8,128)S(1)}) custom-call(bf16[2,2,512,2048]{3,2,1,0:T(8,128)(2,1)} %refs_0_.2, bf16[2,2,512,2048]{3,2,1,0:T(8,128)(2,1)} %refs_1_.2, bf16[2,64,2048]{2,1,0:T(8,128)(2,1)} %bitcast.3, bf16[2,64,2048]{2,1,0:T(8,128)(2,1)} %bitcast.5), custom_call_target="tpu_custom_call" | custom-call | flops 536870912 | bytes 8388608 | tf_op jit(solution)/shard_map/pallas_call | solution.py:120
  18.3 0.8 %collective-permute-start.3 = (s16[528,128]{1,0:T(8,128)(2,1)S(1)}, s16[528,128]{1,0:T(8,128)(2,1)S(1)}, u32[]{:S(2)}, u32[]{:S(2)}) collective-permute-start(s16[528,128]{1,0:T(8,128)(2,1)S(1)} %get-tuple-element.28), channel_id=1, source_target_pairs={{0,4},{4,0},{8,12},{12,8},{1,5},{5,1},{9,13},{13,9},{2,6},{6,2},{1... | collective-permute-start | bytes 405512 | tf_op jit(solution)/shard_map/ppermute | solution.py:250
  19.2 0.0 collective-permute-done.1.first
  19.2 6.0 %collective-permute-done.2.second = s16[544,128]{1,0:T(8,128)(2,1)S(1)} collective-permute-done((s16[544,128]{1,0:T(8,128)(2,1)S(1)}, s16[544,128]{1,0:T(8,128)(2,1)S(1)}, u32[]{:S(2)}, u32[]{:S(2)}) %collective-permute-start.2) | collective-permute-done | bytes 139296 | tf_op jit(solution)/shard_map/ppermute | solution.py:250
  25.2 0.1 shard_map.75.most
  25.3 1.4 %collective-permute-done.3.last = s16[528,128]{1,0:T(8,128)(2,1)S(1)} collective-permute-done((s16[528,128]{1,0:T(8,128)(2,1)S(1)}, s16[528,128]{1,0:T(8,128)(2,1)S(1)}, u32[]{:S(2)}, u32[]{:S(2)}) %collective-permute-start.3) | collective-permute-done | bytes 135200 | tf_op jit(solution)/shard_map/ppermute | solution.py:250
  26.8 1.0 %shard_map.76 = f32[8,16,128]{2,1,0:T(8,128)S(1)} custom-call(s32[2]{0:T(128)S(1)} %copy-done.2, f32[512,128]{1,0:T(8,128)S(1)} %shard_map.75.most, s16[528,128]{1,0:T(8,128)(2,1)S(1)} %collective-permute-done.3.last), custom_call_target="tpu_custom_call" | custom-call | tf_op jit(solution)/shard_map/pallas_call | solution.py:282
  27.7 0.0 collective-permute-done.4.beside
  27.7 10.3 %all_to_all.10.grads = f32[8,16,128]{2,1,0:T(8,128)S(1)} all-to-all(f32[8,16,128]{2,1,0:T(8,128)S(1)} %shard_map.76), channel_id=1, replica_groups=mesh['parts'=2,'tensor'=4,'x'=2,'core'=2] {'tensor','x'}, dimensions={0} | all-to-all | bytes 131072 | tf_op jit(solution)/shard_map/all_to_all | solution.py:291
  38.1 1.2 %shard_map.77 = f32[8,8,512]{2,1,0:T(8,128)S(1)} custom-call(f32[8,16,128]{2,1,0:T(8,128)S(1)} %all_to_all.10.grads, bf16[2,1024,1024]{2,1,0:T(8,128)(2,1)S(1)} %copy-done, bf16[2,1024,1024]{2,1,0:T(8,128)(2,1)S(1)} %collective-permute-done.4.beside), custom_call_target="tpu_custom_call" | custom-call | tf_op jit(solution)/shard_map/pallas_call | solution.py:293
  39.3 0.0 collective-permute-done.across
  39.3 0.1 collective-permute-start.5
  39.4 0.5 collective-permute-start.6
  39.9 9.9 %all_to_all.11.mapped = f32[8,8,512]{2,1,0:T(8,128)S(1)} all-to-all(f32[8,8,512]{2,1,0:T(8,128)S(1)} %shard_map.77), channel_id=1, replica_groups=mesh['parts'=2,'tensor'=4,'x'=2,'core'=2] {'tensor','x'}, dimensions={0} | all-to-all | bytes 262144 | tf_op jit(solution)/shard_map/all_to_all | solution.py:302
  49.8 0.0 collective-permute-done.5.beside
  49.8 0.0 collective-permute-done.6.corner
  49.8 1.9 %shard_map.78 = f32[2,256]{1,0:T(2,128)} custom-call(f32[8,8,512]{2,1,0:T(8,128)S(1)} %all_to_all.11.mapped, bf16[2,256,1024]{2,1,0:T(8,128)(2,1)S(1)} %copy-done.1, bf16[2,256,1024]{2,1,0:T(8,128)(2,1)S(1)} %collective-permute-done.5.beside, bf16[2,256,1024]{2,1,0:T(8,128)(2,1)S(1)} %collective-permute-done.across, ...), custom_call_target="tpu_custom_call" | custom-call | tf_op jit(solution)/shard_map/pallas_call | solution.py:304
  (4 shorter events, 0.0 us)
Async XLA Ops:
  0.0 6.3 %copy-start = (bf16[2,1024,1024]{2,1,0:T(8,128)(2,1)S(1)}, bf16[2,1024,1024]{2,1,0:T(8,128)(2,1)}, u32[]{:S(2)}) copy-start(bf16[2,1024,1024]{2,1,0:T(8,128)(2,1)} %fisher) | copy-start | bytes 12582916
  0.0 6.8 %copy-start.1 = (bf16[2,256,1024]{2,1,0:T(8,128)(2,1)S(1)}, bf16[2,256,1024]{2,1,0:T(8,128)(2,1)}, u32[]{:S(2)}) copy-start(bf16[2,256,1024]{2,1,0:T(8,128)(2,1)} %own) | copy-start | bytes 3145732
  6.3 20.5 %copy-start.2 = (s32[2]{0:T(128)S(1)}, s32[2]{0:T(128)}, u32[]{:S(2)}) copy-start(s32[2]{0:T(128)} %lengths.1) | copy-start | bytes 28
  6.3 21.4 %collective-permute-start.4 = (bf16[2,1024,1024]{2,1,0:T(8,128)(2,1)S(1)}, bf16[2,1024,1024]{2,1,0:T(8,128)(2,1)S(1)}, u32[]{:S(2)}, u32[]{:S(2)}) collective-permute-start(bf16[2,1024,1024]{2,1,0:T(8,128)(2,1)S(1)} %copy-done), channel_id=1, source_target_pairs={{0,1},{1,0},{2,3},{3,2},{4,5},{5,4},{6,7},{7,6},{8,9},{9,8},{10,11... | collective-permute-start | bytes 12582920 | tf_op jit(solution)/shard_map/ppermute | solution.py:250
  6.8 32.5 %collective-permute-start = (bf16[2,256,1024]{2,1,0:T(8,128)(2,1)S(1)}, bf16[2,256,1024]{2,1,0:T(8,128)(2,1)S(1)}, u32[]{:S(2)}, u32[]{:S(2)}) collective-permute-start(bf16[2,256,1024]{2,1,0:T(8,128)(2,1)S(1)} %copy-done.1), channel_id=1, source_target_pairs={{0,2},{2,0},{1,3},{3,1},{4,6},{6,4},{5,7},{7,5},{8,10},{10,8},{9,1... | collective-permute-start | bytes 3145736 | tf_op jit(solution)/shard_map/ppermute | solution.py:250
  9.4 9.8 %collective-permute-start.1 = (s16[544,128]{1,0:T(8,128)(2,1)S(1)}, s16[544,128]{1,0:T(8,128)(2,1)S(1)}, u32[]{:S(2)}, u32[]{:S(2)}) collective-permute-start(s16[544,128]{1,0:T(8,128)(2,1)S(1)} %get-tuple-element.26), channel_id=1, source_target_pairs={{0,12},{4,8},{8,4},{12,0},{1,13},{5,9},{9,5},{13,1},{2,14},{6,10},... | collective-permute-start | bytes 417800 | tf_op jit(solution)/shard_map/ppermute | solution.py:250
  13.0 12.2 %collective-permute-start.2 = (s16[544,128]{1,0:T(8,128)(2,1)S(1)}, s16[544,128]{1,0:T(8,128)(2,1)S(1)}, u32[]{:S(2)}, u32[]{:S(2)}) collective-permute-start(s16[544,128]{1,0:T(8,128)(2,1)S(1)} %get-tuple-element.27), channel_id=1, source_target_pairs={{0,8},{4,12},{8,0},{12,4},{1,9},{5,13},{9,1},{13,5},{2,10},{6,14},... | collective-permute-start | bytes 417800 | tf_op jit(solution)/shard_map/ppermute | solution.py:250
  18.3 8.4 %collective-permute-start.3 = (s16[528,128]{1,0:T(8,128)(2,1)S(1)}, s16[528,128]{1,0:T(8,128)(2,1)S(1)}, u32[]{:S(2)}, u32[]{:S(2)}) collective-permute-start(s16[528,128]{1,0:T(8,128)(2,1)S(1)} %get-tuple-element.28), channel_id=1, source_target_pairs={{0,4},{4,0},{8,12},{12,8},{1,5},{5,1},{9,13},{13,9},{2,6},{6,2},{1... | collective-permute-start | bytes 405512 | tf_op jit(solution)/shard_map/ppermute | solution.py:250
  39.3 10.5 %collective-permute-start.5 = (bf16[2,256,1024]{2,1,0:T(8,128)(2,1)S(1)}, bf16[2,256,1024]{2,1,0:T(8,128)(2,1)S(1)}, u32[]{:S(2)}, u32[]{:S(2)}) collective-permute-start(bf16[2,256,1024]{2,1,0:T(8,128)(2,1)S(1)} %copy-done.1), channel_id=1, source_target_pairs={{0,1},{1,0},{2,3},{3,2},{4,5},{5,4},{6,7},{7,6},{8,9},{9,8},{10,11... | collective-permute-start | bytes 3145736 | tf_op jit(solution)/shard_map/ppermute | solution.py:250
  39.4 10.4 %collective-permute-start.6 = (bf16[2,256,1024]{2,1,0:T(8,128)(2,1)S(1)}, bf16[2,256,1024]{2,1,0:T(8,128)(2,1)S(1)}, u32[]{:S(2)}, u32[]{:S(2)}) collective-permute-start(bf16[2,256,1024]{2,1,0:T(8,128)(2,1)S(1)} %collective-permute-done.across), channel_id=1, source_target_pairs={{0,1},{1,0},{2,3},{3,2},{4,5},{5,4},{6,7},{7,6},{8,9},{9,8},{10,11... | collective-permute-start | bytes 3145736 | tf_op jit(solution)/shard_map/ppermute | solution.py:250

commit v3 on v2

--- a/solution.py
+++ b/solution.py
@@ -7,7 +7,8 @@
 
 STEPS = 64.0
 TOP = 32767.0
-CHUNKS = 2
+PIECES_TWO = ((128, 384), (256, 256))
+PIECES_ONE = ((128, 384),)
 AHEAD = 2
 VMEM = 24 * 1024 * 1024
 
@@ -36,90 +37,91 @@
     return x[:rows] + (x[rows : 2 * rows] + x[2 * rows :])
 
 
-def project(flips, groups, moves, acts, grads, basis_in, basis_out, *refs):
-    *refs, a_buf, g_buf, in_buf, out_buf, scale_log, sems, basis_sems, move_sems = refs
-    outs = refs[-len(flips) :]
+def project(flips, groups, pieces, turn, acts, grads, basis_in, basis_out, *refs):
+    *refs, a_buf, g_buf, in_buf, out_buf, scale_log, sems, basis_sems = refs
+    queries = turned = turn_buf = None
+    if turn:
+        *refs, turn_buf = refs
+        queries, turned, *refs = refs
+    outs = refs
     examples, tokens = acts.shape[1], acts.shape[2]
     here = lax.axis_index("tensor")
     layer = (here ^ flips[0]) // examples
-    size = tokens // CHUNKS
-    bases = (
+    first = [
         pltpu.make_async_copy(basis_out.at[layer], out_buf, basis_sems.at[0]),
         pltpu.make_async_copy(basis_in.at[layer], in_buf, basis_sems.at[1]),
-    )
-    copies = []
+    ]
+    if turn:
+        first.append(pltpu.make_async_copy(queries, turn_buf, basis_sems.at[2]))
+    copies, spans = [], []
     for k, flip in enumerate(flips):
         example = (here ^ flip) % examples
-        for c in range(CHUNKS):
-            rows, at = pl.ds(c * size, size), k * CHUNKS + c
+        begin = 0
+        for size in pieces[k]:
+            rows, at = pl.ds(begin, size), len(copies)
+            spans.append((k, begin, size))
             copies.append(
                 (
-                    pltpu.make_async_copy(grads.at[layer, example, rows, :], g_buf.at[at], sems.at[0, at]),
-                    pltpu.make_async_copy(acts.at[layer, example, rows, :], a_buf.at[at], sems.at[1, at]),
+                    pltpu.make_async_copy(grads.at[layer, example, rows, :], g_buf.at[k, rows, :], sems.at[0, at]),
+                    pltpu.make_async_copy(acts.at[layer, example, rows, :], a_buf.at[k, rows, :], sems.at[1, at]),
                 )
             )
-    moved = [
-        pltpu.make_async_copy(source, target, move_sems.at[i])
-        for i, (source, target) in enumerate(moves(*refs[: -len(flips)]))
-    ]
-    for copy in bases:
+            begin += size
+    for copy in first:
         copy.start()
     for c in range(AHEAD):
         for copy in copies[c]:
             copy.start()
-    for copy in bases:
+    for copy in first:
         copy.wait()
-    for k, out in enumerate(outs):
-        group = groups[k]
-        for c in range(CHUNKS):
-            rows, at = pl.ds(c * size, size), k * CHUNKS + c
-            for copy in copies[at]:
-                copy.wait()
-            if at + AHEAD < len(copies):
-                for copy in copies[at + AHEAD]:
-                    copy.start()
-            elif at + AHEAD == len(copies):
-                for copy in moved:
-                    copy.start()
-            proj_out = nt(g_buf[at], out_buf[...])
-            proj_in = nt(a_buf[at], in_buf[...])
-            both = jnp.concatenate([proj_out, proj_in], axis=1)
-            if not group:
-                out[rows, :] = both
-                continue
-            grouped = both.reshape(size // group, group, both.shape[1])
-            most = jnp.maximum(jnp.max(jnp.abs(grouped), axis=1), 1e-30)
-            log = jnp.ceil(jnp.log2(most) * STEPS)
-            scale = jnp.exp2(log * (-1.0 / STEPS)) * TOP
-            codes = jnp.round(grouped * scale[:, None, :])
-            codes = jnp.minimum(jnp.maximum(codes, -TOP), TOP).reshape(both.shape)
-            out[rows, :] = codes.astype(jnp.int32).astype(jnp.int16)
-            scale_log[pl.ds(c * (size // group), size // group), :] = log
-        if group:
+    if turn:
+        for q in range(turned.shape[0]):
+            turned[q] = turn_buf[q].T
+    for at, (k, begin, size) in enumerate(spans):
+        group, out, rows = groups[k], outs[k], pl.ds(begin, size)
+        for copy in copies[at]:
+            copy.wait()
+        if at + AHEAD < len(copies):
+            for copy in copies[at + AHEAD]:
+                copy.start()
+        proj_out = nt(g_buf[k, rows, :], out_buf[...])
+        proj_in = nt(a_buf[k, rows, :], in_buf[...])
+        both = jnp.concatenate([proj_out, proj_in], axis=1)
+        if not group:
+            out[rows, :] = both
+            continue
+        grouped = both.reshape(size // group, group, both.shape[1])
+        most = jnp.maximum(jnp.max(jnp.abs(grouped), axis=1), 1e-30)
+        log = jnp.ceil(jnp.log2(most) * STEPS)
+        scale = jnp.exp2(log * (-1.0 / STEPS)) * TOP
+        codes = jnp.round(grouped * scale[:, None, :])
+        codes = jnp.minimum(jnp.maximum(codes, -TOP), TOP).reshape(both.shape)
+        out[rows, :] = codes.astype(jnp.int32).astype(jnp.int16)
+        scale_log[pl.ds(begin // group, size // group), :] = log
+        if begin + size == tokens:
             log = scale_log[pl.ds(0, tokens // group), :]
             out[pl.ds(tokens, tokens // group), :] = log.astype(jnp.int32).astype(jnp.int16)
-    for copy in moved:
-        copy.wait()
-
-
-def no_moves():
-    return ()
-
-
-def projector(flips, groups, acts, grads, basis_in, basis_out, sources=(), targets=(), moves=no_moves, count=1):
+
+
+def projector(flips, groups, pieces, acts, grads, basis_in, basis_out, queries=None):
     tokens, width = acts.shape[2], acts.shape[3]
     both = 2 * basis_in.shape[1]
-    pieces = len(flips) * CHUNKS
-    operands = (acts, grads, basis_in, basis_out, *sources)
+    steps = sum(len(p) for p in pieces)
+    operands, turned, turn_buf = [acts, grads, basis_in, basis_out], [], []
+    if queries is not None:
+        layers, count, depth = queries.shape
+        operands.append(queries)
+        turned = [jax.ShapeDtypeStruct((layers, depth, count), queries.dtype)]
+        turn_buf = [pltpu.VMEM(queries.shape, queries.dtype)]
     hbm = pl.BlockSpec(memory_space=pltpu.HBM)
     vmem = pl.BlockSpec(memory_space=pltpu.VMEM)
 
     def project_pairs(*refs):
-        project(flips, groups, moves, *refs)
+        project(flips, groups, pieces, queries is not None, *refs)
 
     return pl.pallas_call(
         project_pairs,
-        out_shape=[*targets]
+        out_shape=turned
         + [
             jax.ShapeDtypeStruct((tokens + tokens // g, both), jnp.int16)
             if g
@@ -127,16 +129,16 @@
             for g in groups
         ],
         in_specs=[hbm] * len(operands),
-        out_specs=[vmem] * (len(targets) + len(groups)),
-        scratch_shapes=[
-            pltpu.VMEM((pieces, tokens // CHUNKS, width), acts.dtype),
-            pltpu.VMEM((pieces, tokens // CHUNKS, width), grads.dtype),
+        out_specs=[vmem] * (len(turned) + len(groups)),
+        scratch_shapes=turn_buf
+        + [
+            pltpu.VMEM((len(flips), tokens, width), acts.dtype),
+            pltpu.VMEM((len(flips), tokens, width), grads.dtype),
             pltpu.VMEM(basis_in.shape[1:], basis_in.dtype),
             pltpu.VMEM(basis_out.shape[1:], basis_out.dtype),
             pltpu.VMEM((tokens // 16, both), jnp.float32),
-            pltpu.SemaphoreType.DMA((2, pieces)),
-            pltpu.SemaphoreType.DMA((2,)),
-            pltpu.SemaphoreType.DMA((count,)),
+            pltpu.SemaphoreType.DMA((2, steps)),
+            pltpu.SemaphoreType.DMA((3,)),
         ],
         compiler_params=pltpu.CompilerParams(vmem_limit_bytes=VMEM),
         cost_estimate=pl.CostEstimate(
@@ -147,13 +149,6 @@
     )(*(pltpu.with_memory_space_constraint(x, pltpu.HBM) for x in operands))
 
 
-def blocks_together(fisher, queries, both):
-    for layer in range(fisher.shape[0]):
-        depth, rows = fisher.shape[1], queries.shape[1]
-        yield fisher.at[layer], both.at[layer, pl.ds(0, depth), :]
-        yield queries.at[layer], both.at[layer, pl.ds(depth, rows), :]
-
-
 def decode(ref, tokens):
     shared = ref.shape[0] - tokens
     both = ref.shape[1]
@@ -175,12 +170,13 @@
     count = lengths[example]
     total = most[...] + decode(last, tokens)
     row = lax.broadcasted_iota(jnp.int32, (tokens, both), 0)
-    lane = lax.broadcasted_iota(jnp.int32, (tokens, both), 1)
-    kept = jnp.where(row < count, total, 0.0)
-    weighted = jnp.where(lane < half, kept / count.astype(jnp.float32), kept)
+    lane = lax.broadcasted_iota(jnp.int32, (1, both), 1)
+    weight = jnp.where(lane < half, 1.0 / jnp.full((1, both), count, jnp.int32).astype(jnp.float32), 1.0)
+    weighted = jnp.where(row < count, total * weight, 0.0)
     first = weighted.astype(jnp.bfloat16)
     rest = (weighted - first.astype(jnp.float32)).astype(jnp.bfloat16)
-    product = tn(first, first) + (tn(first, rest) + tn(rest, first))
+    wide = tn(first, jnp.concatenate([first, rest], axis=1))
+    product = wide[:, :both] + (wide[:, both:] + tn(rest, first))
     grad[...] = product[:half, :]
     even = grad[pl.ds(0, half // 2, stride=2), :][:, half:]
     odd = grad[pl.ds(1, half // 2, stride=2), :][:, half:]
@@ -200,50 +196,43 @@
     halves = width // cut
     core = lax.axis_index("core")
     steps = depth // lanes
+    order = [e * 2 + x for x in range(2) for e in range(rows // 2)]
+    every = []
     for layer in range(layers):
         mapped = None
         for block, owner in ((fisher, core), (beside, 1 - core)):
             parts = [
-                jnp.concatenate([grads[layer * rows + s, pl.ds(owner * steps + r, 1), :] for s in range(rows)], axis=0)
+                jnp.concatenate([grads[layer * rows + s, pl.ds(owner * steps + r, 1), :] for s in order], axis=0)
                 for r in range(steps)
             ]
             term = nn(thirds(jnp.concatenate(parts, axis=1)), block[layer, pl.ds(0, depth), :])
             mapped = term if mapped is None else mapped + term
-        mapped = add_thirds(mapped)
-        for x in range(2):
-            for e in range(rows // 2):
-                row = e * 2 + x
-                for h in range(halves):
-                    at = (layer * (rows // 2) + e) * halves + h
-                    piece = mapped[row : row + 1, h * cut : (h + 1) * cut]
-                    for t in range(4):
-                        out[t * 2 + x, pl.ds(at, 1), :] = piece
+        every.append(add_thirds(mapped))
+    for x in range(2):
+        own = jnp.concatenate([mapped[x * rows // 2 : (x + 1) * rows // 2] for mapped in every], axis=0)
+        mapped = jnp.concatenate([own[:, h * cut : (h + 1) * cut] for h in range(halves)], axis=0)
+        for t in range(4):
+            out[t * 2 + x] = mapped
 
 
 def with_queries(mapped, own, beside, across, corner, out):
-    layers, cut = own.shape[0], mapped.shape[2]
-    halves = own.shape[2] // cut
-    count = out.shape[1]
-    examples = mapped.shape[1] // (layers * halves)
+    layers, depth, count = own.shape
+    halves = depth // mapped.shape[2]
+    rows = mapped.shape[1] // halves
     here = lax.axis_index("x") * 2 + lax.axis_index("core")
-    sums = [None] * (layers * halves)
+    sums = [None] * layers
     for k, block in enumerate((own, beside, across, corner)):
-        left = thirds(mapped[(here ^ k) * 2] + mapped[(here ^ k) * 2 + 1])
-        rows = pl.ds(block.shape[1] - count, count)
+        both = mapped[(here ^ k) * 2] + mapped[(here ^ k) * 2 + 1]
+        left = thirds(jnp.concatenate([both[h * rows : (h + 1) * rows] for h in range(halves)], axis=1))
         for layer in range(layers):
-            for h in range(halves):
-                term = nt(left, block[layer, rows, h * cut : (h + 1) * cut])
-                at = layer * halves + h
-                sums[at] = term if sums[at] is None else sums[at] + term
-    result = [None] * examples
+            term = nn(left, block[layer])
+            sums[layer] = term if sums[layer] is None else sums[layer] + term
+    examples = rows // layers
+    result = None
     for layer in range(layers):
-        for h in range(halves):
-            scores = add_thirds(sums[layer * halves + h])
-            for e in range(examples):
-                row = (layer * examples + e) * halves + h
-                term = scores[row : row + 1]
-                result[e] = term if result[e] is None else result[e] + term
-    out[...] = jnp.concatenate(result, axis=0)
+        scores = add_thirds(sums[layer])[layer * examples : (layer + 1) * examples]
+        result = scores if result is None else result + scores
+    out[...] = result
 
 
 def swap(x, axis, flip):
@@ -260,13 +249,12 @@
     proj_width = basis_in.shape[2]
     operands = (acts_in, grads_out, jnp.swapaxes(basis_in, 1, 2), jnp.swapaxes(basis_out, 1, 2))
 
-    far, middle = projector((3, 2), (16, 16), *operands)
-    acts_in, grads_out, fisher_inv, queries, far, middle = lax.optimization_barrier(
-        (acts_in, grads_out, fisher_inv, queries, far, middle)
-    )
+    queries, far, middle = projector((3, 2), (32, 32), PIECES_TWO, *operands, queries)
+    acts_in, grads_out, queries, far, middle = lax.optimization_barrier((acts_in, grads_out, queries, far, middle))
     far, middle = swap(far, "tensor", 3), swap(middle, "tensor", 2)
     across = swap(queries, "x", 1)
-    near, here = projector((1, 0), (32, 0), acts_in, grads_out, *operands[2:])
+    (near,) = projector((1,), (32,), PIECES_ONE, acts_in, grads_out, *operands[2:])
+    (here,) = projector((0,), (0,), PIECES_ONE, acts_in, grads_out, *operands[2:])
     near = swap(near, "tensor", 1)
     fisher_beside = swap(fisher_inv, "core", 1)
 
@@ -303,7 +291,7 @@
 
     return pl.pallas_call(
         with_queries,
-        out_shape=jax.ShapeDtypeStruct((acts_in.shape[1], queries.shape[1]), jnp.float32),
+        out_shape=jax.ShapeDtypeStruct((acts_in.shape[1], queries.shape[2]), jnp.float32),
         in_specs=[vmem] * 5,
         out_specs=vmem,
         compiler_params=params,

time: 51.9 us -> 49.8 us (0.960)
  waiting for transfers between devices: 7.48 us -> 3.69 us
  blocking collectives: 20.2 us -> 21.1 us
  Pallas kernels: 15.8 us -> 16.6 us
    ppermute x7, waiting for transfers between devices: 7.48 us -> 3.69 us  [swap(): lax.ppermute(x, axis, [(i, i ^ flip) for i in range(lax.axis_size(axis))])]
    pallas_call x2 -> x3, Pallas kernels: 11.6 us -> 13.1 us  [projector(): pl.pallas_call(project_pairs, out_shape=turned + [jax.ShapeDtypeStruct((t...]
    all_to_all x1, blocking collectives: 9.89 us -> 10.8 us  [small(): mapped = lax.all_to_all(mapped, ('tensor', 'x'), 0, 0, tiled=True)]
    pallas_call x1, Pallas kernels: 1.92 us -> 1.24 us  [small(): pl.pallas_call(with_queries, out_shape=jax.ShapeDtypeStruct((acts_in.shap...]
  transfers between devices with their start and end apart: 7 -> 7, of which waited for: 2 -> 1; matrix products, arithmetic and copies ran while one was open for 0% -> 0% of each run, Pallas kernels for 15% -> 31%
where the time goes in v3:
time: 49.8 us; the launch traced here: 49.6 us
  blocking collectives  21.1 us (42%)
  Pallas kernels  16.6 us (33%)
  starting transfers between devices  8.02 us (16%)
  waiting for transfers between devices  3.69 us (7%)
    pallas_call x3, Pallas kernels, projector(): pl.pallas_call(project_pairs, out_shape=turned + [jax.ShapeDtypeStruct((t...  13.1 us
    all_to_all x1, blocking collectives, small(): mapped = lax.all_to_all(mapped, ('tensor', 'x'), 0, 0, tiled=True)  10.8 us
    all_to_all x1, blocking collectives, small(): blocks = lax.all_to_all(blocks, ('tensor', 'x'), 0, 0, tiled=True)  10.3 us
    ppermute x7, starting transfers between devices, swap(): lax.ppermute(x, axis, [(i, i ^ flip) for i in range(lax.axis_size(axis))])  8.02 us
    ppermute x7, waiting for transfers between devices, swap(): lax.ppermute(x, axis, [(i, i ^ flip) for i in range(lax.axis_size(axis))])  3.69 us
    pallas_call x1, Pallas kernels, small(): pl.pallas_call(with_queries, out_shape=jax.ShapeDtypeStruct((acts_in.shap...  1.24 us
    pallas_call x1, Pallas kernels, small(): pl.pallas_call(through_fisher, out_shape=jax.ShapeDtypeStruct((8, 8, fish...  1.22 us
  transfers between devices with their start and end apart: 7, of which 1 were waited for; matrix products, arithmetic and copies ran while one was open for 0% of the time, Pallas kernels for 31%

profile of v3, /device:TPU:0, one launch (start us, length us, event | category | flops | bytes accessed | tf_op | source)
XLA Modules:
  0.0 49.6 jit_solution(2924455318443726696)
XLA Ops:
  0.0 0.5 collective-permute-start.4
  0.5 5.8 %shard_map.73 = (bf16[2,1024,256]{2,1,0:T(8,128)(2,1)S(1)}, s16[528,128]{1,0:T(8,128)(2,1)S(1)}, s16[528,128]{1,0:T(8,128)(2,1)S(1)}) custom-call(bf16[2,2,512,2048]{3,2,1,0:T(8,128)(2,1)} %refs_0_.3, bf16[2,2,512,2048]{3,2,1,0:T(8,128)(2,1)} %refs_1_.3, bf16[2,64,2048]{2,1,0:T(8,128)(2,1)} %bitcast.2, bf16[2,64,2048]{2,1,0:T(8,128)(2,1)} %bitcast.5, ...), custom_call_target="tpu_custom_call" | custom-call | flops 536870912 | bytes 8388608 | tf_op jit(solution)/shard_map/pallas_call | solution.py:122
  6.2 2.5 %collective-permute-start = (bf16[2,1024,256]{2,1,0:T(8,128)(2,1)S(1)}, bf16[2,1024,256]{2,1,0:T(8,128)(2,1)S(1)}, u32[]{:S(2)}, u32[]{:S(2)}) collective-permute-start(bf16[2,1024,256]{2,1,0:T(8,128)(2,1)S(1)} %get-tuple-element.29.own), channel_id=1, source_target_pairs={{0,2},{2,0},{1,3},{3,1},{4,6},{6,4},{5,7},{7,5},{8,10},{10,8},{9,1... | collective-permute-start | bytes 3145736 | tf_op jit(solution)/shard_map/ppermute | solution.py:239
  8.8 3.6 %collective-permute-start.1 = (s16[528,128]{1,0:T(8,128)(2,1)S(1)}, s16[528,128]{1,0:T(8,128)(2,1)S(1)}, u32[]{:S(2)}, u32[]{:S(2)}) collective-permute-start(s16[528,128]{1,0:T(8,128)(2,1)S(1)} %get-tuple-element.24), channel_id=1, source_target_pairs={{0,12},{4,8},{8,4},{12,0},{1,13},{5,9},{9,5},{13,1},{2,14},{6,10},... | collective-permute-start | bytes 405512 | tf_op jit(solution)/shard_map/ppermute | solution.py:239
  12.4 0.0 collective-permute-start.2
  12.4 3.5 %shard_map.76 = s16[528,128]{1,0:T(8,128)(2,1)S(1)} custom-call(bf16[2,2,512,2048]{3,2,1,0:T(8,128)(2,1)} %refs_0_.3, bf16[2,2,512,2048]{3,2,1,0:T(8,128)(2,1)} %refs_1_.3, bf16[2,64,2048]{2,1,0:T(8,128)(2,1)} %bitcast.3, bf16[2,64,2048]{2,1,0:T(8,128)(2,1)} %bitcast.6), custom_call_target="tpu_custom_call" | custom-call | flops 268435456 | bytes 4194304 | tf_op jit(solution)/shard_map/pallas_call | solution.py:122
  15.9 0.0 copy-start.1
  15.9 0.0 copy-start
  15.9 0.8 %collective-permute-start.3 = (s16[528,128]{1,0:T(8,128)(2,1)S(1)}, s16[528,128]{1,0:T(8,128)(2,1)S(1)}, u32[]{:S(2)}, u32[]{:S(2)}) collective-permute-start(s16[528,128]{1,0:T(8,128)(2,1)S(1)} %shard_map.76), channel_id=1, source_target_pairs={{0,4},{4,0},{8,12},{12,8},{1,5},{5,1},{9,13},{13,9},{2,6},{6,2},{1... | collective-permute-start | bytes 405512 | tf_op jit(solution)/shard_map/ppermute | solution.py:239
  16.8 3.9 %shard_map.74.own = f32[512,128]{1,0:T(8,128)S(1)} custom-call(bf16[2,2,512,2048]{3,2,1,0:T(8,128)(2,1)} %refs_0_.3, bf16[2,2,512,2048]{3,2,1,0:T(8,128)(2,1)} %refs_1_.3, bf16[2,64,2048]{2,1,0:T(8,128)(2,1)} %bitcast.4, bf16[2,64,2048]{2,1,0:T(8,128)(2,1)} %bitcast.7), custom_call_target="tpu_custom_call" | custom-call | flops 268435456 | bytes 4194304 | tf_op jit(solution)/shard_map/pallas_call | solution.py:122
  20.6 0.0 collective-permute-done.1.first
  20.6 3.7 %collective-permute-done.2.second = s16[528,128]{1,0:T(8,128)(2,1)S(1)} collective-permute-done((s16[528,128]{1,0:T(8,128)(2,1)S(1)}, s16[528,128]{1,0:T(8,128)(2,1)S(1)}, u32[]{:S(2)}, u32[]{:S(2)}) %collective-permute-start.2) | collective-permute-done | bytes 135200 | tf_op jit(solution)/shard_map/ppermute | solution.py:239
  24.3 0.1 shard_map.75.most
  24.4 0.0 collective-permute-done.3.last
  24.4 0.9 %shard_map.77 = f32[8,16,128]{2,1,0:T(8,128)S(1)} custom-call(s32[2]{0:T(128)S(1)} %copy-done.1, f32[512,128]{1,0:T(8,128)S(1)} %shard_map.75.most, s16[528,128]{1,0:T(8,128)(2,1)S(1)} %collective-permute-done.3.last), custom_call_target="tpu_custom_call" | custom-call | tf_op jit(solution)/shard_map/pallas_call | solution.py:270
  25.4 0.0 collective-permute-done.4.beside
  25.4 10.3 %all_to_all.10.grads = f32[8,16,128]{2,1,0:T(8,128)S(1)} all-to-all(f32[8,16,128]{2,1,0:T(8,128)S(1)} %shard_map.77), channel_id=1, replica_groups=mesh['parts'=2,'tensor'=4,'x'=2,'core'=2] {'tensor','x'}, dimensions={0} | all-to-all | bytes 131072 | tf_op jit(solution)/shard_map/all_to_all | solution.py:279
  35.7 1.2 %shard_map.78 = f32[8,8,512]{2,1,0:T(8,128)S(1)} custom-call(f32[8,16,128]{2,1,0:T(8,128)S(1)} %all_to_all.10.grads, bf16[2,1024,1024]{2,1,0:T(8,128)(2,1)S(1)} %copy-done, bf16[2,1024,1024]{2,1,0:T(8,128)(2,1)S(1)} %collective-permute-done.4.beside), custom_call_target="tpu_custom_call" | custom-call | tf_op jit(solution)/shard_map/pallas_call | solution.py:281
  37.0 0.0 collective-permute-done.across
  37.0 0.1 collective-permute-start.5
  37.0 0.5 %collective-permute-start.6 = (bf16[2,1024,256]{2,1,0:T(8,128)(2,1)S(1)}, bf16[2,1024,256]{2,1,0:T(8,128)(2,1)S(1)}, u32[]{:S(2)}, u32[]{:S(2)}) collective-permute-start(bf16[2,1024,256]{2,1,0:T(8,128)(2,1)S(1)} %collective-permute-done.across), channel_id=1, source_target_pairs={{0,1},{1,0},{2,3},{3,2},{4,5},{5,4},{6,7},{7,6},{8,9},{9,8},{10,11... | collective-permute-start | bytes 3145736 | tf_op jit(solution)/shard_map/ppermute | solution.py:239
  37.5 10.8 %all_to_all.11.mapped = f32[8,8,512]{2,1,0:T(8,128)S(1)} all-to-all(f32[8,8,512]{2,1,0:T(8,128)S(1)} %shard_map.78), channel_id=1, replica_groups=mesh['parts'=2,'tensor'=4,'x'=2,'core'=2] {'tensor','x'}, dimensions={0} | all-to-all | bytes 262144 | tf_op jit(solution)/shard_map/all_to_all | solution.py:290
  48.3 0.0 collective-permute-done.5.beside
  48.3 1.2 %shard_map.79 = f32[2,256]{1,0:T(2,128)} custom-call(f32[8,8,512]{2,1,0:T(8,128)S(1)} %all_to_all.11.mapped, bf16[2,1024,256]{2,1,0:T(8,128)(2,1)S(1)} %get-tuple-element.29.own, bf16[2,1024,256]{2,1,0:T(8,128)(2,1)S(1)} %collective-permute-done.5.beside, bf16[2,1024,256]{2,1,0:T(8,128)(2,1)S(1)} %collective-permute-done.across, ...), custom_call_target="tpu_custom_call" | custom-call | tf_op jit(solution)/shard_map/pallas_call | solution.py:292
  (3 shorter events, 0.0 us)
Async XLA Ops:
  0.0 25.4 %collective-permute-start.4 = (bf16[2,1024,1024]{2,1,0:T(8,128)(2,1)}, bf16[2,1024,1024]{2,1,0:T(8,128)(2,1)S(1)}, u32[]{:S(2)}, u32[]{:S(2)}) collective-permute-start(bf16[2,1024,1024]{2,1,0:T(8,128)(2,1)} %fisher.1), channel_id=1, source_target_pairs={{0,1},{1,0},{2,3},{3,2},{4,5},{5,4},{6,7},{7,6},{8,9},{9,8},{10,11... | collective-permute-start | bytes 12582920 | tf_op jit(solution)/shard_map/ppermute | solution.py:239
  6.2 30.7 %collective-permute-start = (bf16[2,1024,256]{2,1,0:T(8,128)(2,1)S(1)}, bf16[2,1024,256]{2,1,0:T(8,128)(2,1)S(1)}, u32[]{:S(2)}, u32[]{:S(2)}) collective-permute-start(bf16[2,1024,256]{2,1,0:T(8,128)(2,1)S(1)} %get-tuple-element.29.own), channel_id=1, source_target_pairs={{0,2},{2,0},{1,3},{3,1},{4,6},{6,4},{5,7},{7,5},{8,10},{10,8},{9,1... | collective-permute-start | bytes 3145736 | tf_op jit(solution)/shard_map/ppermute | solution.py:239
  8.8 11.8 %collective-permute-start.1 = (s16[528,128]{1,0:T(8,128)(2,1)S(1)}, s16[528,128]{1,0:T(8,128)(2,1)S(1)}, u32[]{:S(2)}, u32[]{:S(2)}) collective-permute-start(s16[528,128]{1,0:T(8,128)(2,1)S(1)} %get-tuple-element.24), channel_id=1, source_target_pairs={{0,12},{4,8},{8,4},{12,0},{1,13},{5,9},{9,5},{13,1},{2,14},{6,10},... | collective-permute-start | bytes 405512 | tf_op jit(solution)/shard_map/ppermute | solution.py:239
  12.4 11.9 %collective-permute-start.2 = (s16[528,128]{1,0:T(8,128)(2,1)S(1)}, s16[528,128]{1,0:T(8,128)(2,1)S(1)}, u32[]{:S(2)}, u32[]{:S(2)}) collective-permute-start(s16[528,128]{1,0:T(8,128)(2,1)S(1)} %get-tuple-element.25), channel_id=1, source_target_pairs={{0,8},{4,12},{8,0},{12,4},{1,9},{5,13},{9,1},{13,5},{2,10},{6,14},... | collective-permute-start | bytes 405512 | tf_op jit(solution)/shard_map/ppermute | solution.py:239
  15.9 8.5 %copy-start.1 = (s32[2]{0:T(128)S(1)}, s32[2]{0:T(128)}, u32[]{:S(2)}) copy-start(s32[2]{0:T(128)} %lengths.1) | copy-start | bytes 28
  15.9 19.8 %copy-start = (bf16[2,1024,1024]{2,1,0:T(8,128)(2,1)S(1)}, bf16[2,1024,1024]{2,1,0:T(8,128)(2,1)}, u32[]{:S(2)}) copy-start(bf16[2,1024,1024]{2,1,0:T(8,128)(2,1)} %fisher.1) | copy-start | bytes 12582916
  15.9 8.5 %collective-permute-start.3 = (s16[528,128]{1,0:T(8,128)(2,1)S(1)}, s16[528,128]{1,0:T(8,128)(2,1)S(1)}, u32[]{:S(2)}, u32[]{:S(2)}) collective-permute-start(s16[528,128]{1,0:T(8,128)(2,1)S(1)} %shard_map.76), channel_id=1, source_target_pairs={{0,4},{4,0},{8,12},{12,8},{1,5},{5,1},{9,13},{13,9},{2,6},{6,2},{1... | collective-permute-start | bytes 405512 | tf_op jit(solution)/shard_map/ppermute | solution.py:239
  37.0 11.4 %collective-permute-start.5 = (bf16[2,1024,256]{2,1,0:T(8,128)(2,1)S(1)}, bf16[2,1024,256]{2,1,0:T(8,128)(2,1)S(1)}, u32[]{:S(2)}, u32[]{:S(2)}) collective-permute-start(bf16[2,1024,256]{2,1,0:T(8,128)(2,1)S(1)} %get-tuple-element.29.own), channel_id=1, source_target_pairs={{0,1},{1,0},{2,3},{3,2},{4,5},{5,4},{6,7},{7,6},{8,9},{9,8},{10,11... | collective-permute-start | bytes 3145736 | tf_op jit(solution)/shard_map/ppermute | solution.py:239
  37.0 11.3 %collective-permute-start.6 = (bf16[2,1024,256]{2,1,0:T(8,128)(2,1)S(1)}, bf16[2,1024,256]{2,1,0:T(8,128)(2,1)S(1)}, u32[]{:S(2)}, u32[]{:S(2)}) collective-permute-start(bf16[2,1024,256]{2,1,0:T(8,128)(2,1)S(1)} %collective-permute-done.across), channel_id=1, source_target_pairs={{0,1},{1,0},{2,3},{3,2},{4,5},{5,4},{6,7},{7,6},{8,9},{9,8},{10,11... | collective-permute-start | bytes 3145736 | tf_op jit(solution)/shard_map/ppermute | solution.py:239

commit v4 on v3

--- a/solution.py
+++ b/solution.py
@@ -225,7 +225,7 @@
         both = mapped[(here ^ k) * 2] + mapped[(here ^ k) * 2 + 1]
         left = thirds(jnp.concatenate([both[h * rows : (h + 1) * rows] for h in range(halves)], axis=1))
         for layer in range(layers):
-            term = nn(left, block[layer])
+            term = nn(left, block[layer]) if k < 2 else nt(left, block[layer])
             sums[layer] = term if sums[layer] is None else sums[layer] + term
     examples = rows // layers
     result = None
@@ -249,10 +249,10 @@
     proj_width = basis_in.shape[2]
     operands = (acts_in, grads_out, jnp.swapaxes(basis_in, 1, 2), jnp.swapaxes(basis_out, 1, 2))
 
+    across = swap(queries, "x", 1)
     queries, far, middle = projector((3, 2), (32, 32), PIECES_TWO, *operands, queries)
-    acts_in, grads_out, queries, far, middle = lax.optimization_barrier((acts_in, grads_out, queries, far, middle))
+    acts_in, grads_out, far, middle = lax.optimization_barrier((acts_in, grads_out, far, middle))
     far, middle = swap(far, "tensor", 3), swap(middle, "tensor", 2)
-    across = swap(queries, "x", 1)
     (near,) = projector((1,), (32,), PIECES_ONE, acts_in, grads_out, *operands[2:])
     (here,) = projector((0,), (0,), PIECES_ONE, acts_in, grads_out, *operands[2:])
     near = swap(near, "tensor", 1)

time: 49.8 us -> 49.2 us (0.988)
  blocking collectives: 21.1 us -> 20.2 us
    all_to_all x1, blocking collectives: 10.8 us -> 9.89 us  [small(): mapped = lax.all_to_all(mapped, ('tensor', 'x'), 0, 0, tiled=True)]
where the time goes in v4:
time: 49.2 us; the launch traced here: 49 us
  blocking collectives  20.2 us (41%)
  Pallas kernels  16.9 us (34%)
  starting transfers between devices  8.02 us (16%)
  waiting for transfers between devices  3.7 us (8%)
    pallas_call x3, Pallas kernels, projector(): pl.pallas_call(project_pairs, out_shape=turned + [jax.ShapeDtypeStruct((t...  13.1 us
    all_to_all x1, blocking collectives, small(): blocks = lax.all_to_all(blocks, ('tensor', 'x'), 0, 0, tiled=True)  10.3 us
    all_to_all x1, blocking collectives, small(): mapped = lax.all_to_all(mapped, ('tensor', 'x'), 0, 0, tiled=True)  9.89 us
    ppermute x7, starting transfers between devices, swap(): lax.ppermute(x, axis, [(i, i ^ flip) for i in range(lax.axis_size(axis))])  8.02 us
    ppermute x7, waiting for transfers between devices, swap(): lax.ppermute(x, axis, [(i, i ^ flip) for i in range(lax.axis_size(axis))])  3.7 us
    pallas_call x1, Pallas kernels, small(): pl.pallas_call(with_queries, out_shape=jax.ShapeDtypeStruct((acts_in.shap...  1.51 us
    pallas_call x1, Pallas kernels, small(): pl.pallas_call(through_fisher, out_shape=jax.ShapeDtypeStruct((8, 8, fish...  1.22 us
  transfers between devices with their start and end apart: 7, of which 1 were waited for; matrix products, arithmetic and copies ran while one was open for 0% of the time, Pallas kernels for 31%

profile of v4, /device:TPU:0, one launch (start us, length us, event | category | flops | bytes accessed | tf_op | source)
XLA Modules:
  0.0 49.0 jit_solution(9512529119707865555)
XLA Ops:
  0.0 0.5 collective-permute-start.4
  0.5 2.5 %collective-permute-start = (bf16[2,256,1024]{2,1,0:T(8,128)(2,1)}, bf16[2,256,1024]{2,1,0:T(8,128)(2,1)S(1)}, u32[]{:S(2)}, u32[]{:S(2)}) collective-permute-start(bf16[2,256,1024]{2,1,0:T(8,128)(2,1)} %refs_4_.1), channel_id=1, source_target_pairs={{0,2},{2,0},{1,3},{3,1},{4,6},{6,4},{5,7},{7,5},{8,10},{10,8},{9,1... | collective-permute-start | bytes 3145736 | tf_op jit(solution)/shard_map/ppermute | solution.py:239
  2.9 5.8 %shard_map.73 = (bf16[2,1024,256]{2,1,0:T(8,128)(2,1)S(1)}, s16[528,128]{1,0:T(8,128)(2,1)S(1)}, s16[528,128]{1,0:T(8,128)(2,1)S(1)}) custom-call(bf16[2,2,512,2048]{3,2,1,0:T(8,128)(2,1)} %refs_0_.3, bf16[2,2,512,2048]{3,2,1,0:T(8,128)(2,1)} %refs_1_.3, bf16[2,64,2048]{2,1,0:T(8,128)(2,1)} %bitcast.2, bf16[2,64,2048]{2,1,0:T(8,128)(2,1)} %bitcast.5, ...), custom_call_target="tpu_custom_call" | custom-call | flops 536870912 | bytes 8388608 | tf_op jit(solution)/shard_map/pallas_call | solution.py:122
  8.7 3.7 %collective-permute-start.1 = (s16[528,128]{1,0:T(8,128)(2,1)S(1)}, s16[528,128]{1,0:T(8,128)(2,1)S(1)}, u32[]{:S(2)}, u32[]{:S(2)}) collective-permute-start(s16[528,128]{1,0:T(8,128)(2,1)S(1)} %get-tuple-element.22), channel_id=1, source_target_pairs={{0,12},{4,8},{8,4},{12,0},{1,13},{5,9},{9,5},{13,1},{2,14},{6,10},... | collective-permute-start | bytes 405512 | tf_op jit(solution)/shard_map/ppermute | solution.py:239
  12.4 0.0 collective-permute-start.2
  12.4 3.5 %shard_map.76 = s16[528,128]{1,0:T(8,128)(2,1)S(1)} custom-call(bf16[2,2,512,2048]{3,2,1,0:T(8,128)(2,1)} %refs_0_.3, bf16[2,2,512,2048]{3,2,1,0:T(8,128)(2,1)} %refs_1_.3, bf16[2,64,2048]{2,1,0:T(8,128)(2,1)} %bitcast.3, bf16[2,64,2048]{2,1,0:T(8,128)(2,1)} %bitcast.6), custom_call_target="tpu_custom_call" | custom-call | flops 268435456 | bytes 4194304 | tf_op jit(solution)/shard_map/pallas_call | solution.py:122
  15.9 0.0 copy-start.1
  15.9 0.0 copy-start
  15.9 0.8 %collective-permute-start.3 = (s16[528,128]{1,0:T(8,128)(2,1)S(1)}, s16[528,128]{1,0:T(8,128)(2,1)S(1)}, u32[]{:S(2)}, u32[]{:S(2)}) collective-permute-start(s16[528,128]{1,0:T(8,128)(2,1)S(1)} %shard_map.76), channel_id=1, source_target_pairs={{0,4},{4,0},{8,12},{12,8},{1,5},{5,1},{9,13},{13,9},{2,6},{6,2},{1... | collective-permute-start | bytes 405512 | tf_op jit(solution)/shard_map/ppermute | solution.py:239
  16.8 3.9 %shard_map.74.own = f32[512,128]{1,0:T(8,128)S(1)} custom-call(bf16[2,2,512,2048]{3,2,1,0:T(8,128)(2,1)} %refs_0_.3, bf16[2,2,512,2048]{3,2,1,0:T(8,128)(2,1)} %refs_1_.3, bf16[2,64,2048]{2,1,0:T(8,128)(2,1)} %bitcast.4, bf16[2,64,2048]{2,1,0:T(8,128)(2,1)} %bitcast.7), custom_call_target="tpu_custom_call" | custom-call | flops 268435456 | bytes 4194304 | tf_op jit(solution)/shard_map/pallas_call | solution.py:122
  20.6 0.0 collective-permute-done.1.first
  20.6 3.7 %collective-permute-done.2.second = s16[528,128]{1,0:T(8,128)(2,1)S(1)} collective-permute-done((s16[528,128]{1,0:T(8,128)(2,1)S(1)}, s16[528,128]{1,0:T(8,128)(2,1)S(1)}, u32[]{:S(2)}, u32[]{:S(2)}) %collective-permute-start.2) | collective-permute-done | bytes 135200 | tf_op jit(solution)/shard_map/ppermute | solution.py:239
  24.3 0.1 shard_map.75.most
  24.4 0.0 collective-permute-done.3.last
  24.4 0.9 %shard_map.77 = f32[8,16,128]{2,1,0:T(8,128)S(1)} custom-call(s32[2]{0:T(128)S(1)} %copy-done.1, f32[512,128]{1,0:T(8,128)S(1)} %shard_map.75.most, s16[528,128]{1,0:T(8,128)(2,1)S(1)} %collective-permute-done.3.last), custom_call_target="tpu_custom_call" | custom-call | tf_op jit(solution)/shard_map/pallas_call | solution.py:270
  25.4 0.0 collective-permute-done.4.beside
  25.4 10.3 %all_to_all.10.grads = f32[8,16,128]{2,1,0:T(8,128)S(1)} all-to-all(f32[8,16,128]{2,1,0:T(8,128)S(1)} %shard_map.77), channel_id=1, replica_groups=mesh['parts'=2,'tensor'=4,'x'=2,'core'=2] {'tensor','x'}, dimensions={0} | all-to-all | bytes 131072 | tf_op jit(solution)/shard_map/all_to_all | solution.py:279
  35.7 1.2 %shard_map.78 = f32[8,8,512]{2,1,0:T(8,128)S(1)} custom-call(f32[8,16,128]{2,1,0:T(8,128)S(1)} %all_to_all.10.grads, bf16[2,1024,1024]{2,1,0:T(8,128)(2,1)S(1)} %copy-done, bf16[2,1024,1024]{2,1,0:T(8,128)(2,1)S(1)} %collective-permute-done.4.beside), custom_call_target="tpu_custom_call" | custom-call | tf_op jit(solution)/shard_map/pallas_call | solution.py:281
  37.0 0.0 collective-permute-done.across
  37.0 0.1 collective-permute-start.5
  37.1 0.5 %collective-permute-start.6 = (bf16[2,256,1024]{2,1,0:T(8,128)(2,1)S(1)}, bf16[2,256,1024]{2,1,0:T(8,128)(2,1)S(1)}, u32[]{:S(2)}, u32[]{:S(2)}) collective-permute-start(bf16[2,256,1024]{2,1,0:T(8,128)(2,1)S(1)} %collective-permute-done.across), channel_id=1, source_target_pairs={{0,1},{1,0},{2,3},{3,2},{4,5},{5,4},{6,7},{7,6},{8,9},{9,8},{10,11... | collective-permute-start | bytes 3145736 | tf_op jit(solution)/shard_map/ppermute | solution.py:239
  37.6 9.9 %all_to_all.11.mapped = f32[8,8,512]{2,1,0:T(8,128)S(1)} all-to-all(f32[8,8,512]{2,1,0:T(8,128)S(1)} %shard_map.78), channel_id=1, replica_groups=mesh['parts'=2,'tensor'=4,'x'=2,'core'=2] {'tensor','x'}, dimensions={0} | all-to-all | bytes 262144 | tf_op jit(solution)/shard_map/all_to_all | solution.py:290
  47.4 0.0 collective-permute-done.6.corner
  47.4 1.5 %shard_map.79 = f32[2,256]{1,0:T(2,128)} custom-call(f32[8,8,512]{2,1,0:T(8,128)S(1)} %all_to_all.11.mapped, bf16[2,1024,256]{2,1,0:T(8,128)(2,1)S(1)} %get-tuple-element.27.own, bf16[2,1024,256]{2,1,0:T(8,128)(2,1)S(1)} %collective-permute-done.5.beside, bf16[2,256,1024]{2,1,0:T(8,128)(2,1)S(1)} %collective-permute-done.across, ...), custom_call_target="tpu_custom_call" | custom-call | tf_op jit(solution)/shard_map/pallas_call | solution.py:292
  (3 shorter events, 0.0 us)
Async XLA Ops:
  0.0 25.4 %collective-permute-start.4 = (bf16[2,1024,1024]{2,1,0:T(8,128)(2,1)}, bf16[2,1024,1024]{2,1,0:T(8,128)(2,1)S(1)}, u32[]{:S(2)}, u32[]{:S(2)}) collective-permute-start(bf16[2,1024,1024]{2,1,0:T(8,128)(2,1)} %fisher.1), channel_id=1, source_target_pairs={{0,1},{1,0},{2,3},{3,2},{4,5},{5,4},{6,7},{7,6},{8,9},{9,8},{10,11... | collective-permute-start | bytes 12582920 | tf_op jit(solution)/shard_map/ppermute | solution.py:239
  0.5 36.5 %collective-permute-start = (bf16[2,256,1024]{2,1,0:T(8,128)(2,1)}, bf16[2,256,1024]{2,1,0:T(8,128)(2,1)S(1)}, u32[]{:S(2)}, u32[]{:S(2)}) collective-permute-start(bf16[2,256,1024]{2,1,0:T(8,128)(2,1)} %refs_4_.1), channel_id=1, source_target_pairs={{0,2},{2,0},{1,3},{3,1},{4,6},{6,4},{5,7},{7,5},{8,10},{10,8},{9,1... | collective-permute-start | bytes 3145736 | tf_op jit(solution)/shard_map/ppermute | solution.py:239
  8.7 11.9 %collective-permute-start.1 = (s16[528,128]{1,0:T(8,128)(2,1)S(1)}, s16[528,128]{1,0:T(8,128)(2,1)S(1)}, u32[]{:S(2)}, u32[]{:S(2)}) collective-permute-start(s16[528,128]{1,0:T(8,128)(2,1)S(1)} %get-tuple-element.22), channel_id=1, source_target_pairs={{0,12},{4,8},{8,4},{12,0},{1,13},{5,9},{9,5},{13,1},{2,14},{6,10},... | collective-permute-start | bytes 405512 | tf_op jit(solution)/shard_map/ppermute | solution.py:239
  12.4 11.9 %collective-permute-start.2 = (s16[528,128]{1,0:T(8,128)(2,1)S(1)}, s16[528,128]{1,0:T(8,128)(2,1)S(1)}, u32[]{:S(2)}, u32[]{:S(2)}) collective-permute-start(s16[528,128]{1,0:T(8,128)(2,1)S(1)} %get-tuple-element.23), channel_id=1, source_target_pairs={{0,8},{4,12},{8,0},{12,4},{1,9},{5,13},{9,1},{13,5},{2,10},{6,14},... | collective-permute-start | bytes 405512 | tf_op jit(solution)/shard_map/ppermute | solution.py:239
  15.9 8.5 %copy-start.1 = (s32[2]{0:T(128)S(1)}, s32[2]{0:T(128)}, u32[]{:S(2)}) copy-start(s32[2]{0:T(128)} %lengths.1) | copy-start | bytes 28
  15.9 19.8 %copy-start = (bf16[2,1024,1024]{2,1,0:T(8,128)(2,1)S(1)}, bf16[2,1024,1024]{2,1,0:T(8,128)(2,1)}, u32[]{:S(2)}) copy-start(bf16[2,1024,1024]{2,1,0:T(8,128)(2,1)} %fisher.1) | copy-start | bytes 12582916
  15.9 8.5 %collective-permute-start.3 = (s16[528,128]{1,0:T(8,128)(2,1)S(1)}, s16[528,128]{1,0:T(8,128)(2,1)S(1)}, u32[]{:S(2)}, u32[]{:S(2)}) collective-permute-start(s16[528,128]{1,0:T(8,128)(2,1)S(1)} %shard_map.76), channel_id=1, source_target_pairs={{0,4},{4,0},{8,12},{12,8},{1,5},{5,1},{9,13},{13,9},{2,6},{6,2},{1... | collective-permute-start | bytes 405512 | tf_op jit(solution)/shard_map/ppermute | solution.py:239
  37.0 10.5 %collective-permute-start.5 = (bf16[2,1024,256]{2,1,0:T(8,128)(2,1)S(1)}, bf16[2,1024,256]{2,1,0:T(8,128)(2,1)S(1)}, u32[]{:S(2)}, u32[]{:S(2)}) collective-permute-start(bf16[2,1024,256]{2,1,0:T(8,128)(2,1)S(1)} %get-tuple-element.27.own), channel_id=1, source_target_pairs={{0,1},{1,0},{2,3},{3,2},{4,5},{5,4},{6,7},{7,6},{8,9},{9,8},{10,11... | collective-permute-start | bytes 3145736 | tf_op jit(solution)/shard_map/ppermute | solution.py:239
  37.1 10.4 %collective-permute-start.6 = (bf16[2,256,1024]{2,1,0:T(8,128)(2,1)S(1)}, bf16[2,256,1024]{2,1,0:T(8,128)(2,1)S(1)}, u32[]{:S(2)}, u32[]{:S(2)}) collective-permute-start(bf16[2,256,1024]{2,1,0:T(8,128)(2,1)S(1)} %collective-permute-done.across), channel_id=1, source_target_pairs={{0,1},{1,0},{2,3},{3,2},{4,5},{5,4},{6,7},{7,6},{8,9},{9,8},{10,11... | collective-permute-start | bytes 3145736 | tf_op jit(solution)/shard_map/ppermute | solution.py:239

commit v5 on v4

--- a/solution.py
+++ b/solution.py
@@ -39,10 +39,10 @@
 
 def project(flips, groups, pieces, turn, acts, grads, basis_in, basis_out, *refs):
     *refs, a_buf, g_buf, in_buf, out_buf, scale_log, sems, basis_sems = refs
-    queries = turned = turn_buf = None
+    queries = beside = turned = turned_beside = turn_buf = None
     if turn:
         *refs, turn_buf = refs
-        queries, turned, *refs = refs
+        queries, beside, turned, turned_beside, *refs = refs
     outs = refs
     examples, tokens = acts.shape[1], acts.shape[2]
     here = lax.axis_index("tensor")
@@ -75,8 +75,9 @@
     for copy in first:
         copy.wait()
     if turn:
-        for q in range(turned.shape[0]):
-            turned[q] = turn_buf[q].T
+        for i in range(turned.shape[0]):
+            turned[i] = turn_buf[i].T
+            turned_beside[i] = beside[i].T
     for at, (k, begin, size) in enumerate(spans):
         group, out, rows = groups[k], outs[k], pl.ds(begin, size)
         for copy in copies[at]:
@@ -103,15 +104,16 @@
             out[pl.ds(tokens, tokens // group), :] = log.astype(jnp.int32).astype(jnp.int16)
 
 
-def projector(flips, groups, pieces, acts, grads, basis_in, basis_out, queries=None):
+def projector(flips, groups, pieces, acts, grads, basis_in, basis_out, queries=None, beside=None):
     tokens, width = acts.shape[2], acts.shape[3]
     both = 2 * basis_in.shape[1]
     steps = sum(len(p) for p in pieces)
-    operands, turned, turn_buf = [acts, grads, basis_in, basis_out], [], []
+    operands, inside, turned, turn_buf = [acts, grads, basis_in, basis_out], [], [], []
     if queries is not None:
+        operands.append(queries)
+        inside.append(beside)
         layers, count, depth = queries.shape
-        operands.append(queries)
-        turned = [jax.ShapeDtypeStruct((layers, depth, count), queries.dtype)]
+        turned = [jax.ShapeDtypeStruct((layers, depth, count), queries.dtype)] * 2
         turn_buf = [pltpu.VMEM(queries.shape, queries.dtype)]
     hbm = pl.BlockSpec(memory_space=pltpu.HBM)
     vmem = pl.BlockSpec(memory_space=pltpu.VMEM)
@@ -128,7 +130,7 @@
             else jax.ShapeDtypeStruct((tokens, both), jnp.float32)
             for g in groups
         ],
-        in_specs=[hbm] * len(operands),
+        in_specs=[hbm] * len(operands) + [vmem] * len(inside),
         out_specs=[vmem] * (len(turned) + len(groups)),
         scratch_shapes=turn_buf
         + [
@@ -146,7 +148,7 @@
             bytes_accessed=4 * len(flips) * tokens * width,
             transcendentals=0,
         ),
-    )(*(pltpu.with_memory_space_constraint(x, pltpu.HBM) for x in operands))
+    )(*(pltpu.with_memory_space_constraint(x, pltpu.HBM) for x in operands), *inside)
 
 
 def decode(ref, tokens):
@@ -249,12 +251,12 @@
     proj_width = basis_in.shape[2]
     operands = (acts_in, grads_out, jnp.swapaxes(basis_in, 1, 2), jnp.swapaxes(basis_out, 1, 2))
 
-    across = swap(queries, "x", 1)
-    queries, far, middle = projector((3, 2), (32, 32), PIECES_TWO, *operands, queries)
+    across, beside = swap(queries, "x", 1), swap(queries, "core", 1)
+    far, middle = projector((3, 2), (32, 32), PIECES_TWO, *operands)
     acts_in, grads_out, far, middle = lax.optimization_barrier((acts_in, grads_out, far, middle))
     far, middle = swap(far, "tensor", 3), swap(middle, "tensor", 2)
     (near,) = projector((1,), (32,), PIECES_ONE, acts_in, grads_out, *operands[2:])
-    (here,) = projector((0,), (0,), PIECES_ONE, acts_in, grads_out, *operands[2:])
+    queries, beside, here = projector((0,), (0,), PIECES_ONE, acts_in, grads_out, *operands[2:], queries, beside)
     near = swap(near, "tensor", 1)
     fisher_beside = swap(fisher_inv, "core", 1)
 
@@ -285,8 +287,8 @@
         out_specs=vmem,
         compiler_params=params,
     )(blocks, in_vmem(fisher_inv), in_vmem(fisher_beside))
-    across, queries, mapped = lax.optimization_barrier((across, queries, mapped))
-    corner, beside = swap(across, "core", 1), swap(queries, "core", 1)
+    across, mapped = lax.optimization_barrier((across, mapped))
+    corner = swap(across, "core", 1)
     mapped = lax.all_to_all(mapped, ("tensor", "x"), 0, 0, tiled=True)
 
     return pl.pallas_call(

time: 49.2 us -> 48.5 us (0.986)
  waiting for transfers between devices: 3.7 us -> 2.29 us
  blocking collectives: 20.2 us -> 20.7 us
    ppermute x7, waiting for transfers between devices: 3.7 us -> 2.29 us  [swap(): lax.ppermute(x, axis, [(i, i ^ flip) for i in range(lax.axis_size(axis))])]
  transfers between devices with their start and end apart: 7 -> 7, of which waited for: 1 -> 1; matrix products, arithmetic and copies ran while one was open for 0% -> 0% of each run, Pallas kernels for 31% -> 32%
where the time goes in v5:
time: 48.5 us; the launch traced here: 48.3 us
  blocking collectives  20.7 us (43%)
  Pallas kernels  17.2 us (35%)
  starting transfers between devices  8.04 us (17%)
  waiting for transfers between devices  2.29 us (5%)
    pallas_call x3, Pallas kernels, projector(): pl.pallas_call(project_pairs, out_shape=turned + [jax.ShapeDtypeStruct((t...  13.4 us
    all_to_all x1, blocking collectives, small(): blocks = lax.all_to_all(blocks, ('tensor', 'x'), 0, 0, tiled=True)  10.3 us
    all_to_all x1, blocking collectives, small(): mapped = lax.all_to_all(mapped, ('tensor', 'x'), 0, 0, tiled=True)  10.3 us
    ppermute x7, starting transfers between devices, swap(): lax.ppermute(x, axis, [(i, i ^ flip) for i in range(lax.axis_size(axis))])  8.04 us
    ppermute x7, waiting for transfers between devices, swap(): lax.ppermute(x, axis, [(i, i ^ flip) for i in range(lax.axis_size(axis))])  2.29 us
    pallas_call x1, Pallas kernels, small(): pl.pallas_call(with_queries, out_shape=jax.ShapeDtypeStruct((acts_in.shap...  1.52 us
    pallas_call x1, Pallas kernels, small(): pl.pallas_call(through_fisher, out_shape=jax.ShapeDtypeStruct((8, 8, fish...  1.22 us
  transfers between devices with their start and end apart: 7, of which 1 were waited for; matrix products, arithmetic and copies ran while one was open for 0% of the time, Pallas kernels for 32%

profile of v5, /device:TPU:0, one launch (start us, length us, event | category | flops | bytes accessed | tf_op | source)
XLA Modules:
  0.0 48.3 jit_solution(11401495072837366105)
XLA Ops:
  0.0 0.5 collective-permute-start.5
  0.5 0.1 collective-permute-start.1
  0.5 2.9 %collective-permute-start = (bf16[2,256,1024]{2,1,0:T(8,128)(2,1)}, bf16[2,256,1024]{2,1,0:T(8,128)(2,1)S(1)}, u32[]{:S(2)}, u32[]{:S(2)}) collective-permute-start(bf16[2,256,1024]{2,1,0:T(8,128)(2,1)} %refs_4_.1), channel_id=1, source_target_pairs={{0,2},{2,0},{1,3},{3,1},{4,6},{6,4},{5,7},{7,5},{8,10},{10,8},{9,1... | collective-permute-start | bytes 3145736 | tf_op jit(solution)/shard_map/ppermute | solution.py:241
  3.5 5.2 %shard_map.73 = (s16[528,128]{1,0:T(8,128)(2,1)S(1)}, s16[528,128]{1,0:T(8,128)(2,1)S(1)}) custom-call(bf16[2,2,512,2048]{3,2,1,0:T(8,128)(2,1)} %refs_0_.3, bf16[2,2,512,2048]{3,2,1,0:T(8,128)(2,1)} %refs_1_.3, bf16[2,64,2048]{2,1,0:T(8,128)(2,1)} %bitcast.2, bf16[2,64,2048]{2,1,0:T(8,128)(2,1)} %bitcast.5), custom_call_target="tpu_custom_call" | custom-call | flops 536870912 | bytes 8388608 | tf_op jit(solution)/shard_map/pallas_call | solution.py:124
  8.6 3.7 %collective-permute-start.2 = (s16[528,128]{1,0:T(8,128)(2,1)S(1)}, s16[528,128]{1,0:T(8,128)(2,1)S(1)}, u32[]{:S(2)}, u32[]{:S(2)}) collective-permute-start(s16[528,128]{1,0:T(8,128)(2,1)S(1)} %get-tuple-element.23), channel_id=1, source_target_pairs={{0,12},{4,8},{8,4},{12,0},{1,13},{5,9},{9,5},{13,1},{2,14},{6,10},... | collective-permute-start | bytes 405512 | tf_op jit(solution)/shard_map/ppermute | solution.py:241
  12.3 0.0 collective-permute-start.3
  12.3 3.5 %shard_map.76 = s16[528,128]{1,0:T(8,128)(2,1)S(1)} custom-call(bf16[2,2,512,2048]{3,2,1,0:T(8,128)(2,1)} %refs_0_.3, bf16[2,2,512,2048]{3,2,1,0:T(8,128)(2,1)} %refs_1_.3, bf16[2,64,2048]{2,1,0:T(8,128)(2,1)} %bitcast.3, bf16[2,64,2048]{2,1,0:T(8,128)(2,1)} %bitcast.6), custom_call_target="tpu_custom_call" | custom-call | flops 268435456 | bytes 4194304 | tf_op jit(solution)/shard_map/pallas_call | solution.py:124
  15.8 0.0 copy-start.1
  15.8 0.0 copy-start
  15.8 0.0 collective-permute-done.1.refs_5_
  15.8 0.8 %collective-permute-start.4 = (s16[528,128]{1,0:T(8,128)(2,1)S(1)}, s16[528,128]{1,0:T(8,128)(2,1)S(1)}, u32[]{:S(2)}, u32[]{:S(2)}) collective-permute-start(s16[528,128]{1,0:T(8,128)(2,1)S(1)} %shard_map.76), channel_id=1, source_target_pairs={{0,4},{4,0},{8,12},{12,8},{1,5},{5,1},{9,13},{13,9},{2,6},{6,2},{1... | collective-permute-start | bytes 405512 | tf_op jit(solution)/shard_map/ppermute | solution.py:241
  16.7 4.7 %shard_map.74 = (bf16[2,1024,256]{2,1,0:T(8,128)(2,1)S(1)}, bf16[2,1024,256]{2,1,0:T(8,128)(2,1)S(1)}, f32[512,128]{1,0:T(8,128)S(1)}) custom-call(bf16[2,2,512,2048]{3,2,1,0:T(8,128)(2,1)} %refs_0_.3, bf16[2,2,512,2048]{3,2,1,0:T(8,128)(2,1)} %refs_1_.3, bf16[2,64,2048]{2,1,0:T(8,128)(2,1)} %bitcast.4, bf16[2,64,2048]{2,1,0:T(8,128)(2,1)} %bitcast.7, ...), custom_call_target="tpu_custom_call" | custom-call | flops 268435456 | bytes 4194304 | tf_op jit(solution)/shard_map/pallas_call | solution.py:124
  21.4 0.0 collective-permute-done.2.first
  21.4 2.3 %collective-permute-done.3.second = s16[528,128]{1,0:T(8,128)(2,1)S(1)} collective-permute-done((s16[528,128]{1,0:T(8,128)(2,1)S(1)}, s16[528,128]{1,0:T(8,128)(2,1)S(1)}, u32[]{:S(2)}, u32[]{:S(2)}) %collective-permute-start.3) | collective-permute-done | bytes 135200 | tf_op jit(solution)/shard_map/ppermute | solution.py:241
  23.7 0.1 shard_map.75.most
  23.8 0.0 collective-permute-done.4.last
  23.8 0.9 %shard_map.77 = f32[8,16,128]{2,1,0:T(8,128)S(1)} custom-call(s32[2]{0:T(128)S(1)} %copy-done.1, f32[512,128]{1,0:T(8,128)S(1)} %shard_map.75.most, s16[528,128]{1,0:T(8,128)(2,1)S(1)} %collective-permute-done.4.last), custom_call_target="tpu_custom_call" | custom-call | tf_op jit(solution)/shard_map/pallas_call | solution.py:272
  24.8 10.3 %all_to_all.10.grads = f32[8,16,128]{2,1,0:T(8,128)S(1)} all-to-all(f32[8,16,128]{2,1,0:T(8,128)S(1)} %shard_map.77), channel_id=1, replica_groups=mesh['parts'=2,'tensor'=4,'x'=2,'core'=2] {'tensor','x'}, dimensions={0} | all-to-all | bytes 131072 | tf_op jit(solution)/shard_map/all_to_all | solution.py:281
  35.1 1.2 %shard_map.78 = f32[8,8,512]{2,1,0:T(8,128)S(1)} custom-call(f32[8,16,128]{2,1,0:T(8,128)S(1)} %all_to_all.10.grads, bf16[2,1024,1024]{2,1,0:T(8,128)(2,1)S(1)} %copy-done, bf16[2,1024,1024]{2,1,0:T(8,128)(2,1)S(1)} %collective-permute-done.5.beside), custom_call_target="tpu_custom_call" | custom-call | tf_op jit(solution)/shard_map/pallas_call | solution.py:283
  36.3 0.0 collective-permute-done.across
  36.4 0.1 collective-permute-start.6
  36.4 10.3 %all_to_all.11.mapped = f32[8,8,512]{2,1,0:T(8,128)S(1)} all-to-all(f32[8,8,512]{2,1,0:T(8,128)S(1)} %shard_map.78), channel_id=1, replica_groups=mesh['parts'=2,'tensor'=4,'x'=2,'core'=2] {'tensor','x'}, dimensions={0} | all-to-all | bytes 262144 | tf_op jit(solution)/shard_map/all_to_all | solution.py:292
  46.7 0.0 collective-permute-done.6.corner
  46.7 1.5 %shard_map.79 = f32[2,256]{1,0:T(2,128)} custom-call(f32[8,8,512]{2,1,0:T(8,128)S(1)} %all_to_all.11.mapped, bf16[2,1024,256]{2,1,0:T(8,128)(2,1)S(1)} %get-tuple-element.28.own, bf16[2,1024,256]{2,1,0:T(8,128)(2,1)S(1)} %get-tuple-element.29.beside, bf16[2,256,1024]{2,1,0:T(8,128)(2,1)S(1)} %collective-permute-done.across, ...), custom_call_target="tpu_custom_call" | custom-call | tf_op jit(solution)/shard_map/pallas_call | solution.py:294
  (3 shorter events, 0.0 us)
Async XLA Ops:
  0.0 24.8 %collective-permute-start.5 = (bf16[2,1024,1024]{2,1,0:T(8,128)(2,1)}, bf16[2,1024,1024]{2,1,0:T(8,128)(2,1)S(1)}, u32[]{:S(2)}, u32[]{:S(2)}) collective-permute-start(bf16[2,1024,1024]{2,1,0:T(8,128)(2,1)} %fisher.1), channel_id=1, source_target_pairs={{0,1},{1,0},{2,3},{3,2},{4,5},{5,4},{6,7},{7,6},{8,9},{9,8},{10,11... | collective-permute-start | bytes 12582920 | tf_op jit(solution)/shard_map/ppermute | solution.py:241
  0.5 15.4 %collective-permute-start.1 = (bf16[2,256,1024]{2,1,0:T(8,128)(2,1)}, bf16[2,256,1024]{2,1,0:T(8,128)(2,1)S(1)}, u32[]{:S(2)}, u32[]{:S(2)}) collective-permute-start(bf16[2,256,1024]{2,1,0:T(8,128)(2,1)} %refs_4_.1), channel_id=1, source_target_pairs={{0,1},{1,0},{2,3},{3,2},{4,5},{5,4},{6,7},{7,6},{8,9},{9,8},{10,11... | collective-permute-start | bytes 3145736 | tf_op jit(solution)/shard_map/ppermute | solution.py:241
  0.5 35.8 %collective-permute-start = (bf16[2,256,1024]{2,1,0:T(8,128)(2,1)}, bf16[2,256,1024]{2,1,0:T(8,128)(2,1)S(1)}, u32[]{:S(2)}, u32[]{:S(2)}) collective-permute-start(bf16[2,256,1024]{2,1,0:T(8,128)(2,1)} %refs_4_.1), channel_id=1, source_target_pairs={{0,2},{2,0},{1,3},{3,1},{4,6},{6,4},{5,7},{7,5},{8,10},{10,8},{9,1... | collective-permute-start | bytes 3145736 | tf_op jit(solution)/shard_map/ppermute | solution.py:241
  8.6 12.8 %collective-permute-start.2 = (s16[528,128]{1,0:T(8,128)(2,1)S(1)}, s16[528,128]{1,0:T(8,128)(2,1)S(1)}, u32[]{:S(2)}, u32[]{:S(2)}) collective-permute-start(s16[528,128]{1,0:T(8,128)(2,1)S(1)} %get-tuple-element.23), channel_id=1, source_target_pairs={{0,12},{4,8},{8,4},{12,0},{1,13},{5,9},{9,5},{13,1},{2,14},{6,10},... | collective-permute-start | bytes 405512 | tf_op jit(solution)/shard_map/ppermute | solution.py:241
  12.3 11.4 %collective-permute-start.3 = (s16[528,128]{1,0:T(8,128)(2,1)S(1)}, s16[528,128]{1,0:T(8,128)(2,1)S(1)}, u32[]{:S(2)}, u32[]{:S(2)}) collective-permute-start(s16[528,128]{1,0:T(8,128)(2,1)S(1)} %get-tuple-element.24), channel_id=1, source_target_pairs={{0,8},{4,12},{8,0},{12,4},{1,9},{5,13},{9,1},{13,5},{2,10},{6,14},... | collective-permute-start | bytes 405512 | tf_op jit(solution)/shard_map/ppermute | solution.py:241
  15.8 8.0 %copy-start.1 = (s32[2]{0:T(128)S(1)}, s32[2]{0:T(128)}, u32[]{:S(2)}) copy-start(s32[2]{0:T(128)} %lengths.1) | copy-start | bytes 28
  15.8 19.3 %copy-start = (bf16[2,1024,1024]{2,1,0:T(8,128)(2,1)S(1)}, bf16[2,1024,1024]{2,1,0:T(8,128)(2,1)}, u32[]{:S(2)}) copy-start(bf16[2,1024,1024]{2,1,0:T(8,128)(2,1)} %fisher.1) | copy-start | bytes 12582916
  15.8 8.0 %collective-permute-start.4 = (s16[528,128]{1,0:T(8,128)(2,1)S(1)}, s16[528,128]{1,0:T(8,128)(2,1)S(1)}, u32[]{:S(2)}, u32[]{:S(2)}) collective-permute-start(s16[528,128]{1,0:T(8,128)(2,1)S(1)} %shard_map.76), channel_id=1, source_target_pairs={{0,4},{4,0},{8,12},{12,8},{1,5},{5,1},{9,13},{13,9},{2,6},{6,2},{1... | collective-permute-start | bytes 405512 | tf_op jit(solution)/shard_map/ppermute | solution.py:241
  36.4 10.4 %collective-permute-start.6 = (bf16[2,256,1024]{2,1,0:T(8,128)(2,1)S(1)}, bf16[2,256,1024]{2,1,0:T(8,128)(2,1)S(1)}, u32[]{:S(2)}, u32[]{:S(2)}) collective-permute-start(bf16[2,256,1024]{2,1,0:T(8,128)(2,1)S(1)} %collective-permute-done.across), channel_id=1, source_target_pairs={{0,1},{1,0},{2,3},{3,2},{4,5},{5,4},{6,7},{7,6},{8,9},{9,8},{10,11... | collective-permute-start | bytes 3145736 | tf_op jit(solution)/shard_map/ppermute | solution.py:241

commit v6 on v5

--- a/solution.py
+++ b/solution.py
@@ -46,13 +46,13 @@
     outs = refs
     examples, tokens = acts.shape[1], acts.shape[2]
     here = lax.axis_index("tensor")
-    layer = (here ^ flips[0]) // examples
-    first = [
-        pltpu.make_async_copy(basis_out.at[layer], out_buf, basis_sems.at[0]),
-        pltpu.make_async_copy(basis_in.at[layer], in_buf, basis_sems.at[1]),
-    ]
+    layers = [(here ^ flip) // examples for flip in flips]
+    first = []
+    for k, layer in enumerate(layers):
+        first.append(pltpu.make_async_copy(basis_out.at[layer], out_buf.at[k], basis_sems.at[0, k]))
+        first.append(pltpu.make_async_copy(basis_in.at[layer], in_buf.at[k], basis_sems.at[1, k]))
     if turn:
-        first.append(pltpu.make_async_copy(queries, turn_buf, basis_sems.at[2]))
+        first.append(pltpu.make_async_copy(queries, turn_buf, basis_sems.at[2, 0]))
     copies, spans = [], []
     for k, flip in enumerate(flips):
         example = (here ^ flip) % examples
@@ -62,8 +62,8 @@
             spans.append((k, begin, size))
             copies.append(
                 (
-                    pltpu.make_async_copy(grads.at[layer, example, rows, :], g_buf.at[k, rows, :], sems.at[0, at]),
-                    pltpu.make_async_copy(acts.at[layer, example, rows, :], a_buf.at[k, rows, :], sems.at[1, at]),
+                    pltpu.make_async_copy(grads.at[layers[k], example, rows, :], g_buf.at[k, rows, :], sems.at[0, at]),
+                    pltpu.make_async_copy(acts.at[layers[k], example, rows, :], a_buf.at[k, rows, :], sems.at[1, at]),
                 )
             )
             begin += size
@@ -85,8 +85,8 @@
         if at + AHEAD < len(copies):
             for copy in copies[at + AHEAD]:
                 copy.start()
-        proj_out = nt(g_buf[k, rows, :], out_buf[...])
-        proj_in = nt(a_buf[k, rows, :], in_buf[...])
+        proj_out = nt(g_buf[k, rows, :], out_buf[k])
+        proj_in = nt(a_buf[k, rows, :], in_buf[k])
         both = jnp.concatenate([proj_out, proj_in], axis=1)
         if not group:
             out[rows, :] = both
@@ -136,18 +136,13 @@
         + [
             pltpu.VMEM((len(flips), tokens, width), acts.dtype),
             pltpu.VMEM((len(flips), tokens, width), grads.dtype),
-            pltpu.VMEM(basis_in.shape[1:], basis_in.dtype),
-            pltpu.VMEM(basis_out.shape[1:], basis_out.dtype),
+            pltpu.VMEM((len(flips), *basis_in.shape[1:]), basis_in.dtype),
+            pltpu.VMEM((len(flips), *basis_out.shape[1:]), basis_out.dtype),
             pltpu.VMEM((tokens // 16, both), jnp.float32),
             pltpu.SemaphoreType.DMA((2, steps)),
-            pltpu.SemaphoreType.DMA((3,)),
+            pltpu.SemaphoreType.DMA((3, len(flips))),
         ],
         compiler_params=pltpu.CompilerParams(vmem_limit_bytes=VMEM),
-        cost_estimate=pl.CostEstimate(
-            flops=2 * len(flips) * tokens * width * both,
-            bytes_accessed=4 * len(flips) * tokens * width,
-            transcendentals=0,
-        ),
     )(*(pltpu.with_memory_space_constraint(x, pltpu.HBM) for x in operands), *inside)
 
 
@@ -160,9 +155,8 @@
     return (codes.reshape(shared, tokens // shared, both) * scale[:, None, :]).reshape(tokens, both)
 
 
-def add_up(own, first, second, out):
-    tokens = own.shape[0]
-    out[...] = own[...] + decode(first, tokens) + decode(second, tokens)
+def add_up(total, partial, out):
+    out[...] = total[...] + decode(partial, total.shape[0])
 
 
 def outer(lengths, most, last, out, grad):
@@ -252,22 +246,23 @@
     operands = (acts_in, grads_out, jnp.swapaxes(basis_in, 1, 2), jnp.swapaxes(basis_out, 1, 2))
 
     across, beside = swap(queries, "x", 1), swap(queries, "core", 1)
-    far, middle = projector((3, 2), (32, 32), PIECES_TWO, *operands)
-    acts_in, grads_out, far, middle = lax.optimization_barrier((acts_in, grads_out, far, middle))
+    (far,) = projector((3,), (32,), PIECES_ONE, *operands)
+    acts_in, grads_out, far = lax.optimization_barrier((acts_in, grads_out, far))
+    middle, near = projector((2, 1), (32, 32), PIECES_TWO, acts_in, grads_out, *operands[2:])
+    acts_in, middle, near = lax.optimization_barrier((acts_in, middle, near))
+    queries, beside, here = projector((0,), (0,), PIECES_ONE, acts_in, grads_out, *operands[2:], queries, beside)
     far, middle = swap(far, "tensor", 3), swap(middle, "tensor", 2)
-    (near,) = projector((1,), (32,), PIECES_ONE, acts_in, grads_out, *operands[2:])
-    queries, beside, here = projector((0,), (0,), PIECES_ONE, acts_in, grads_out, *operands[2:], queries, beside)
     near = swap(near, "tensor", 1)
     fisher_beside = swap(fisher_inv, "core", 1)
 
-    most = pl.pallas_call(
-        add_up,
-        out_shape=jax.ShapeDtypeStruct(here.shape, jnp.float32),
-        in_specs=[vmem] * 3,
-        out_specs=vmem,
-        compiler_params=params,
-        cost_estimate=pl.CostEstimate(flops=0, bytes_accessed=1 << 21, transcendentals=0),
-    )(here, far, middle)
+    for partial in (far, middle):
+        here = pl.pallas_call(
+            add_up,
+            out_shape=jax.ShapeDtypeStruct(here.shape, jnp.float32),
+            in_specs=[vmem] * 2,
+            out_specs=vmem,
+            compiler_params=params,
+        )(here, partial)
 
     blocks = pl.pallas_call(
         outer,
@@ -276,7 +271,7 @@
         out_specs=vmem,
         scratch_shapes=[pltpu.VMEM((proj_width, 2 * proj_width), jnp.float32)],
         compiler_params=params,
-    )(lengths, most, near)
+    )(lengths, here, near)
     blocks, fisher_beside = lax.optimization_barrier((blocks, fisher_beside))
     blocks = lax.all_to_all(blocks, ("tensor", "x"), 0, 0, tiled=True)
 

time: 48.5 us -> 47.6 us (0.981)
  blocking collectives: 20.7 us -> 19.7 us
    all_to_all x1, blocking collectives: 10.3 us -> 9.37 us  [small(): blocks = lax.all_to_all(blocks, ('tensor', 'x'), 0, 0, tiled=True)]
  transfers between devices with their start and end apart: 7 -> 7, of which waited for: 1 -> 2; matrix products, arithmetic and copies ran while one was open for 0% -> 0% of each run, Pallas kernels for 32% -> 33%
where the time goes in v6:
time: 47.6 us; the launch traced here: 47.4 us
  blocking collectives  19.7 us (41%)
  Pallas kernels  17.4 us (37%)
  starting transfers between devices  8.02 us (17%)
  waiting for transfers between devices  2.26 us (5%)
    pallas_call x3, Pallas kernels, projector(): pl.pallas_call(project_pairs, out_shape=turned + [jax.ShapeDtypeStruct((t...  13.6 us
    all_to_all x1, blocking collectives, small(): mapped = lax.all_to_all(mapped, ('tensor', 'x'), 0, 0, tiled=True)  10.3 us
    all_to_all x1, blocking collectives, small(): blocks = lax.all_to_all(blocks, ('tensor', 'x'), 0, 0, tiled=True)  9.37 us
    ppermute x7, starting transfers between devices, swap(): lax.ppermute(x, axis, [(i, i ^ flip) for i in range(lax.axis_size(axis))])  8.02 us
    ppermute x7, waiting for transfers between devices, swap(): lax.ppermute(x, axis, [(i, i ^ flip) for i in range(lax.axis_size(axis))])  2.26 us
    pallas_call x1, Pallas kernels, small(): pl.pallas_call(with_queries, out_shape=jax.ShapeDtypeStruct((acts_in.shap...  1.52 us
    pallas_call x1, Pallas kernels, small(): pl.pallas_call(through_fisher, out_shape=jax.ShapeDtypeStruct((8, 8, fish...  1.22 us
  transfers between devices with their start and end apart: 7, of which 2 were waited for; matrix products, arithmetic and copies ran while one was open for 0% of the time, Pallas kernels for 33%

profile of v6, /device:TPU:0, one launch (start us, length us, event | category | flops | bytes accessed | tf_op | source)
XLA Modules:
  0.0 47.4 jit_solution(4038592420712228577)
XLA Ops:
  0.0 0.5 collective-permute-start.5
  0.5 0.1 collective-permute-start.1
  0.5 2.9 %collective-permute-start = (bf16[2,256,1024]{2,1,0:T(8,128)(2,1)}, bf16[2,256,1024]{2,1,0:T(8,128)(2,1)S(1)}, u32[]{:S(2)}, u32[]{:S(2)}) collective-permute-start(bf16[2,256,1024]{2,1,0:T(8,128)(2,1)} %refs_4_.1), channel_id=1, source_target_pairs={{0,2},{2,0},{1,3},{3,1},{4,6},{6,4},{5,7},{7,5},{8,10},{10,8},{9,1... | collective-permute-start | bytes 3145736 | tf_op jit(solution)/shard_map/ppermute | solution.py:235
  3.5 3.5 %shard_map.73 = s16[528,128]{1,0:T(8,128)(2,1)S(1)} custom-call(bf16[2,2,512,2048]{3,2,1,0:T(8,128)(2,1)} %refs_0_.3, bf16[2,2,512,2048]{3,2,1,0:T(8,128)(2,1)} %refs_1_.3, bf16[2,64,2048]{2,1,0:T(8,128)(2,1)} %bitcast.2, bf16[2,64,2048]{2,1,0:T(8,128)(2,1)} %bitcast.5), custom_call_target="tpu_custom_call" | custom-call | tf_op jit(solution)/shard_map/pallas_call | solution.py:124
  7.0 3.7 %collective-permute-start.2 = (s16[528,128]{1,0:T(8,128)(2,1)S(1)}, s16[528,128]{1,0:T(8,128)(2,1)S(1)}, u32[]{:S(2)}, u32[]{:S(2)}) collective-permute-start(s16[528,128]{1,0:T(8,128)(2,1)S(1)} %shard_map.73), channel_id=1, source_target_pairs={{0,12},{4,8},{8,4},{12,0},{1,13},{5,9},{9,5},{13,1},{2,14},{6,10},... | collective-permute-start | bytes 405512 | tf_op jit(solution)/shard_map/ppermute | solution.py:235
  10.6 5.3 %shard_map.74 = (s16[528,128]{1,0:T(8,128)(2,1)S(1)}, s16[528,128]{1,0:T(8,128)(2,1)S(1)}) custom-call(bf16[2,2,512,2048]{3,2,1,0:T(8,128)(2,1)} %refs_0_.3, bf16[2,2,512,2048]{3,2,1,0:T(8,128)(2,1)} %refs_1_.3, bf16[2,64,2048]{2,1,0:T(8,128)(2,1)} %bitcast.3, bf16[2,64,2048]{2,1,0:T(8,128)(2,1)} %bitcast.6), custom_call_target="tpu_custom_call" | custom-call | tf_op jit(solution)/shard_map/pallas_call | solution.py:124
  16.0 0.0 copy-start.1
  16.0 0.0 copy-start
  16.0 0.1 collective-permute-start.3
  16.1 0.0 collective-permute-done.1.refs_5_
  16.1 0.8 %collective-permute-start.4 = (s16[528,128]{1,0:T(8,128)(2,1)S(1)}, s16[528,128]{1,0:T(8,128)(2,1)S(1)}, u32[]{:S(2)}, u32[]{:S(2)}) collective-permute-start(s16[528,128]{1,0:T(8,128)(2,1)S(1)} %get-tuple-element.28), channel_id=1, source_target_pairs={{0,4},{4,0},{8,12},{12,8},{1,5},{5,1},{9,13},{13,9},{2,6},{6,2},{1... | collective-permute-start | bytes 405512 | tf_op jit(solution)/shard_map/ppermute | solution.py:235
  16.8 4.8 %shard_map.75 = (bf16[2,1024,256]{2,1,0:T(8,128)(2,1)S(1)}, bf16[2,1024,256]{2,1,0:T(8,128)(2,1)S(1)}, f32[512,128]{1,0:T(8,128)S(1)}) custom-call(bf16[2,2,512,2048]{3,2,1,0:T(8,128)(2,1)} %refs_0_.3, bf16[2,2,512,2048]{3,2,1,0:T(8,128)(2,1)} %refs_1_.3, bf16[2,64,2048]{2,1,0:T(8,128)(2,1)} %bitcast.4, bf16[2,64,2048]{2,1,0:T(8,128)(2,1)} %bitcast.7, ...), custom_call_target="tpu_custom_call" | custom-call | tf_op jit(solution)/shard_map/pallas_call | solution.py:124
  21.6 0.0 collective-permute-done.2.partial
  21.7 2.2 %collective-permute-done.3.partial = s16[528,128]{1,0:T(8,128)(2,1)S(1)} collective-permute-done((s16[528,128]{1,0:T(8,128)(2,1)S(1)}, s16[528,128]{1,0:T(8,128)(2,1)S(1)}, u32[]{:S(2)}, u32[]{:S(2)}) %collective-permute-start.3) | collective-permute-done | bytes 135200 | tf_op jit(solution)/shard_map/ppermute | solution.py:235
  23.9 0.1 collective-permute-done.4.last
  24.0 0.9 %shard_map.78 = f32[8,16,128]{2,1,0:T(8,128)S(1)} custom-call(s32[2]{0:T(128)S(1)} %copy-done.1, f32[512,128]{1,0:T(8,128)S(1)} %shard_map.77.most, s16[528,128]{1,0:T(8,128)(2,1)S(1)} %collective-permute-done.4.last), custom_call_target="tpu_custom_call" | custom-call | tf_op jit(solution)/shard_map/pallas_call | solution.py:267
  24.9 0.0 collective-permute-done.5.beside
  24.9 9.4 %all_to_all.10.grads = f32[8,16,128]{2,1,0:T(8,128)S(1)} all-to-all(f32[8,16,128]{2,1,0:T(8,128)S(1)} %shard_map.78), channel_id=1, replica_groups=mesh['parts'=2,'tensor'=4,'x'=2,'core'=2] {'tensor','x'}, dimensions={0} | all-to-all | bytes 131072 | tf_op jit(solution)/shard_map/all_to_all | solution.py:276
  34.3 1.2 %shard_map.79 = f32[8,8,512]{2,1,0:T(8,128)S(1)} custom-call(f32[8,16,128]{2,1,0:T(8,128)S(1)} %all_to_all.10.grads, bf16[2,1024,1024]{2,1,0:T(8,128)(2,1)S(1)} %copy-done, bf16[2,1024,1024]{2,1,0:T(8,128)(2,1)S(1)} %collective-permute-done.5.beside), custom_call_target="tpu_custom_call" | custom-call | tf_op jit(solution)/shard_map/pallas_call | solution.py:278
  35.5 0.0 collective-permute-done.across
  35.5 0.1 collective-permute-start.6
  35.6 10.3 %all_to_all.11.mapped = f32[8,8,512]{2,1,0:T(8,128)S(1)} all-to-all(f32[8,8,512]{2,1,0:T(8,128)S(1)} %shard_map.79), channel_id=1, replica_groups=mesh['parts'=2,'tensor'=4,'x'=2,'core'=2] {'tensor','x'}, dimensions={0} | all-to-all | bytes 262144 | tf_op jit(solution)/shard_map/all_to_all | solution.py:287
  45.9 0.0 collective-permute-done.6.corner
  45.9 1.5 %shard_map.80 = f32[2,256]{1,0:T(2,128)} custom-call(f32[8,8,512]{2,1,0:T(8,128)S(1)} %all_to_all.11.mapped, bf16[2,1024,256]{2,1,0:T(8,128)(2,1)S(1)} %get-tuple-element.32.own, bf16[2,1024,256]{2,1,0:T(8,128)(2,1)S(1)} %get-tuple-element.33.beside, bf16[2,256,1024]{2,1,0:T(8,128)(2,1)S(1)} %collective-permute-done.across, ...), custom_call_target="tpu_custom_call" | custom-call | tf_op jit(solution)/shard_map/pallas_call | solution.py:289
  (4 shorter events, 0.1 us)
Async XLA Ops:
  0.0 24.9 %collective-permute-start.5 = (bf16[2,1024,1024]{2,1,0:T(8,128)(2,1)}, bf16[2,1024,1024]{2,1,0:T(8,128)(2,1)S(1)}, u32[]{:S(2)}, u32[]{:S(2)}) collective-permute-start(bf16[2,1024,1024]{2,1,0:T(8,128)(2,1)} %fisher.1), channel_id=1, source_target_pairs={{0,1},{1,0},{2,3},{3,2},{4,5},{5,4},{6,7},{7,6},{8,9},{9,8},{10,11... | collective-permute-start | bytes 12582920 | tf_op jit(solution)/shard_map/ppermute | solution.py:235
  0.5 15.6 %collective-permute-start.1 = (bf16[2,256,1024]{2,1,0:T(8,128)(2,1)}, bf16[2,256,1024]{2,1,0:T(8,128)(2,1)S(1)}, u32[]{:S(2)}, u32[]{:S(2)}) collective-permute-start(bf16[2,256,1024]{2,1,0:T(8,128)(2,1)} %refs_4_.1), channel_id=1, source_target_pairs={{0,1},{1,0},{2,3},{3,2},{4,5},{5,4},{6,7},{7,6},{8,9},{9,8},{10,11... | collective-permute-start | bytes 3145736 | tf_op jit(solution)/shard_map/ppermute | solution.py:235
  0.5 35.0 %collective-permute-start = (bf16[2,256,1024]{2,1,0:T(8,128)(2,1)}, bf16[2,256,1024]{2,1,0:T(8,128)(2,1)S(1)}, u32[]{:S(2)}, u32[]{:S(2)}) collective-permute-start(bf16[2,256,1024]{2,1,0:T(8,128)(2,1)} %refs_4_.1), channel_id=1, source_target_pairs={{0,2},{2,0},{1,3},{3,1},{4,6},{6,4},{5,7},{7,5},{8,10},{10,8},{9,1... | collective-permute-start | bytes 3145736 | tf_op jit(solution)/shard_map/ppermute | solution.py:235
  7.0 14.7 %collective-permute-start.2 = (s16[528,128]{1,0:T(8,128)(2,1)S(1)}, s16[528,128]{1,0:T(8,128)(2,1)S(1)}, u32[]{:S(2)}, u32[]{:S(2)}) collective-permute-start(s16[528,128]{1,0:T(8,128)(2,1)S(1)} %shard_map.73), channel_id=1, source_target_pairs={{0,12},{4,8},{8,4},{12,0},{1,13},{5,9},{9,5},{13,1},{2,14},{6,10},... | collective-permute-start | bytes 405512 | tf_op jit(solution)/shard_map/ppermute | solution.py:235
  16.0 8.0 %copy-start.1 = (s32[2]{0:T(128)S(1)}, s32[2]{0:T(128)}, u32[]{:S(2)}) copy-start(s32[2]{0:T(128)} %lengths.1) | copy-start | bytes 28
  16.0 18.3 %copy-start = (bf16[2,1024,1024]{2,1,0:T(8,128)(2,1)S(1)}, bf16[2,1024,1024]{2,1,0:T(8,128)(2,1)}, u32[]{:S(2)}) copy-start(bf16[2,1024,1024]{2,1,0:T(8,128)(2,1)} %fisher.1) | copy-start | bytes 12582916
  16.0 7.8 %collective-permute-start.3 = (s16[528,128]{1,0:T(8,128)(2,1)S(1)}, s16[528,128]{1,0:T(8,128)(2,1)S(1)}, u32[]{:S(2)}, u32[]{:S(2)}) collective-permute-start(s16[528,128]{1,0:T(8,128)(2,1)S(1)} %get-tuple-element.27), channel_id=1, source_target_pairs={{0,8},{4,12},{8,0},{12,4},{1,9},{5,13},{9,1},{13,5},{2,10},{6,14},... | collective-permute-start | bytes 405512 | tf_op jit(solution)/shard_map/ppermute | solution.py:235
  16.1 7.9 %collective-permute-start.4 = (s16[528,128]{1,0:T(8,128)(2,1)S(1)}, s16[528,128]{1,0:T(8,128)(2,1)S(1)}, u32[]{:S(2)}, u32[]{:S(2)}) collective-permute-start(s16[528,128]{1,0:T(8,128)(2,1)S(1)} %get-tuple-element.28), channel_id=1, source_target_pairs={{0,4},{4,0},{8,12},{12,8},{1,5},{5,1},{9,13},{13,9},{2,6},{6,2},{1... | collective-permute-start | bytes 405512 | tf_op jit(solution)/shard_map/ppermute | solution.py:235
  35.5 10.4 %collective-permute-start.6 = (bf16[2,256,1024]{2,1,0:T(8,128)(2,1)S(1)}, bf16[2,256,1024]{2,1,0:T(8,128)(2,1)S(1)}, u32[]{:S(2)}, u32[]{:S(2)}) collective-permute-start(bf16[2,256,1024]{2,1,0:T(8,128)(2,1)S(1)} %collective-permute-done.across), channel_id=1, source_target_pairs={{0,1},{1,0},{2,3},{3,2},{4,5},{5,4},{6,7},{7,6},{8,9},{9,8},{10,11... | collective-permute-start | bytes 3145736 | tf_op jit(solution)/shard_map/ppermute | solution.py:235

commit v7 on v6

--- a/solution.py
+++ b/solution.py
@@ -39,10 +39,10 @@
 
 def project(flips, groups, pieces, turn, acts, grads, basis_in, basis_out, *refs):
     *refs, a_buf, g_buf, in_buf, out_buf, scale_log, sems, basis_sems = refs
-    queries = beside = turned = turned_beside = turn_buf = None
+    queries = beside = lengths = turned = turned_beside = weights = turn_buf = None
     if turn:
         *refs, turn_buf = refs
-        queries, beside, turned, turned_beside, *refs = refs
+        queries, beside, lengths, turned, turned_beside, weights, *refs = refs
     outs = refs
     examples, tokens = acts.shape[1], acts.shape[2]
     here = lax.axis_index("tensor")
@@ -78,6 +78,7 @@
         for i in range(turned.shape[0]):
             turned[i] = turn_buf[i].T
             turned_beside[i] = beside[i].T
+        weigh(lengths, weights)
     for at, (k, begin, size) in enumerate(spans):
         group, out, rows = groups[k], outs[k], pl.ds(begin, size)
         for copy in copies[at]:
@@ -104,19 +105,20 @@
             out[pl.ds(tokens, tokens // group), :] = log.astype(jnp.int32).astype(jnp.int16)
 
 
-def projector(flips, groups, pieces, acts, grads, basis_in, basis_out, queries=None, beside=None):
+def projector(flips, groups, pieces, acts, grads, basis_in, basis_out, queries=None, beside=None, lengths=None):
     tokens, width = acts.shape[2], acts.shape[3]
     both = 2 * basis_in.shape[1]
     steps = sum(len(p) for p in pieces)
     operands, inside, turned, turn_buf = [acts, grads, basis_in, basis_out], [], [], []
     if queries is not None:
         operands.append(queries)
-        inside.append(beside)
+        inside += [beside, lengths]
         layers, count, depth = queries.shape
         turned = [jax.ShapeDtypeStruct((layers, depth, count), queries.dtype)] * 2
+        turned.append(jax.ShapeDtypeStruct((tokens, both), jnp.float32))
         turn_buf = [pltpu.VMEM(queries.shape, queries.dtype)]
     hbm = pl.BlockSpec(memory_space=pltpu.HBM)
-    vmem = pl.BlockSpec(memory_space=pltpu.VMEM)
+    vmem, smem = pl.BlockSpec(memory_space=pltpu.VMEM), pl.BlockSpec(memory_space=pltpu.SMEM)
 
     def project_pairs(*refs):
         project(flips, groups, pieces, queries is not None, *refs)
@@ -130,7 +132,7 @@
             else jax.ShapeDtypeStruct((tokens, both), jnp.float32)
             for g in groups
         ],
-        in_specs=[hbm] * len(operands) + [vmem] * len(inside),
+        in_specs=[hbm] * len(operands) + [vmem, smem][: len(inside)],
         out_specs=[vmem] * (len(turned) + len(groups)),
         scratch_shapes=turn_buf
         + [
@@ -159,16 +161,19 @@
     out[...] = total[...] + decode(partial, total.shape[0])
 
 
-def outer(lengths, most, last, out, grad):
+def weigh(lengths, weights):
+    tokens, both = weights.shape
+    count = lengths[lax.axis_index("tensor") % lengths.shape[0]]
+    row = lax.broadcasted_iota(jnp.int32, (tokens, both), 0)
+    lane = lax.broadcasted_iota(jnp.int32, (1, both), 1)
+    share = 1.0 / jnp.full((1, both), count, jnp.int32).astype(jnp.float32)
+    weights[...] = jnp.where(row < count, jnp.where(lane < both // 2, share, 1.0), 0.0)
+
+
+def outer(weights, most, last, out, grad):
     tokens, both = most.shape
     half = both // 2
-    example = lax.axis_index("tensor") % lengths.shape[0]
-    count = lengths[example]
-    total = most[...] + decode(last, tokens)
-    row = lax.broadcasted_iota(jnp.int32, (tokens, both), 0)
-    lane = lax.broadcasted_iota(jnp.int32, (1, both), 1)
-    weight = jnp.where(lane < half, 1.0 / jnp.full((1, both), count, jnp.int32).astype(jnp.float32), 1.0)
-    weighted = jnp.where(row < count, total * weight, 0.0)
+    weighted = (most[...] + decode(last, tokens)) * weights[...]
     first = weighted.astype(jnp.bfloat16)
     rest = (weighted - first.astype(jnp.float32)).astype(jnp.bfloat16)
     wide = tn(first, jnp.concatenate([first, rest], axis=1))
@@ -250,7 +255,9 @@
     acts_in, grads_out, far = lax.optimization_barrier((acts_in, grads_out, far))
     middle, near = projector((2, 1), (32, 32), PIECES_TWO, acts_in, grads_out, *operands[2:])
     acts_in, middle, near = lax.optimization_barrier((acts_in, middle, near))
-    queries, beside, here = projector((0,), (0,), PIECES_ONE, acts_in, grads_out, *operands[2:], queries, beside)
+    queries, beside, weights, here = projector(
+        (0,), (0,), PIECES_ONE, acts_in, grads_out, *operands[2:], queries, beside, lengths
+    )
     far, middle = swap(far, "tensor", 3), swap(middle, "tensor", 2)
     near = swap(near, "tensor", 1)
     fisher_beside = swap(fisher_inv, "core", 1)
@@ -267,11 +274,11 @@
     blocks = pl.pallas_call(
         outer,
         out_shape=jax.ShapeDtypeStruct((8, proj_width // 4, 2 * proj_width), jnp.float32),
-        in_specs=[pl.BlockSpec(memory_space=pltpu.SMEM)] + [vmem] * 2,
+        in_specs=[vmem] * 3,
         out_specs=vmem,
         scratch_shapes=[pltpu.VMEM((proj_width, 2 * proj_width), jnp.float32)],
         compiler_params=params,
-    )(lengths, here, near)
+    )(weights, here, near)
     blocks, fisher_beside = lax.optimization_barrier((blocks, fisher_beside))
     blocks = lax.all_to_all(blocks, ("tensor", "x"), 0, 0, tiled=True)
 

time: 47.6 us -> 47.2 us (level)
    pallas_call x1, Pallas kernels: 0.94 us -> 0.36 us  [small(): pl.pallas_call(outer, out_shape=jax.ShapeDtypeStruct((8, proj_width // 4,...]
where the time goes in v7:
time: 47.2 us; the launch traced here: 47 us
  blocking collectives  19.9 us (42%)
  Pallas kernels  17 us (36%)
  starting transfers between devices  8.02 us (17%)
  waiting for transfers between devices  2.05 us (4%)
    pallas_call x3, Pallas kernels, projector(): pl.pallas_call(project_pairs, out_shape=turned + [jax.ShapeDtypeStruct((t...  13.8 us
    all_to_all x1, blocking collectives, small(): mapped = lax.all_to_all(mapped, ('tensor', 'x'), 0, 0, tiled=True)  10.3 us
    all_to_all x1, blocking collectives, small(): blocks = lax.all_to_all(blocks, ('tensor', 'x'), 0, 0, tiled=True)  9.57 us
    ppermute x7, starting transfers between devices, swap(): lax.ppermute(x, axis, [(i, i ^ flip) for i in range(lax.axis_size(axis))])  8.02 us
    ppermute x7, waiting for transfers between devices, swap(): lax.ppermute(x, axis, [(i, i ^ flip) for i in range(lax.axis_size(axis))])  2.05 us
    pallas_call x1, Pallas kernels, small(): pl.pallas_call(with_queries, out_shape=jax.ShapeDtypeStruct((acts_in.shap...  1.52 us
    pallas_call x1, Pallas kernels, small(): pl.pallas_call(through_fisher, out_shape=jax.ShapeDtypeStruct((8, 8, fish...  1.22 us
  transfers between devices with their start and end apart: 7, of which 2 were waited for; matrix products, arithmetic and copies ran while one was open for 0% of the time, Pallas kernels for 33%

profile of v7, /device:TPU:0, one launch (start us, length us, event | category | flops | bytes accessed | tf_op | source)
XLA Modules:
  0.0 47.0 jit_solution(14072214694316254148)
XLA Ops:
  0.0 0.5 collective-permute-start.5
  0.5 0.1 collective-permute-start.1
  0.5 2.9 %collective-permute-start = (bf16[2,256,1024]{2,1,0:T(8,128)(2,1)}, bf16[2,256,1024]{2,1,0:T(8,128)(2,1)S(1)}, u32[]{:S(2)}, u32[]{:S(2)}) collective-permute-start(bf16[2,256,1024]{2,1,0:T(8,128)(2,1)} %refs_4_.1), channel_id=1, source_target_pairs={{0,2},{2,0},{1,3},{3,1},{4,6},{6,4},{5,7},{7,5},{8,10},{10,8},{9,1... | collective-permute-start | bytes 3145736 | tf_op jit(solution)/shard_map/ppermute | solution.py:240
  3.5 3.5 %shard_map.73 = s16[528,128]{1,0:T(8,128)(2,1)S(1)} custom-call(bf16[2,2,512,2048]{3,2,1,0:T(8,128)(2,1)} %refs_0_.3, bf16[2,2,512,2048]{3,2,1,0:T(8,128)(2,1)} %refs_1_.3, bf16[2,64,2048]{2,1,0:T(8,128)(2,1)} %bitcast.2, bf16[2,64,2048]{2,1,0:T(8,128)(2,1)} %bitcast.5), custom_call_target="tpu_custom_call" | custom-call | tf_op jit(solution)/shard_map/pallas_call | solution.py:126
  7.0 0.0 copy-start.1
  7.0 3.7 %collective-permute-start.2 = (s16[528,128]{1,0:T(8,128)(2,1)S(1)}, s16[528,128]{1,0:T(8,128)(2,1)S(1)}, u32[]{:S(2)}, u32[]{:S(2)}) collective-permute-start(s16[528,128]{1,0:T(8,128)(2,1)S(1)} %shard_map.73), channel_id=1, source_target_pairs={{0,12},{4,8},{8,4},{12,0},{1,13},{5,9},{9,5},{13,1},{2,14},{6,10},... | collective-permute-start | bytes 405512 | tf_op jit(solution)/shard_map/ppermute | solution.py:240
  10.6 5.3 %shard_map.74 = (s16[528,128]{1,0:T(8,128)(2,1)S(1)}, s16[528,128]{1,0:T(8,128)(2,1)S(1)}) custom-call(bf16[2,2,512,2048]{3,2,1,0:T(8,128)(2,1)} %refs_0_.3, bf16[2,2,512,2048]{3,2,1,0:T(8,128)(2,1)} %refs_1_.3, bf16[2,64,2048]{2,1,0:T(8,128)(2,1)} %bitcast.3, bf16[2,64,2048]{2,1,0:T(8,128)(2,1)} %bitcast.6), custom_call_target="tpu_custom_call" | custom-call | tf_op jit(solution)/shard_map/pallas_call | solution.py:126
  16.0 0.0 copy-start
  16.0 0.1 collective-permute-start.3
  16.1 0.0 collective-permute-done.1.refs_5_
  16.1 0.8 %collective-permute-start.4 = (s16[528,128]{1,0:T(8,128)(2,1)S(1)}, s16[528,128]{1,0:T(8,128)(2,1)S(1)}, u32[]{:S(2)}, u32[]{:S(2)}) collective-permute-start(s16[528,128]{1,0:T(8,128)(2,1)S(1)} %get-tuple-element.30), channel_id=1, source_target_pairs={{0,4},{4,0},{8,12},{12,8},{1,5},{5,1},{9,13},{13,9},{2,6},{6,2},{1... | collective-permute-start | bytes 405512 | tf_op jit(solution)/shard_map/ppermute | solution.py:240
  16.8 5.0 %shard_map.75 = (bf16[2,1024,256]{2,1,0:T(8,128)(2,1)S(1)}, bf16[2,1024,256]{2,1,0:T(8,128)(2,1)S(1)}, f32[512,128]{1,0:T(8,128)S(1)}, f32[512,128]{1,0:T(8,128)S(1)}) custom-call(bf16[2,2,512,2048]{3,2,1,0:T(8,128)(2,1)} %refs_0_.3, bf16[2,2,512,2048]{3,2,1,0:T(8,128)(2,1)} %refs_1_.3, bf16[2,64,2048]{2,1,0:T(8,128)(2,1)} %bitcast.4, ...), custom_call_target="tpu_custom_call" | custom-call | tf_op jit(solution)/shard_map/pallas_call | solution.py:126
  21.8 0.0 collective-permute-done.2.partial
  21.9 1.9 %collective-permute-done.3.partial = s16[528,128]{1,0:T(8,128)(2,1)S(1)} collective-permute-done((s16[528,128]{1,0:T(8,128)(2,1)S(1)}, s16[528,128]{1,0:T(8,128)(2,1)S(1)}, u32[]{:S(2)}, u32[]{:S(2)}) %collective-permute-start.3) | collective-permute-done | bytes 135200 | tf_op jit(solution)/shard_map/ppermute | solution.py:240
  23.9 0.1 collective-permute-done.4.last
  24.0 0.4 shard_map.78
  24.3 0.0 collective-permute-done.5.beside
  24.3 9.6 %all_to_all.10.grads = f32[8,16,128]{2,1,0:T(8,128)S(1)} all-to-all(f32[8,16,128]{2,1,0:T(8,128)S(1)} %shard_map.78), channel_id=1, replica_groups=mesh['parts'=2,'tensor'=4,'x'=2,'core'=2] {'tensor','x'}, dimensions={0} | all-to-all | bytes 131072 | tf_op jit(solution)/shard_map/all_to_all | solution.py:283
  33.9 1.2 %shard_map.79 = f32[8,8,512]{2,1,0:T(8,128)S(1)} custom-call(f32[8,16,128]{2,1,0:T(8,128)S(1)} %all_to_all.10.grads, bf16[2,1024,1024]{2,1,0:T(8,128)(2,1)S(1)} %copy-done, bf16[2,1024,1024]{2,1,0:T(8,128)(2,1)S(1)} %collective-permute-done.5.beside), custom_call_target="tpu_custom_call" | custom-call | tf_op jit(solution)/shard_map/pallas_call | solution.py:285
  35.1 0.0 collective-permute-done.across
  35.1 0.1 collective-permute-start.6
  35.2 10.3 %all_to_all.11.mapped = f32[8,8,512]{2,1,0:T(8,128)S(1)} all-to-all(f32[8,8,512]{2,1,0:T(8,128)S(1)} %shard_map.79), channel_id=1, replica_groups=mesh['parts'=2,'tensor'=4,'x'=2,'core'=2] {'tensor','x'}, dimensions={0} | all-to-all | bytes 262144 | tf_op jit(solution)/shard_map/all_to_all | solution.py:294
  45.5 0.0 collective-permute-done.6.corner
  45.5 1.5 %shard_map.80 = f32[2,256]{1,0:T(2,128)} custom-call(f32[8,8,512]{2,1,0:T(8,128)S(1)} %all_to_all.11.mapped, bf16[2,1024,256]{2,1,0:T(8,128)(2,1)S(1)} %get-tuple-element.34.own, bf16[2,1024,256]{2,1,0:T(8,128)(2,1)S(1)} %get-tuple-element.35.beside, bf16[2,256,1024]{2,1,0:T(8,128)(2,1)S(1)} %collective-permute-done.across, ...), custom_call_target="tpu_custom_call" | custom-call | tf_op jit(solution)/shard_map/pallas_call | solution.py:296
  (4 shorter events, 0.1 us)
Async XLA Ops:
  0.0 24.3 %collective-permute-start.5 = (bf16[2,1024,1024]{2,1,0:T(8,128)(2,1)}, bf16[2,1024,1024]{2,1,0:T(8,128)(2,1)S(1)}, u32[]{:S(2)}, u32[]{:S(2)}) collective-permute-start(bf16[2,1024,1024]{2,1,0:T(8,128)(2,1)} %fisher.1), channel_id=1, source_target_pairs={{0,1},{1,0},{2,3},{3,2},{4,5},{5,4},{6,7},{7,6},{8,9},{9,8},{10,11... | collective-permute-start | bytes 12582920 | tf_op jit(solution)/shard_map/ppermute | solution.py:240
  0.5 15.6 %collective-permute-start.1 = (bf16[2,256,1024]{2,1,0:T(8,128)(2,1)}, bf16[2,256,1024]{2,1,0:T(8,128)(2,1)S(1)}, u32[]{:S(2)}, u32[]{:S(2)}) collective-permute-start(bf16[2,256,1024]{2,1,0:T(8,128)(2,1)} %refs_4_.1), channel_id=1, source_target_pairs={{0,1},{1,0},{2,3},{3,2},{4,5},{5,4},{6,7},{7,6},{8,9},{9,8},{10,11... | collective-permute-start | bytes 3145736 | tf_op jit(solution)/shard_map/ppermute | solution.py:240
  0.5 34.6 %collective-permute-start = (bf16[2,256,1024]{2,1,0:T(8,128)(2,1)}, bf16[2,256,1024]{2,1,0:T(8,128)(2,1)S(1)}, u32[]{:S(2)}, u32[]{:S(2)}) collective-permute-start(bf16[2,256,1024]{2,1,0:T(8,128)(2,1)} %refs_4_.1), channel_id=1, source_target_pairs={{0,2},{2,0},{1,3},{3,1},{4,6},{6,4},{5,7},{7,5},{8,10},{10,8},{9,1... | collective-permute-start | bytes 3145736 | tf_op jit(solution)/shard_map/ppermute | solution.py:240
  7.0 9.9 %copy-start.1 = (s32[2]{0:T(128)S(1)}, s32[2]{0:T(128)}, u32[]{:S(2)}) copy-start(s32[2]{0:T(128)} %refs_6_.1) | copy-start | bytes 28
  7.0 14.9 %collective-permute-start.2 = (s16[528,128]{1,0:T(8,128)(2,1)S(1)}, s16[528,128]{1,0:T(8,128)(2,1)S(1)}, u32[]{:S(2)}, u32[]{:S(2)}) collective-permute-start(s16[528,128]{1,0:T(8,128)(2,1)S(1)} %shard_map.73), channel_id=1, source_target_pairs={{0,12},{4,8},{8,4},{12,0},{1,13},{5,9},{9,5},{13,1},{2,14},{6,10},... | collective-permute-start | bytes 405512 | tf_op jit(solution)/shard_map/ppermute | solution.py:240
  16.0 17.9 %copy-start = (bf16[2,1024,1024]{2,1,0:T(8,128)(2,1)S(1)}, bf16[2,1024,1024]{2,1,0:T(8,128)(2,1)}, u32[]{:S(2)}) copy-start(bf16[2,1024,1024]{2,1,0:T(8,128)(2,1)} %fisher.1) | copy-start | bytes 12582916
  16.0 7.8 %collective-permute-start.3 = (s16[528,128]{1,0:T(8,128)(2,1)S(1)}, s16[528,128]{1,0:T(8,128)(2,1)S(1)}, u32[]{:S(2)}, u32[]{:S(2)}) collective-permute-start(s16[528,128]{1,0:T(8,128)(2,1)S(1)} %get-tuple-element.29), channel_id=1, source_target_pairs={{0,8},{4,12},{8,0},{12,4},{1,9},{5,13},{9,1},{13,5},{2,10},{6,14},... | collective-permute-start | bytes 405512 | tf_op jit(solution)/shard_map/ppermute | solution.py:240
  16.1 7.9 %collective-permute-start.4 = (s16[528,128]{1,0:T(8,128)(2,1)S(1)}, s16[528,128]{1,0:T(8,128)(2,1)S(1)}, u32[]{:S(2)}, u32[]{:S(2)}) collective-permute-start(s16[528,128]{1,0:T(8,128)(2,1)S(1)} %get-tuple-element.30), channel_id=1, source_target_pairs={{0,4},{4,0},{8,12},{12,8},{1,5},{5,1},{9,13},{13,9},{2,6},{6,2},{1... | collective-permute-start | bytes 405512 | tf_op jit(solution)/shard_map/ppermute | solution.py:240
  35.1 10.4 %collective-permute-start.6 = (bf16[2,256,1024]{2,1,0:T(8,128)(2,1)S(1)}, bf16[2,256,1024]{2,1,0:T(8,128)(2,1)S(1)}, u32[]{:S(2)}, u32[]{:S(2)}) collective-permute-start(bf16[2,256,1024]{2,1,0:T(8,128)(2,1)S(1)} %collective-permute-done.across), channel_id=1, source_target_pairs={{0,1},{1,0},{2,3},{3,2},{4,5},{5,4},{6,7},{7,6},{8,9},{9,8},{10,11... | collective-permute-start | bytes 3145736 | tf_op jit(solution)/shard_map/ppermute | solution.py:240

commit v8 on v7

--- a/solution.py
+++ b/solution.py
@@ -193,8 +193,6 @@
     lanes = grads.shape[2]
     rows = grads.shape[0] // layers
     depth = grads.shape[1] * lanes // 2
-    cut = out.shape[2]
-    halves = width // cut
     core = lax.axis_index("core")
     steps = depth // lanes
     order = [e * 2 + x for x in range(2) for e in range(rows // 2)]
@@ -211,24 +209,37 @@
         every.append(add_thirds(mapped))
     for x in range(2):
         own = jnp.concatenate([mapped[x * rows // 2 : (x + 1) * rows // 2] for mapped in every], axis=0)
-        mapped = jnp.concatenate([own[:, h * cut : (h + 1) * cut] for h in range(halves)], axis=0)
+        log = jnp.ceil(jnp.log2(jnp.maximum(jnp.max(jnp.abs(own), axis=1, keepdims=True), 1e-30)) * STEPS)
+        codes = jnp.round(own * (jnp.exp2(log * (-1.0 / STEPS)) * TOP))
+        codes = jnp.minimum(jnp.maximum(codes, -TOP), TOP)
+        shared = jnp.broadcast_to(log, (own.shape[0], lanes))
+        pieces = [codes[:, at : at + lanes] for at in range(0, width, lanes)] + [shared]
+        rest = out.shape[1] - own.shape[0] * len(pieces)
+        message = jnp.concatenate([*pieces, jnp.zeros((rest, lanes), jnp.float32)], axis=0)
+        message = message.astype(jnp.int32).astype(jnp.int16)
         for t in range(4):
-            out[t * 2 + x] = mapped
+            out[t * 2 + x] = message
 
 
 def with_queries(mapped, own, beside, across, corner, out):
     layers, depth, count = own.shape
-    halves = depth // mapped.shape[2]
-    rows = mapped.shape[1] // halves
+    lanes = mapped.shape[2]
+    examples = out.shape[0]
+    rows = layers * examples
     here = lax.axis_index("x") * 2 + lax.axis_index("core")
+
+    def read(source):
+        message = mapped[source].astype(jnp.int32).astype(jnp.float32)
+        last = depth // lanes * rows
+        scale = jnp.exp2(message[last : last + rows] * (1.0 / STEPS)) * (1.0 / TOP)
+        return jnp.concatenate([message[at : at + rows] * scale for at in range(0, last, rows)], axis=1)
+
     sums = [None] * layers
     for k, block in enumerate((own, beside, across, corner)):
-        both = mapped[(here ^ k) * 2] + mapped[(here ^ k) * 2 + 1]
-        left = thirds(jnp.concatenate([both[h * rows : (h + 1) * rows] for h in range(halves)], axis=1))
+        left = thirds(read((here ^ k) * 2) + read((here ^ k) * 2 + 1))
         for layer in range(layers):
             term = nn(left, block[layer]) if k < 2 else nt(left, block[layer])
             sums[layer] = term if sums[layer] is None else sums[layer] + term
-    examples = rows // layers
     result = None
     for layer in range(layers):
         scores = add_thirds(sums[layer])[layer * examples : (layer + 1) * examples]
@@ -284,7 +295,7 @@
 
     mapped = pl.pallas_call(
         through_fisher,
-        out_shape=jax.ShapeDtypeStruct((8, 8, fisher_inv.shape[2] // 2), jnp.float32),
+        out_shape=jax.ShapeDtypeStruct((8, 48, 128), jnp.int16),
         in_specs=[vmem] * 3,
         out_specs=vmem,
         compiler_params=params,

time: 47.2 us -> 46.9 us (level)
  blocking collectives: 19.9 us -> 19.4 us
    all_to_all x1, blocking collectives: 10.3 us -> 9.82 us  [small(): mapped = lax.all_to_all(mapped, ('tensor', 'x'), 0, 0, tiled=True)]
where the time goes in v8:
time: 46.9 us; the launch traced here: 46.7 us
  blocking collectives  19.4 us (41%)
  Pallas kernels  17.1 us (36%)
  starting transfers between devices  8.02 us (17%)
  waiting for transfers between devices  2.05 us (4%)
    pallas_call x3, Pallas kernels, projector(): pl.pallas_call(project_pairs, out_shape=turned + [jax.ShapeDtypeStruct((t...  13.8 us
    all_to_all x1, blocking collectives, small(): mapped = lax.all_to_all(mapped, ('tensor', 'x'), 0, 0, tiled=True)  9.82 us
    all_to_all x1, blocking collectives, small(): blocks = lax.all_to_all(blocks, ('tensor', 'x'), 0, 0, tiled=True)  9.57 us
    ppermute x7, starting transfers between devices, swap(): lax.ppermute(x, axis, [(i, i ^ flip) for i in range(lax.axis_size(axis))])  8.02 us
    ppermute x7, waiting for transfers between devices, swap(): lax.ppermute(x, axis, [(i, i ^ flip) for i in range(lax.axis_size(axis))])  2.05 us
    pallas_call x1, Pallas kernels, small(): pl.pallas_call(with_queries, out_shape=jax.ShapeDtypeStruct((acts_in.shap...  1.52 us
    pallas_call x1, Pallas kernels, small(): pl.pallas_call(through_fisher, out_shape=jax.ShapeDtypeStruct((8, 48, 128...  1.33 us
  transfers between devices with their start and end apart: 7, of which 2 were waited for; matrix products, arithmetic and copies ran while one was open for 0% of the time, Pallas kernels for 33%

profile of v8, /device:TPU:0, one launch (start us, length us, event | category | flops | bytes accessed | tf_op | source)
XLA Modules:
  0.0 46.7 jit_solution(1560335823876414745)
XLA Ops:
  0.0 0.5 collective-permute-start.5
  0.5 0.1 collective-permute-start.1
  0.5 2.9 %collective-permute-start = (bf16[2,256,1024]{2,1,0:T(8,128)(2,1)}, bf16[2,256,1024]{2,1,0:T(8,128)(2,1)S(1)}, u32[]{:S(2)}, u32[]{:S(2)}) collective-permute-start(bf16[2,256,1024]{2,1,0:T(8,128)(2,1)} %refs_4_.1), channel_id=1, source_target_pairs={{0,2},{2,0},{1,3},{3,1},{4,6},{6,4},{5,7},{7,5},{8,10},{10,8},{9,1... | collective-permute-start | bytes 3145736 | tf_op jit(solution)/shard_map/ppermute | solution.py:251
  3.5 3.5 %shard_map.73 = s16[528,128]{1,0:T(8,128)(2,1)S(1)} custom-call(bf16[2,2,512,2048]{3,2,1,0:T(8,128)(2,1)} %refs_0_.3, bf16[2,2,512,2048]{3,2,1,0:T(8,128)(2,1)} %refs_1_.3, bf16[2,64,2048]{2,1,0:T(8,128)(2,1)} %bitcast.2, bf16[2,64,2048]{2,1,0:T(8,128)(2,1)} %bitcast.5), custom_call_target="tpu_custom_call" | custom-call | tf_op jit(solution)/shard_map/pallas_call | solution.py:126
  7.0 0.0 copy-start.1
  7.0 3.7 %collective-permute-start.2 = (s16[528,128]{1,0:T(8,128)(2,1)S(1)}, s16[528,128]{1,0:T(8,128)(2,1)S(1)}, u32[]{:S(2)}, u32[]{:S(2)}) collective-permute-start(s16[528,128]{1,0:T(8,128)(2,1)S(1)} %shard_map.73), channel_id=1, source_target_pairs={{0,12},{4,8},{8,4},{12,0},{1,13},{5,9},{9,5},{13,1},{2,14},{6,10},... | collective-permute-start | bytes 405512 | tf_op jit(solution)/shard_map/ppermute | solution.py:251
  10.6 5.3 %shard_map.74 = (s16[528,128]{1,0:T(8,128)(2,1)S(1)}, s16[528,128]{1,0:T(8,128)(2,1)S(1)}) custom-call(bf16[2,2,512,2048]{3,2,1,0:T(8,128)(2,1)} %refs_0_.3, bf16[2,2,512,2048]{3,2,1,0:T(8,128)(2,1)} %refs_1_.3, bf16[2,64,2048]{2,1,0:T(8,128)(2,1)} %bitcast.3, bf16[2,64,2048]{2,1,0:T(8,128)(2,1)} %bitcast.6), custom_call_target="tpu_custom_call" | custom-call | tf_op jit(solution)/shard_map/pallas_call | solution.py:126
  16.0 0.0 copy-start
  16.0 0.1 collective-permute-start.3
  16.1 0.0 collective-permute-done.1.refs_5_
  16.1 0.8 %collective-permute-start.4 = (s16[528,128]{1,0:T(8,128)(2,1)S(1)}, s16[528,128]{1,0:T(8,128)(2,1)S(1)}, u32[]{:S(2)}, u32[]{:S(2)}) collective-permute-start(s16[528,128]{1,0:T(8,128)(2,1)S(1)} %get-tuple-element.30), channel_id=1, source_target_pairs={{0,4},{4,0},{8,12},{12,8},{1,5},{5,1},{9,13},{13,9},{2,6},{6,2},{1... | collective-permute-start | bytes 405512 | tf_op jit(solution)/shard_map/ppermute | solution.py:251
  16.8 5.0 %shard_map.75 = (bf16[2,1024,256]{2,1,0:T(8,128)(2,1)S(1)}, bf16[2,1024,256]{2,1,0:T(8,128)(2,1)S(1)}, f32[512,128]{1,0:T(8,128)S(1)}, f32[512,128]{1,0:T(8,128)S(1)}) custom-call(bf16[2,2,512,2048]{3,2,1,0:T(8,128)(2,1)} %refs_0_.3, bf16[2,2,512,2048]{3,2,1,0:T(8,128)(2,1)} %refs_1_.3, bf16[2,64,2048]{2,1,0:T(8,128)(2,1)} %bitcast.4, ...), custom_call_target="tpu_custom_call" | custom-call | tf_op jit(solution)/shard_map/pallas_call | solution.py:126
  21.8 0.0 collective-permute-done.2.partial
  21.9 1.9 %collective-permute-done.3.partial = s16[528,128]{1,0:T(8,128)(2,1)S(1)} collective-permute-done((s16[528,128]{1,0:T(8,128)(2,1)S(1)}, s16[528,128]{1,0:T(8,128)(2,1)S(1)}, u32[]{:S(2)}, u32[]{:S(2)}) %collective-permute-start.3) | collective-permute-done | bytes 135200 | tf_op jit(solution)/shard_map/ppermute | solution.py:251
  23.9 0.1 collective-permute-done.4.last
  24.0 0.4 shard_map.78
  24.3 0.0 collective-permute-done.5.beside
  24.3 9.6 %all_to_all.10.grads = f32[8,16,128]{2,1,0:T(8,128)S(1)} all-to-all(f32[8,16,128]{2,1,0:T(8,128)S(1)} %shard_map.78), channel_id=1, replica_groups=mesh['parts'=2,'tensor'=4,'x'=2,'core'=2] {'tensor','x'}, dimensions={0} | all-to-all | bytes 131072 | tf_op jit(solution)/shard_map/all_to_all | solution.py:294
  33.9 1.3 %shard_map.79 = s16[8,48,128]{2,1,0:T(8,128)(2,1)S(1)} custom-call(f32[8,16,128]{2,1,0:T(8,128)S(1)} %all_to_all.10.grads, bf16[2,1024,1024]{2,1,0:T(8,128)(2,1)S(1)} %copy-done, bf16[2,1024,1024]{2,1,0:T(8,128)(2,1)S(1)} %collective-permute-done.5.beside), custom_call_target="tpu_custom_call" | custom-call | tf_op jit(solution)/shard_map/pallas_call | solution.py:296
  35.2 0.0 collective-permute-done.across
  35.2 0.1 collective-permute-start.6
  35.3 9.8 %all_to_all.11.mapped = s16[8,48,128]{2,1,0:T(8,128)(2,1)S(1)} all-to-all(s16[8,48,128]{2,1,0:T(8,128)(2,1)S(1)} %shard_map.79), channel_id=1, replica_groups=mesh['parts'=2,'tensor'=4,'x'=2,'core'=2] {'tensor','x'}, dimensions={0} | all-to-all | bytes 196608 | tf_op jit(solution)/shard_map/all_to_all | solution.py:305
  45.1 0.0 collective-permute-done.6.corner
  45.1 1.5 %shard_map.80 = f32[2,256]{1,0:T(2,128)} custom-call(s16[8,48,128]{2,1,0:T(8,128)(2,1)S(1)} %all_to_all.11.mapped, bf16[2,1024,256]{2,1,0:T(8,128)(2,1)S(1)} %get-tuple-element.34.own, bf16[2,1024,256]{2,1,0:T(8,128)(2,1)S(1)} %get-tuple-element.35.beside, bf16[2,256,1024]{2,1,0:T(8,128)(2,1)S(1)} %collective-permute-done.across, ...), custom_call_target="tpu_custom_call" | custom-call | tf_op jit(solution)/shard_map/pallas_call | solution.py:307
  (4 shorter events, 0.1 us)
Async XLA Ops:
  0.0 24.3 %collective-permute-start.5 = (bf16[2,1024,1024]{2,1,0:T(8,128)(2,1)}, bf16[2,1024,1024]{2,1,0:T(8,128)(2,1)S(1)}, u32[]{:S(2)}, u32[]{:S(2)}) collective-permute-start(bf16[2,1024,1024]{2,1,0:T(8,128)(2,1)} %fisher.1), channel_id=1, source_target_pairs={{0,1},{1,0},{2,3},{3,2},{4,5},{5,4},{6,7},{7,6},{8,9},{9,8},{10,11... | collective-permute-start | bytes 12582920 | tf_op jit(solution)/shard_map/ppermute | solution.py:251
  0.5 15.6 %collective-permute-start.1 = (bf16[2,256,1024]{2,1,0:T(8,128)(2,1)}, bf16[2,256,1024]{2,1,0:T(8,128)(2,1)S(1)}, u32[]{:S(2)}, u32[]{:S(2)}) collective-permute-start(bf16[2,256,1024]{2,1,0:T(8,128)(2,1)} %refs_4_.1), channel_id=1, source_target_pairs={{0,1},{1,0},{2,3},{3,2},{4,5},{5,4},{6,7},{7,6},{8,9},{9,8},{10,11... | collective-permute-start | bytes 3145736 | tf_op jit(solution)/shard_map/ppermute | solution.py:251
  0.5 34.7 %collective-permute-start = (bf16[2,256,1024]{2,1,0:T(8,128)(2,1)}, bf16[2,256,1024]{2,1,0:T(8,128)(2,1)S(1)}, u32[]{:S(2)}, u32[]{:S(2)}) collective-permute-start(bf16[2,256,1024]{2,1,0:T(8,128)(2,1)} %refs_4_.1), channel_id=1, source_target_pairs={{0,2},{2,0},{1,3},{3,1},{4,6},{6,4},{5,7},{7,5},{8,10},{10,8},{9,1... | collective-permute-start | bytes 3145736 | tf_op jit(solution)/shard_map/ppermute | solution.py:251
  7.0 9.9 %copy-start.1 = (s32[2]{0:T(128)S(1)}, s32[2]{0:T(128)}, u32[]{:S(2)}) copy-start(s32[2]{0:T(128)} %refs_6_.1) | copy-start | bytes 28
  7.0 14.9 %collective-permute-start.2 = (s16[528,128]{1,0:T(8,128)(2,1)S(1)}, s16[528,128]{1,0:T(8,128)(2,1)S(1)}, u32[]{:S(2)}, u32[]{:S(2)}) collective-permute-start(s16[528,128]{1,0:T(8,128)(2,1)S(1)} %shard_map.73), channel_id=1, source_target_pairs={{0,12},{4,8},{8,4},{12,0},{1,13},{5,9},{9,5},{13,1},{2,14},{6,10},... | collective-permute-start | bytes 405512 | tf_op jit(solution)/shard_map/ppermute | solution.py:251
  16.0 17.9 %copy-start = (bf16[2,1024,1024]{2,1,0:T(8,128)(2,1)S(1)}, bf16[2,1024,1024]{2,1,0:T(8,128)(2,1)}, u32[]{:S(2)}) copy-start(bf16[2,1024,1024]{2,1,0:T(8,128)(2,1)} %fisher.1) | copy-start | bytes 12582916
  16.0 7.8 %collective-permute-start.3 = (s16[528,128]{1,0:T(8,128)(2,1)S(1)}, s16[528,128]{1,0:T(8,128)(2,1)S(1)}, u32[]{:S(2)}, u32[]{:S(2)}) collective-permute-start(s16[528,128]{1,0:T(8,128)(2,1)S(1)} %get-tuple-element.29), channel_id=1, source_target_pairs={{0,8},{4,12},{8,0},{12,4},{1,9},{5,13},{9,1},{13,5},{2,10},{6,14},... | collective-permute-start | bytes 405512 | tf_op jit(solution)/shard_map/ppermute | solution.py:251
  16.1 7.9 %collective-permute-start.4 = (s16[528,128]{1,0:T(8,128)(2,1)S(1)}, s16[528,128]{1,0:T(8,128)(2,1)S(1)}, u32[]{:S(2)}, u32[]{:S(2)}) collective-permute-start(s16[528,128]{1,0:T(8,128)(2,1)S(1)} %get-tuple-element.30), channel_id=1, source_target_pairs={{0,4},{4,0},{8,12},{12,8},{1,5},{5,1},{9,13},{13,9},{2,6},{6,2},{1... | collective-permute-start | bytes 405512 | tf_op jit(solution)/shard_map/ppermute | solution.py:251
  35.2 9.9 %collective-permute-start.6 = (bf16[2,256,1024]{2,1,0:T(8,128)(2,1)S(1)}, bf16[2,256,1024]{2,1,0:T(8,128)(2,1)S(1)}, u32[]{:S(2)}, u32[]{:S(2)}) collective-permute-start(bf16[2,256,1024]{2,1,0:T(8,128)(2,1)S(1)} %collective-permute-done.across), channel_id=1, source_target_pairs={{0,1},{1,0},{2,3},{3,2},{4,5},{5,4},{6,7},{7,6},{8,9},{9,8},{10,11... | collective-permute-start | bytes 3145736 | tf_op jit(solution)/shard_map/ppermute | solution.py:251

commit v9 on v8

--- a/solution.py
+++ b/solution.py
@@ -209,11 +209,13 @@
         every.append(add_thirds(mapped))
     for x in range(2):
         own = jnp.concatenate([mapped[x * rows // 2 : (x + 1) * rows // 2] for mapped in every], axis=0)
-        log = jnp.ceil(jnp.log2(jnp.maximum(jnp.max(jnp.abs(own), axis=1, keepdims=True), 1e-30)) * STEPS)
-        codes = jnp.round(own * (jnp.exp2(log * (-1.0 / STEPS)) * TOP))
-        codes = jnp.minimum(jnp.maximum(codes, -TOP), TOP)
-        shared = jnp.broadcast_to(log, (own.shape[0], lanes))
-        pieces = [codes[:, at : at + lanes] for at in range(0, width, lanes)] + [shared]
+        pieces = [own[:, at : at + lanes] for at in range(0, width, lanes)]
+        most = jnp.abs(pieces[0])
+        for piece in pieces[1:]:
+            most = jnp.maximum(most, jnp.abs(piece))
+        log = jnp.ceil(jnp.log2(jnp.maximum(most, 1e-30)) * STEPS)
+        scale = jnp.exp2(log * (-1.0 / STEPS)) * TOP
+        pieces = [jnp.minimum(jnp.maximum(jnp.round(piece * scale), -TOP), TOP) for piece in pieces] + [log]
         rest = out.shape[1] - own.shape[0] * len(pieces)
         message = jnp.concatenate([*pieces, jnp.zeros((rest, lanes), jnp.float32)], axis=0)
         message = message.astype(jnp.int32).astype(jnp.int16)

time: 46.9 us -> 46.8 us (level)
  no operation moved by 1% of the time
where the time goes in v9:
time: 46.8 us; the launch traced here: 46.6 us
  blocking collectives  19.4 us (41%)
  Pallas kernels  17 us (36%)
  starting transfers between devices  8.02 us (17%)
  waiting for transfers between devices  2.05 us (4%)
    pallas_call x3, Pallas kernels, projector(): pl.pallas_call(project_pairs, out_shape=turned + [jax.ShapeDtypeStruct((t...  13.8 us
    all_to_all x1, blocking collectives, small(): mapped = lax.all_to_all(mapped, ('tensor', 'x'), 0, 0, tiled=True)  9.82 us
    all_to_all x1, blocking collectives, small(): blocks = lax.all_to_all(blocks, ('tensor', 'x'), 0, 0, tiled=True)  9.57 us
    ppermute x7, starting transfers between devices, swap(): lax.ppermute(x, axis, [(i, i ^ flip) for i in range(lax.axis_size(axis))])  8.02 us
    ppermute x7, waiting for transfers between devices, swap(): lax.ppermute(x, axis, [(i, i ^ flip) for i in range(lax.axis_size(axis))])  2.05 us
    pallas_call x1, Pallas kernels, small(): pl.pallas_call(with_queries, out_shape=jax.ShapeDtypeStruct((acts_in.shap...  1.52 us
    pallas_call x1, Pallas kernels, small(): pl.pallas_call(through_fisher, out_shape=jax.ShapeDtypeStruct((8, 48, 128...  1.25 us
  transfers between devices with their start and end apart: 7, of which 2 were waited for; matrix products, arithmetic and copies ran while one was open for 0% of the time, Pallas kernels for 33%

profile of v9, /device:TPU:0, one launch (start us, length us, event | category | flops | bytes accessed | tf_op | source)
XLA Modules:
  0.0 46.6 jit_solution(10242067738061397210)
XLA Ops:
  0.0 0.5 collective-permute-start.5
  0.5 0.1 collective-permute-start.1
  0.5 2.9 %collective-permute-start = (bf16[2,256,1024]{2,1,0:T(8,128)(2,1)}, bf16[2,256,1024]{2,1,0:T(8,128)(2,1)S(1)}, u32[]{:S(2)}, u32[]{:S(2)}) collective-permute-start(bf16[2,256,1024]{2,1,0:T(8,128)(2,1)} %refs_4_.1), channel_id=1, source_target_pairs={{0,2},{2,0},{1,3},{3,1},{4,6},{6,4},{5,7},{7,5},{8,10},{10,8},{9,1... | collective-permute-start | bytes 3145736 | tf_op jit(solution)/shard_map/ppermute | solution.py:253
  3.5 3.5 %shard_map.73 = s16[528,128]{1,0:T(8,128)(2,1)S(1)} custom-call(bf16[2,2,512,2048]{3,2,1,0:T(8,128)(2,1)} %refs_0_.3, bf16[2,2,512,2048]{3,2,1,0:T(8,128)(2,1)} %refs_1_.3, bf16[2,64,2048]{2,1,0:T(8,128)(2,1)} %bitcast.2, bf16[2,64,2048]{2,1,0:T(8,128)(2,1)} %bitcast.5), custom_call_target="tpu_custom_call" | custom-call | tf_op jit(solution)/shard_map/pallas_call | solution.py:126
  7.0 0.0 copy-start.1
  7.0 3.7 %collective-permute-start.2 = (s16[528,128]{1,0:T(8,128)(2,1)S(1)}, s16[528,128]{1,0:T(8,128)(2,1)S(1)}, u32[]{:S(2)}, u32[]{:S(2)}) collective-permute-start(s16[528,128]{1,0:T(8,128)(2,1)S(1)} %shard_map.73), channel_id=1, source_target_pairs={{0,12},{4,8},{8,4},{12,0},{1,13},{5,9},{9,5},{13,1},{2,14},{6,10},... | collective-permute-start | bytes 405512 | tf_op jit(solution)/shard_map/ppermute | solution.py:253
  10.6 5.3 %shard_map.74 = (s16[528,128]{1,0:T(8,128)(2,1)S(1)}, s16[528,128]{1,0:T(8,128)(2,1)S(1)}) custom-call(bf16[2,2,512,2048]{3,2,1,0:T(8,128)(2,1)} %refs_0_.3, bf16[2,2,512,2048]{3,2,1,0:T(8,128)(2,1)} %refs_1_.3, bf16[2,64,2048]{2,1,0:T(8,128)(2,1)} %bitcast.3, bf16[2,64,2048]{2,1,0:T(8,128)(2,1)} %bitcast.6), custom_call_target="tpu_custom_call" | custom-call | tf_op jit(solution)/shard_map/pallas_call | solution.py:126
  16.0 0.0 copy-start
  16.0 0.1 collective-permute-start.3
  16.1 0.0 collective-permute-done.1.refs_5_
  16.1 0.8 %collective-permute-start.4 = (s16[528,128]{1,0:T(8,128)(2,1)S(1)}, s16[528,128]{1,0:T(8,128)(2,1)S(1)}, u32[]{:S(2)}, u32[]{:S(2)}) collective-permute-start(s16[528,128]{1,0:T(8,128)(2,1)S(1)} %get-tuple-element.30), channel_id=1, source_target_pairs={{0,4},{4,0},{8,12},{12,8},{1,5},{5,1},{9,13},{13,9},{2,6},{6,2},{1... | collective-permute-start | bytes 405512 | tf_op jit(solution)/shard_map/ppermute | solution.py:253
  16.8 5.0 %shard_map.75 = (bf16[2,1024,256]{2,1,0:T(8,128)(2,1)S(1)}, bf16[2,1024,256]{2,1,0:T(8,128)(2,1)S(1)}, f32[512,128]{1,0:T(8,128)S(1)}, f32[512,128]{1,0:T(8,128)S(1)}) custom-call(bf16[2,2,512,2048]{3,2,1,0:T(8,128)(2,1)} %refs_0_.3, bf16[2,2,512,2048]{3,2,1,0:T(8,128)(2,1)} %refs_1_.3, bf16[2,64,2048]{2,1,0:T(8,128)(2,1)} %bitcast.4, ...), custom_call_target="tpu_custom_call" | custom-call | tf_op jit(solution)/shard_map/pallas_call | solution.py:126
  21.8 0.0 collective-permute-done.2.partial
  21.9 1.9 %collective-permute-done.3.partial = s16[528,128]{1,0:T(8,128)(2,1)S(1)} collective-permute-done((s16[528,128]{1,0:T(8,128)(2,1)S(1)}, s16[528,128]{1,0:T(8,128)(2,1)S(1)}, u32[]{:S(2)}, u32[]{:S(2)}) %collective-permute-start.3) | collective-permute-done | bytes 135200 | tf_op jit(solution)/shard_map/ppermute | solution.py:253
  23.9 0.1 collective-permute-done.4.last
  24.0 0.4 shard_map.78
  24.3 0.0 collective-permute-done.5.beside
  24.3 9.6 %all_to_all.10.grads = f32[8,16,128]{2,1,0:T(8,128)S(1)} all-to-all(f32[8,16,128]{2,1,0:T(8,128)S(1)} %shard_map.78), channel_id=1, replica_groups=mesh['parts'=2,'tensor'=4,'x'=2,'core'=2] {'tensor','x'}, dimensions={0} | all-to-all | bytes 131072 | tf_op jit(solution)/shard_map/all_to_all | solution.py:296
  33.9 1.2 %shard_map.79 = s16[8,48,128]{2,1,0:T(8,128)(2,1)S(1)} custom-call(f32[8,16,128]{2,1,0:T(8,128)S(1)} %all_to_all.10.grads, bf16[2,1024,1024]{2,1,0:T(8,128)(2,1)S(1)} %copy-done, bf16[2,1024,1024]{2,1,0:T(8,128)(2,1)S(1)} %collective-permute-done.5.beside), custom_call_target="tpu_custom_call" | custom-call | tf_op jit(solution)/shard_map/pallas_call | solution.py:298
  35.2 0.0 collective-permute-done.across
  35.2 0.1 collective-permute-start.6
  35.2 9.8 %all_to_all.11.mapped = s16[8,48,128]{2,1,0:T(8,128)(2,1)S(1)} all-to-all(s16[8,48,128]{2,1,0:T(8,128)(2,1)S(1)} %shard_map.79), channel_id=1, replica_groups=mesh['parts'=2,'tensor'=4,'x'=2,'core'=2] {'tensor','x'}, dimensions={0} | all-to-all | bytes 196608 | tf_op jit(solution)/shard_map/all_to_all | solution.py:307
  45.1 0.0 collective-permute-done.6.corner
  45.1 1.5 %shard_map.80 = f32[2,256]{1,0:T(2,128)} custom-call(s16[8,48,128]{2,1,0:T(8,128)(2,1)S(1)} %all_to_all.11.mapped, bf16[2,1024,256]{2,1,0:T(8,128)(2,1)S(1)} %get-tuple-element.34.own, bf16[2,1024,256]{2,1,0:T(8,128)(2,1)S(1)} %get-tuple-element.35.beside, bf16[2,256,1024]{2,1,0:T(8,128)(2,1)S(1)} %collective-permute-done.across, ...), custom_call_target="tpu_custom_call" | custom-call | tf_op jit(solution)/shard_map/pallas_call | solution.py:309
  (4 shorter events, 0.1 us)
Async XLA Ops:
  0.0 24.3 %collective-permute-start.5 = (bf16[2,1024,1024]{2,1,0:T(8,128)(2,1)}, bf16[2,1024,1024]{2,1,0:T(8,128)(2,1)S(1)}, u32[]{:S(2)}, u32[]{:S(2)}) collective-permute-start(bf16[2,1024,1024]{2,1,0:T(8,128)(2,1)} %fisher.1), channel_id=1, source_target_pairs={{0,1},{1,0},{2,3},{3,2},{4,5},{5,4},{6,7},{7,6},{8,9},{9,8},{10,11... | collective-permute-start | bytes 12582920 | tf_op jit(solution)/shard_map/ppermute | solution.py:253
  0.5 15.6 %collective-permute-start.1 = (bf16[2,256,1024]{2,1,0:T(8,128)(2,1)}, bf16[2,256,1024]{2,1,0:T(8,128)(2,1)S(1)}, u32[]{:S(2)}, u32[]{:S(2)}) collective-permute-start(bf16[2,256,1024]{2,1,0:T(8,128)(2,1)} %refs_4_.1), channel_id=1, source_target_pairs={{0,1},{1,0},{2,3},{3,2},{4,5},{5,4},{6,7},{7,6},{8,9},{9,8},{10,11... | collective-permute-start | bytes 3145736 | tf_op jit(solution)/shard_map/ppermute | solution.py:253
  0.5 34.6 %collective-permute-start = (bf16[2,256,1024]{2,1,0:T(8,128)(2,1)}, bf16[2,256,1024]{2,1,0:T(8,128)(2,1)S(1)}, u32[]{:S(2)}, u32[]{:S(2)}) collective-permute-start(bf16[2,256,1024]{2,1,0:T(8,128)(2,1)} %refs_4_.1), channel_id=1, source_target_pairs={{0,2},{2,0},{1,3},{3,1},{4,6},{6,4},{5,7},{7,5},{8,10},{10,8},{9,1... | collective-permute-start | bytes 3145736 | tf_op jit(solution)/shard_map/ppermute | solution.py:253
  7.0 9.9 %copy-start.1 = (s32[2]{0:T(128)S(1)}, s32[2]{0:T(128)}, u32[]{:S(2)}) copy-start(s32[2]{0:T(128)} %refs_6_.1) | copy-start | bytes 28
  7.0 14.9 %collective-permute-start.2 = (s16[528,128]{1,0:T(8,128)(2,1)S(1)}, s16[528,128]{1,0:T(8,128)(2,1)S(1)}, u32[]{:S(2)}, u32[]{:S(2)}) collective-permute-start(s16[528,128]{1,0:T(8,128)(2,1)S(1)} %shard_map.73), channel_id=1, source_target_pairs={{0,12},{4,8},{8,4},{12,0},{1,13},{5,9},{9,5},{13,1},{2,14},{6,10},... | collective-permute-start | bytes 405512 | tf_op jit(solution)/shard_map/ppermute | solution.py:253
  16.0 17.9 %copy-start = (bf16[2,1024,1024]{2,1,0:T(8,128)(2,1)S(1)}, bf16[2,1024,1024]{2,1,0:T(8,128)(2,1)}, u32[]{:S(2)}) copy-start(bf16[2,1024,1024]{2,1,0:T(8,128)(2,1)} %fisher.1) | copy-start | bytes 12582916
  16.0 7.8 %collective-permute-start.3 = (s16[528,128]{1,0:T(8,128)(2,1)S(1)}, s16[528,128]{1,0:T(8,128)(2,1)S(1)}, u32[]{:S(2)}, u32[]{:S(2)}) collective-permute-start(s16[528,128]{1,0:T(8,128)(2,1)S(1)} %get-tuple-element.29), channel_id=1, source_target_pairs={{0,8},{4,12},{8,0},{12,4},{1,9},{5,13},{9,1},{13,5},{2,10},{6,14},... | collective-permute-start | bytes 405512 | tf_op jit(solution)/shard_map/ppermute | solution.py:253
  16.1 7.9 %collective-permute-start.4 = (s16[528,128]{1,0:T(8,128)(2,1)S(1)}, s16[528,128]{1,0:T(8,128)(2,1)S(1)}, u32[]{:S(2)}, u32[]{:S(2)}) collective-permute-start(s16[528,128]{1,0:T(8,128)(2,1)S(1)} %get-tuple-element.30), channel_id=1, source_target_pairs={{0,4},{4,0},{8,12},{12,8},{1,5},{5,1},{9,13},{13,9},{2,6},{6,2},{1... | collective-permute-start | bytes 405512 | tf_op jit(solution)/shard_map/ppermute | solution.py:253
  35.2 9.9 %collective-permute-start.6 = (bf16[2,256,1024]{2,1,0:T(8,128)(2,1)S(1)}, bf16[2,256,1024]{2,1,0:T(8,128)(2,1)S(1)}, u32[]{:S(2)}, u32[]{:S(2)}) collective-permute-start(bf16[2,256,1024]{2,1,0:T(8,128)(2,1)S(1)} %collective-permute-done.across), channel_id=1, source_target_pairs={{0,1},{1,0},{2,3},{3,2},{4,5},{5,4},{6,7},{7,6},{8,9},{9,8},{10,11... | collective-permute-start | bytes 3145736 | tf_op jit(solution)/shard_map/ppermute | solution.py:253

commit v10 on v9

--- a/solution.py
+++ b/solution.py
@@ -236,17 +236,14 @@
         scale = jnp.exp2(message[last : last + rows] * (1.0 / STEPS)) * (1.0 / TOP)
         return jnp.concatenate([message[at : at + rows] * scale for at in range(0, last, rows)], axis=1)
 
-    sums = [None] * layers
+    sums = None
     for k, block in enumerate((own, beside, across, corner)):
         left = thirds(read((here ^ k) * 2) + read((here ^ k) * 2 + 1))
         for layer in range(layers):
-            term = nn(left, block[layer]) if k < 2 else nt(left, block[layer])
-            sums[layer] = term if sums[layer] is None else sums[layer] + term
-    result = None
-    for layer in range(layers):
-        scores = add_thirds(sums[layer])[layer * examples : (layer + 1) * examples]
-        result = scores if result is None else result + scores
-    out[...] = result
+            wanted = jnp.concatenate([left[at + layer * examples : at + (layer + 1) * examples] for at in range(0, 3 * rows, rows)], axis=0)
+            term = nn(wanted, block[layer]) if k < 2 else nt(wanted, block[layer])
+            sums = term if sums is None else sums + term
+    out[...] = add_thirds(sums)
 
 
 def swap(x, axis, flip):
@@ -263,7 +260,7 @@
     proj_width = basis_in.shape[2]
     operands = (acts_in, grads_out, jnp.swapaxes(basis_in, 1, 2), jnp.swapaxes(basis_out, 1, 2))
 
-    across, beside = swap(queries, "x", 1), swap(queries, "core", 1)
+    beside, across = swap(queries, "core", 1), swap(queries, "x", 1)
     (far,) = projector((3,), (32,), PIECES_ONE, *operands)
     acts_in, grads_out, far = lax.optimization_barrier((acts_in, grads_out, far))
     middle, near = projector((2, 1), (32, 32), PIECES_TWO, acts_in, grads_out, *operands[2:])

time: 46.8 us -> 46.8 us (level)
  no operation moved by 1% of the time
where the time goes in v10:
time: 46.8 us; the launch traced here: 46.6 us
  blocking collectives  19.4 us (41%)
  Pallas kernels  17 us (36%)
  starting transfers between devices  8.02 us (17%)
  waiting for transfers between devices  2.05 us (4%)
    pallas_call x3, Pallas kernels, projector(): pl.pallas_call(project_pairs, out_shape=turned + [jax.ShapeDtypeStruct((t...  13.8 us
    all_to_all x1, blocking collectives, small(): mapped = lax.all_to_all(mapped, ('tensor', 'x'), 0, 0, tiled=True)  9.82 us
    all_to_all x1, blocking collectives, small(): blocks = lax.all_to_all(blocks, ('tensor', 'x'), 0, 0, tiled=True)  9.57 us
    ppermute x7, starting transfers between devices, swap(): lax.ppermute(x, axis, [(i, i ^ flip) for i in range(lax.axis_size(axis))])  8.02 us
    ppermute x7, waiting for transfers between devices, swap(): lax.ppermute(x, axis, [(i, i ^ flip) for i in range(lax.axis_size(axis))])  2.05 us
    pallas_call x1, Pallas kernels, small(): pl.pallas_call(with_queries, out_shape=jax.ShapeDtypeStruct((acts_in.shap...  1.52 us
    pallas_call x1, Pallas kernels, small(): pl.pallas_call(through_fisher, out_shape=jax.ShapeDtypeStruct((8, 48, 128...  1.25 us
  transfers between devices with their start and end apart: 7, of which 2 were waited for; matrix products, arithmetic and copies ran while one was open for 0% of the time, Pallas kernels for 33%

profile of v10, /device:TPU:0, one launch (start us, length us, event | category | flops | bytes accessed | tf_op | source)
XLA Modules:
  0.0 46.6 jit_solution(9900330875622828452)
XLA Ops:
  0.0 0.5 collective-permute-start.5
  0.5 0.1 collective-permute-start.1
  0.5 2.9 %collective-permute-start = (bf16[2,256,1024]{2,1,0:T(8,128)(2,1)}, bf16[2,256,1024]{2,1,0:T(8,128)(2,1)S(1)}, u32[]{:S(2)}, u32[]{:S(2)}) collective-permute-start(bf16[2,256,1024]{2,1,0:T(8,128)(2,1)} %refs_4_.1), channel_id=1, source_target_pairs={{0,2},{2,0},{1,3},{3,1},{4,6},{6,4},{5,7},{7,5},{8,10},{10,8},{9,1... | collective-permute-start | bytes 3145736 | tf_op jit(solution)/shard_map/ppermute | solution.py:250
  3.5 3.5 %shard_map.73 = s16[528,128]{1,0:T(8,128)(2,1)S(1)} custom-call(bf16[2,2,512,2048]{3,2,1,0:T(8,128)(2,1)} %refs_0_.3, bf16[2,2,512,2048]{3,2,1,0:T(8,128)(2,1)} %refs_1_.3, bf16[2,64,2048]{2,1,0:T(8,128)(2,1)} %bitcast.2, bf16[2,64,2048]{2,1,0:T(8,128)(2,1)} %bitcast.5), custom_call_target="tpu_custom_call" | custom-call | tf_op jit(solution)/shard_map/pallas_call | solution.py:126
  7.0 0.0 copy-start.1
  7.0 3.7 %collective-permute-start.2 = (s16[528,128]{1,0:T(8,128)(2,1)S(1)}, s16[528,128]{1,0:T(8,128)(2,1)S(1)}, u32[]{:S(2)}, u32[]{:S(2)}) collective-permute-start(s16[528,128]{1,0:T(8,128)(2,1)S(1)} %shard_map.73), channel_id=1, source_target_pairs={{0,12},{4,8},{8,4},{12,0},{1,13},{5,9},{9,5},{13,1},{2,14},{6,10},... | collective-permute-start | bytes 405512 | tf_op jit(solution)/shard_map/ppermute | solution.py:250
  10.6 5.3 %shard_map.74 = (s16[528,128]{1,0:T(8,128)(2,1)S(1)}, s16[528,128]{1,0:T(8,128)(2,1)S(1)}) custom-call(bf16[2,2,512,2048]{3,2,1,0:T(8,128)(2,1)} %refs_0_.3, bf16[2,2,512,2048]{3,2,1,0:T(8,128)(2,1)} %refs_1_.3, bf16[2,64,2048]{2,1,0:T(8,128)(2,1)} %bitcast.3, bf16[2,64,2048]{2,1,0:T(8,128)(2,1)} %bitcast.6), custom_call_target="tpu_custom_call" | custom-call | tf_op jit(solution)/shard_map/pallas_call | solution.py:126
  16.0 0.0 copy-start
  16.0 0.1 collective-permute-start.3
  16.1 0.0 collective-permute-done.1.refs_5_
  16.1 0.8 %collective-permute-start.4 = (s16[528,128]{1,0:T(8,128)(2,1)S(1)}, s16[528,128]{1,0:T(8,128)(2,1)S(1)}, u32[]{:S(2)}, u32[]{:S(2)}) collective-permute-start(s16[528,128]{1,0:T(8,128)(2,1)S(1)} %get-tuple-element.30), channel_id=1, source_target_pairs={{0,4},{4,0},{8,12},{12,8},{1,5},{5,1},{9,13},{13,9},{2,6},{6,2},{1... | collective-permute-start | bytes 405512 | tf_op jit(solution)/shard_map/ppermute | solution.py:250
  16.8 5.0 %shard_map.75 = (bf16[2,1024,256]{2,1,0:T(8,128)(2,1)S(1)}, bf16[2,1024,256]{2,1,0:T(8,128)(2,1)S(1)}, f32[512,128]{1,0:T(8,128)S(1)}, f32[512,128]{1,0:T(8,128)S(1)}) custom-call(bf16[2,2,512,2048]{3,2,1,0:T(8,128)(2,1)} %refs_0_.3, bf16[2,2,512,2048]{3,2,1,0:T(8,128)(2,1)} %refs_1_.3, bf16[2,64,2048]{2,1,0:T(8,128)(2,1)} %bitcast.4, ...), custom_call_target="tpu_custom_call" | custom-call | tf_op jit(solution)/shard_map/pallas_call | solution.py:126
  21.8 0.0 collective-permute-done.2.partial
  21.9 1.9 %collective-permute-done.3.partial = s16[528,128]{1,0:T(8,128)(2,1)S(1)} collective-permute-done((s16[528,128]{1,0:T(8,128)(2,1)S(1)}, s16[528,128]{1,0:T(8,128)(2,1)S(1)}, u32[]{:S(2)}, u32[]{:S(2)}) %collective-permute-start.3) | collective-permute-done | bytes 135200 | tf_op jit(solution)/shard_map/ppermute | solution.py:250
  23.9 0.1 collective-permute-done.4.last
  24.0 0.4 shard_map.78
  24.3 0.0 collective-permute-done.5.beside
  24.3 9.6 %all_to_all.10.grads = f32[8,16,128]{2,1,0:T(8,128)S(1)} all-to-all(f32[8,16,128]{2,1,0:T(8,128)S(1)} %shard_map.78), channel_id=1, replica_groups=mesh['parts'=2,'tensor'=4,'x'=2,'core'=2] {'tensor','x'}, dimensions={0} | all-to-all | bytes 131072 | tf_op jit(solution)/shard_map/all_to_all | solution.py:293
  33.9 1.2 %shard_map.79 = s16[8,48,128]{2,1,0:T(8,128)(2,1)S(1)} custom-call(f32[8,16,128]{2,1,0:T(8,128)S(1)} %all_to_all.10.grads, bf16[2,1024,1024]{2,1,0:T(8,128)(2,1)S(1)} %copy-done, bf16[2,1024,1024]{2,1,0:T(8,128)(2,1)S(1)} %collective-permute-done.5.beside), custom_call_target="tpu_custom_call" | custom-call | tf_op jit(solution)/shard_map/pallas_call | solution.py:295
  35.2 0.0 collective-permute-done.across
  35.2 0.1 collective-permute-start.6
  35.2 9.8 %all_to_all.11.mapped = s16[8,48,128]{2,1,0:T(8,128)(2,1)S(1)} all-to-all(s16[8,48,128]{2,1,0:T(8,128)(2,1)S(1)} %shard_map.79), channel_id=1, replica_groups=mesh['parts'=2,'tensor'=4,'x'=2,'core'=2] {'tensor','x'}, dimensions={0} | all-to-all | bytes 196608 | tf_op jit(solution)/shard_map/all_to_all | solution.py:304
  45.1 0.0 collective-permute-done.6.corner
  45.1 1.5 %shard_map.80 = f32[2,256]{1,0:T(2,128)} custom-call(s16[8,48,128]{2,1,0:T(8,128)(2,1)S(1)} %all_to_all.11.mapped, bf16[2,1024,256]{2,1,0:T(8,128)(2,1)S(1)} %get-tuple-element.34.own, bf16[2,1024,256]{2,1,0:T(8,128)(2,1)S(1)} %get-tuple-element.35.beside, bf16[2,256,1024]{2,1,0:T(8,128)(2,1)S(1)} %collective-permute-done.across, ...), custom_call_target="tpu_custom_call" | custom-call | tf_op jit(solution)/shard_map/pallas_call | solution.py:306
  (4 shorter events, 0.1 us)
Async XLA Ops:
  0.0 24.3 %collective-permute-start.5 = (bf16[2,1024,1024]{2,1,0:T(8,128)(2,1)}, bf16[2,1024,1024]{2,1,0:T(8,128)(2,1)S(1)}, u32[]{:S(2)}, u32[]{:S(2)}) collective-permute-start(bf16[2,1024,1024]{2,1,0:T(8,128)(2,1)} %fisher.1), channel_id=1, source_target_pairs={{0,1},{1,0},{2,3},{3,2},{4,5},{5,4},{6,7},{7,6},{8,9},{9,8},{10,11... | collective-permute-start | bytes 12582920 | tf_op jit(solution)/shard_map/ppermute | solution.py:250
  0.5 15.6 %collective-permute-start.1 = (bf16[2,256,1024]{2,1,0:T(8,128)(2,1)}, bf16[2,256,1024]{2,1,0:T(8,128)(2,1)S(1)}, u32[]{:S(2)}, u32[]{:S(2)}) collective-permute-start(bf16[2,256,1024]{2,1,0:T(8,128)(2,1)} %refs_4_.1), channel_id=1, source_target_pairs={{0,1},{1,0},{2,3},{3,2},{4,5},{5,4},{6,7},{7,6},{8,9},{9,8},{10,11... | collective-permute-start | bytes 3145736 | tf_op jit(solution)/shard_map/ppermute | solution.py:250
  0.5 34.6 %collective-permute-start = (bf16[2,256,1024]{2,1,0:T(8,128)(2,1)}, bf16[2,256,1024]{2,1,0:T(8,128)(2,1)S(1)}, u32[]{:S(2)}, u32[]{:S(2)}) collective-permute-start(bf16[2,256,1024]{2,1,0:T(8,128)(2,1)} %refs_4_.1), channel_id=1, source_target_pairs={{0,2},{2,0},{1,3},{3,1},{4,6},{6,4},{5,7},{7,5},{8,10},{10,8},{9,1... | collective-permute-start | bytes 3145736 | tf_op jit(solution)/shard_map/ppermute | solution.py:250
  7.0 9.9 %copy-start.1 = (s32[2]{0:T(128)S(1)}, s32[2]{0:T(128)}, u32[]{:S(2)}) copy-start(s32[2]{0:T(128)} %refs_6_.1) | copy-start | bytes 28
  7.0 14.9 %collective-permute-start.2 = (s16[528,128]{1,0:T(8,128)(2,1)S(1)}, s16[528,128]{1,0:T(8,128)(2,1)S(1)}, u32[]{:S(2)}, u32[]{:S(2)}) collective-permute-start(s16[528,128]{1,0:T(8,128)(2,1)S(1)} %shard_map.73), channel_id=1, source_target_pairs={{0,12},{4,8},{8,4},{12,0},{1,13},{5,9},{9,5},{13,1},{2,14},{6,10},... | collective-permute-start | bytes 405512 | tf_op jit(solution)/shard_map/ppermute | solution.py:250
  16.0 17.9 %copy-start = (bf16[2,1024,1024]{2,1,0:T(8,128)(2,1)S(1)}, bf16[2,1024,1024]{2,1,0:T(8,128)(2,1)}, u32[]{:S(2)}) copy-start(bf16[2,1024,1024]{2,1,0:T(8,128)(2,1)} %fisher.1) | copy-start | bytes 12582916
  16.0 7.8 %collective-permute-start.3 = (s16[528,128]{1,0:T(8,128)(2,1)S(1)}, s16[528,128]{1,0:T(8,128)(2,1)S(1)}, u32[]{:S(2)}, u32[]{:S(2)}) collective-permute-start(s16[528,128]{1,0:T(8,128)(2,1)S(1)} %get-tuple-element.29), channel_id=1, source_target_pairs={{0,8},{4,12},{8,0},{12,4},{1,9},{5,13},{9,1},{13,5},{2,10},{6,14},... | collective-permute-start | bytes 405512 | tf_op jit(solution)/shard_map/ppermute | solution.py:250
  16.1 7.9 %collective-permute-start.4 = (s16[528,128]{1,0:T(8,128)(2,1)S(1)}, s16[528,128]{1,0:T(8,128)(2,1)S(1)}, u32[]{:S(2)}, u32[]{:S(2)}) collective-permute-start(s16[528,128]{1,0:T(8,128)(2,1)S(1)} %get-tuple-element.30), channel_id=1, source_target_pairs={{0,4},{4,0},{8,12},{12,8},{1,5},{5,1},{9,13},{13,9},{2,6},{6,2},{1... | collective-permute-start | bytes 405512 | tf_op jit(solution)/shard_map/ppermute | solution.py:250
  35.2 9.9 %collective-permute-start.6 = (bf16[2,256,1024]{2,1,0:T(8,128)(2,1)S(1)}, bf16[2,256,1024]{2,1,0:T(8,128)(2,1)S(1)}, u32[]{:S(2)}, u32[]{:S(2)}) collective-permute-start(bf16[2,256,1024]{2,1,0:T(8,128)(2,1)S(1)} %collective-permute-done.across), channel_id=1, source_target_pairs={{0,1},{1,0},{2,3},{3,2},{4,5},{5,4},{6,7},{7,6},{8,9},{9,8},{10,11... | collective-permute-start | bytes 3145736 | tf_op jit(solution)/shard_map/ppermute | solution.py:250
